TPU v7x, 128 devices: a whole 4x4x4 slice. The times are simulated.
128 devices in a mesh: dp: 8 (over x, core), mp: 16 (over y, z).
Axes of the slice: x: 4, y: 4, z: 4, core: 2. Of those that a mesh axis runs over, the one named last changes fastest.
Arguments:
- queries: bfloat16 [1024, 4096], P('dp'), may hold values from -103 to 103
- new_kv: bfloat16 [2, 1024, 1024], P(None, 'dp'), may hold values from -6 to 6
- residual: bfloat16 [1024, 4096], P('dp', 'mp'), may hold values from -2.4 to 2.4
- out_weight: bfloat16 [4096, 4096], P('mp'), may hold values from -0.125 to 0.125
- norm_gain: float32 [4096], replicated, may hold values from 0.5 to 1.5
- router: bfloat16 [4096, 8], replicated, may hold values from -0.09375 to 0.09375
- expert_in: bfloat16 [8, 2, 8192, 4096], P('dp', None, 'mp'), may hold values from -0.09375 to 0.09375
- expert_out: bfloat16 [8, 8192, 4096], P('dp', 'mp'), may hold values from -0.09375 to 0.09375
- node_cache: bfloat16 [2, 768, 16, 64, 128], P(None, 'dp', 'mp'), may hold values from -6 to 6
- leaf_cache: bfloat16 [2, 1024, 16, 64, 128], P(None, 'dp', 'mp'), may hold values from -6 to 6
- slot_request: int32 [1024], replicated, may hold values from 0 to 1023, each once
- request_branch: int32 [1024], replicated, may hold values from 0 to 63, as said below
- branch_parent: int32 [64], replicated, may hold values from 0 to 15, as said below
- root_owner: int32 [16], replicated, may hold values from 0 to 7, as said below
- branch_owner: int32 [64], replicated, may hold values from 0 to 7, as said below
- root_pages: int32 [16, 32], replicated, may hold values from 0 to 95, as said below
- branch_pages: int32 [64, 4], replicated, may hold values from 0 to 95, as said below
- root_len: int32 [16], replicated, may hold values from 1 to 4096, as said below
- branch_len: int32 [64], replicated, may hold values from 1 to 512
- leaf_len: int32 [1024], P('dp'), may hold values from 1 to 128
- routes: int32 [1024, 2], P('dp'), may hold values from 0 to 7, all different within a row; in each aligned block of 128 rows (0 to 127, 128 to 255, ...) at most 64 rows name the same one
Outputs:
- layer_out: bfloat16 [1024, 4096], P('dp', 'mp')
Inputs may be any that keep to these rules, and one draw needn't show every extreme that they name: `request_branch`: at most 32 requests share a branch, and some branch has exactly 32. `branch_parent`: every root has exactly 4 branches. `root_owner`: every index of dp holds exactly 2 roots. `branch_owner`: every index of dp holds exactly 8 branches. `root_pages`: no slot of an owner's pool serves two pages of its nodes. `branch_pages`: no slot of an owner's pool serves two pages of its nodes. `root_len`: some root has 32 full pages.
All inputs are finite; a program needn't handle non-finite values.
Results may differ from a plain program's by a relative error of at most 0.034.
Values may be sent and summed in bfloat16 or wider, within the bound.
A program may use at most 576 MiB of HBM per device.

v0:
```python
import jax
import jax.numpy as jnp
from jax import lax
from jax.sharding import PartitionSpec as P

HEADS = 32
KVH = 8
EXPERTS = 8
TOP = 2
PAGE = 128
ROOT_DEV = 2
BR_DEV = 8
BR_CAP = 32
E_CAP = 64


MASKED_SCORE = -1e30
NORM_EPS = 1e-05


def partner(x, axis, apart):
    return lax.ppermute(x, axis, [(i, i ^ 1 << apart) for i in range(lax.axis_size(axis))])


def merge_partials(first_part, second_part):
    first_sum, first_max, first_total = first_part
    second_sum, second_max, second_total = second_part
    common_max = jnp.maximum(first_max, second_max)
    first_factor = jnp.exp(first_max - common_max)
    second_factor = jnp.exp(second_max - common_max)
    merged_sum = first_sum * first_factor[..., None] + second_sum * second_factor[..., None]
    return (merged_sum, common_max, first_total * first_factor + second_total * second_factor)


def weigh_scores(scores, usable, values, pattern):
    masked_scores = jnp.where(usable, scores, MASKED_SCORE)
    row_max = jnp.max(masked_scores, axis=-1)
    weights = jnp.where(usable, jnp.exp(masked_scores - row_max[..., None]), 0.0)
    weight_total = jnp.sum(weights, axis=-1)
    weighted_sum = jnp.einsum(
        pattern, weights.astype(jnp.bfloat16), values, preferred_element_type=jnp.float32
    )
    return (weighted_sum, row_max, weight_total)


def node_partial(all_queries, members, page_pool, page_list, node_length, part_index):
    token_width = page_pool.shape[2]
    head_width = page_pool.shape[3]
    query_rows = jnp.take(all_queries, members, axis=0, mode="fill", fill_value=0)
    node_block = jnp.take(page_pool, page_list, axis=1)
    node_keys = node_block[0].reshape(-1, head_width)
    node_values = node_block[1].reshape(-1, head_width)
    positions = (
        jnp.arange(page_list.shape[0])[:, None] * PAGE
        + part_index * token_width
        + jnp.arange(token_width)[None, :]
    ).reshape(-1)
    usable = (positions < node_length)[None, None, :]
    scores = jnp.einsum(
        "sgd,ld->sgl", query_rows, node_keys, preferred_element_type=jnp.float32
    ) * head_width ** (-0.5)
    return weigh_scores(scores, usable, node_values, "sgl,ld->sgd")


def spread_rows(member_ids, partial_value, requests):
    weighted_sum, row_max, weight_total = partial_value
    flat_ids = member_ids.reshape(-1)
    groups = row_max.shape[-1]
    head_width = weighted_sum.shape[-1]
    sum_rows = (
        jnp.zeros((requests, groups, head_width), jnp.float32)
        .at[flat_ids]
        .set(weighted_sum.reshape(-1, groups, head_width), mode="drop")
    )
    max_rows = (
        jnp.zeros((requests, groups), jnp.float32)
        .at[flat_ids]
        .set(row_max.reshape(-1, groups), mode="drop")
    )
    total_rows = (
        jnp.zeros((requests, groups), jnp.float32)
        .at[flat_ids]
        .set(weight_total.reshape(-1, groups), mode="drop")
    )
    return (sum_rows, max_rows, total_rows)


def shards(
    queries,
    new_kv,
    residual,
    out_weight,
    norm_gain,
    router,
    expert_in,
    expert_out,
    node_cache,
    leaf_cache,
    slot_request,
    request_branch,
    branch_parent,
    root_owner,
    branch_owner,
    root_pages,
    branch_pages,
    root_len,
    branch_len,
    leaf_len,
    routes,
):
    head_width = node_cache.shape[-1]
    token_width = node_cache.shape[-2]
    part_count = lax.axis_size("mp") // KVH
    group_size = HEADS // KVH
    own_heads = HEADS // lax.axis_size("mp")
    local_rows = queries.shape[0]
    requests = slot_request.shape[0]
    branches = branch_parent.shape[0]
    root_count = root_owner.shape[0]
    kid_count = branches // root_count
    mp_index = lax.axis_index("mp")
    dp_index = lax.axis_index("dp")
    kv_head = mp_index // part_count
    part_index = mp_index % part_count
    group_queries = lax.dynamic_slice_in_dim(
        queries, kv_head * group_size * head_width, group_size * head_width, 1
    )
    all_queries = lax.all_gather(group_queries, "dp", axis=0, tiled=True).reshape(
        requests, group_size, head_width
    )
    slot_branch = jnp.take(request_branch, slot_request)
    branch_order = jnp.argsort(slot_branch, stable=True)
    branch_counts = jnp.sum(
        (slot_branch[None, :] == jnp.arange(branches)[:, None]).astype(jnp.int32), axis=1
    )
    branch_starts = jnp.cumsum(branch_counts) - branch_counts
    offsets = jnp.arange(BR_CAP)[None, :]
    spots = jnp.minimum(branch_starts[:, None] + offsets, requests - 1)
    members = jnp.where(offsets < branch_counts[:, None], jnp.take(branch_order, spots), requests)
    kids_of = jnp.argsort(branch_parent, stable=True).reshape(root_count, kid_count)
    page_pool = node_cache[:, :, 0]
    local_roots = jnp.nonzero(root_owner == dp_index, size=ROOT_DEV)[0]
    local_branches = jnp.nonzero(branch_owner == dp_index, size=BR_DEV)[0]

    def root_work(root_node):
        member_ids = jnp.take(members, kids_of[root_node], axis=0).reshape(-1)
        return (
            member_ids,
            node_partial(
                all_queries,
                member_ids,
                page_pool,
                root_pages[root_node],
                root_len[root_node],
                part_index,
            ),
        )

    def branch_work(branch_node):
        member_ids = members[branch_node]
        return (
            member_ids,
            node_partial(
                all_queries,
                member_ids,
                page_pool,
                branch_pages[branch_node],
                branch_len[branch_node],
                part_index,
            ),
        )

    root_ids, root_partial = jax.vmap(root_work)(local_roots)
    branch_ids, branch_partial = jax.vmap(branch_work)(local_branches)
    root_sum, root_max, root_total = spread_rows(root_ids, root_partial, requests)
    branch_sum, branch_max, branch_total = spread_rows(branch_ids, branch_partial, requests)
    returned = (
        lax.psum_scatter(root_sum, "dp", scatter_dimension=0, tiled=True),
        lax.psum_scatter(root_max, "dp", scatter_dimension=0, tiled=True),
        lax.psum_scatter(root_total, "dp", scatter_dimension=0, tiled=True),
        lax.psum_scatter(branch_sum, "dp", scatter_dimension=0, tiled=True),
        lax.psum_scatter(branch_max, "dp", scatter_dimension=0, tiled=True),
        lax.psum_scatter(branch_total, "dp", scatter_dimension=0, tiled=True),
    )
    leaf_block = leaf_cache[:, :, 0]
    mine_queries = group_queries.reshape(local_rows, group_size, head_width)
    leaf_places = part_index * token_width + jnp.arange(token_width)
    leaf_usable = (leaf_places[None, :] < leaf_len[:, None])[:, None, :]
    leaf_scores = jnp.einsum(
        "rgd,rtd->rgt", mine_queries, leaf_block[0], preferred_element_type=jnp.float32
    ) * head_width ** (-0.5)
    leaf_partial = weigh_scores(leaf_scores, leaf_usable, leaf_block[1], "rgt,rtd->rgd")
    running = merge_partials(
        (returned[0], returned[1], returned[2]), (returned[3], returned[4], returned[5])
    )
    running = merge_partials(running, leaf_partial)
    bit_count = part_count.bit_length() - 1
    for bit_index in reversed(range(bit_count)):
        half_heads = running[1].shape[1] // 2
        upper_side = mp_index >> bit_index & 1 == 1
        kept_half = tuple(
            (
                jnp.where(upper_side, component[:, half_heads:], component[:, :half_heads])
                for component in running
            )
        )
        sent_half = tuple(
            (
                jnp.where(upper_side, component[:, :half_heads], component[:, half_heads:])
                for component in running
            )
        )
        received = partner((sent_half[0], sent_half[1], sent_half[2]), "mp", bit_index)
        running = merge_partials(kept_half, received)
    own_queries = lax.dynamic_slice_in_dim(
        queries, mp_index * own_heads * head_width, own_heads * head_width, 1
    ).reshape(local_rows, own_heads, head_width)
    fresh_kv = lax.dynamic_slice_in_dim(new_kv, kv_head * head_width, head_width, 2)
    self_score = jnp.einsum(
        "rhd,rd->rh", own_queries, fresh_kv[0], preferred_element_type=jnp.float32
    ) * head_width ** (-0.5)
    weighted, row_max, weight_total = running
    common_max = jnp.maximum(row_max, self_score)
    old_factor = jnp.exp(row_max - common_max)
    new_factor = jnp.exp(self_score - common_max)
    weighted = (
        weighted * old_factor[..., None]
        + new_factor[..., None] * fresh_kv[1].astype(jnp.float32)[:, None, :]
    )
    weight_total = weight_total * old_factor + new_factor
    attended = (
        (weighted / weight_total[..., None])
        .astype(jnp.bfloat16)
        .reshape(local_rows, own_heads * head_width)
    )
    projected = jnp.dot(attended, out_weight, preferred_element_type=jnp.float32)
    slice_width = residual.shape[1]
    start_col = mp_index * slice_width
    own_cols = lax.dynamic_slice_in_dim(projected, start_col, slice_width, 1) + residual.astype(
        jnp.float32
    )
    projected = lax.dynamic_update_slice_in_dim(projected, own_cols, start_col, 1)
    hidden = lax.psum(projected.astype(jnp.bfloat16), "mp").astype(jnp.float32)
    inv_rms = lax.rsqrt(jnp.mean(hidden * hidden, axis=1) + NORM_EPS)
    normed = (hidden * inv_rms[:, None] * norm_gain[None, :]).astype(jnp.bfloat16)
    kept_cols = lax.dynamic_slice_in_dim(hidden, start_col, slice_width, 1)
    logits = jnp.dot(normed, router, preferred_element_type=jnp.float32)
    route_hits = routes[:, :, None] == jnp.arange(EXPERTS)[None, None, :]
    chosen = jnp.sum(jnp.where(route_hits, logits[:, None, :], 0.0), axis=2)
    gate_weights = jax.nn.softmax(chosen, axis=1)
    pair_experts = routes.reshape(-1)
    pair_onehot = (pair_experts[:, None] == jnp.arange(EXPERTS)[None, :]).astype(jnp.int32)
    pair_rank = jnp.sum((jnp.cumsum(pair_onehot, axis=0) - 1) * pair_onehot, axis=1)
    pair_slot = pair_experts * E_CAP + pair_rank
    slot_source = (
        jnp.full((EXPERTS * E_CAP,), local_rows, jnp.int32)
        .at[pair_slot]
        .set(jnp.arange(pair_experts.shape[0], dtype=jnp.int32) // TOP)
    )
    padded = jnp.concatenate([normed, jnp.zeros((1, normed.shape[1]), jnp.bfloat16)], axis=0)
    dp_count = lax.axis_size("dp")
    local_experts = expert_in.shape[0]
    outgoing = jnp.take(padded, slot_source, axis=0).reshape(
        dp_count, local_experts * E_CAP, normed.shape[1]
    )
    incoming = lax.all_to_all(outgoing, "dp", split_axis=0, concat_axis=0, tiled=True).reshape(
        dp_count, local_experts, E_CAP, normed.shape[1]
    )
    gate_up = jnp.einsum(
        "sjcd,jkfd->ksjcf", incoming, expert_in, preferred_element_type=jnp.float32
    )
    expert_hidden = (jax.nn.silu(gate_up[0]) * gate_up[1]).astype(jnp.bfloat16)
    expert_partial = jnp.einsum(
        "sjcf,jfd->sjcd", expert_hidden, expert_out, preferred_element_type=jnp.float32
    )
    summed = lax.psum_scatter(
        expert_partial.astype(jnp.bfloat16), "mp", scatter_dimension=3, tiled=True
    )
    returned_rows = lax.all_to_all(
        summed.reshape(dp_count, local_experts * E_CAP, slice_width),
        "dp",
        split_axis=0,
        concat_axis=0,
        tiled=True,
    )
    results = jnp.take(returned_rows.reshape(-1, slice_width), pair_slot, axis=0).reshape(
        local_rows, TOP, slice_width
    )
    layer_out = kept_cols + jnp.sum(gate_weights[:, :, None] * results.astype(jnp.float32), axis=1)
    return layer_out.astype(jnp.bfloat16)


def solution(mesh):
    placed = (
        P("dp", None),
        P(None, "dp", None),
        P("dp", "mp"),
        P("mp", None),
        P(),
        P(),
        P("dp", None, "mp", None),
        P("dp", "mp", None),
        P(None, "dp", "mp", None, None),
        P(None, "dp", "mp", None, None),
        P(),
        P(),
        P(),
        P(),
        P(),
        P(),
        P(),
        P(),
        P(),
        P("dp"),
        P("dp", None),
    )
    return jax.shard_map(
        shards, mesh=mesh, in_specs=placed, out_specs=P("dp", "mp"), check_vma=False
    )
```

profile of v0, /device:TPU:0, one launch (start us, length us, event | category | flops | bytes accessed | tf_op | source)
XLA Modules:
  0.0 537.3 jit_solution(13685772760149976128)
XLA Ops:
  11.5 2.7 sort.34
  16.2 4.5 gather_fusion.1
  21.4 4.4 sort.35
  25.8 8.6 %gather_fusion.2 = s32[2048]{0:T(1024)S(1)} fusion(s32[1024]{0:T(1024)S(1)} %get-tuple-element.8, s32[2048]{0:T(1024)S(1)} %broadcast_clamp_fusion), kind=kCustom, calls=%fused_computation.2 | custom fusion | bytes 24576 | tf_op jit(solution)/shard_map/jit(_take)/gather | solution.py:139
  41.5 2.2 gather_fusion.7
  55.8 3.6 fusion.3
  59.6 2.0 scatter_custom_fusion.6
  62.8 2.0 scatter_custom_fusion.2
  65.9 1.9 scatter_custom_fusion.7
  68.2 1.9 scatter_custom_fusion.4
  70.2 3.5 fusion.8
  76.3 25.1 %scatter_fusion = f32[1024,4,128]{2,1,0:T(4,128)} fusion(f32[1024,4,128]{2,1,0:T(4,128)} %broadcast.701.clone.1, s32[256]{0:T(256)S(1)} %bitcast.192, f32[256,4,128]{2,1,0:T(4,128)S(1)} %copy.271), kind=kCustom, calls=%fused_computation.16 | custom fusion | bytes 1573888 | tf_op jit(solution)/shard_map/scatter | solution.py:73
  101.7 7.2 %scatter_fusion.1 = f32[1024,4,128]{2,1,0:T(4,128)S(1)} fusion(f32[1024,4,128]{2,1,0:T(4,128)S(1)} %broadcast.701.clone, s32[256]{0:T(256)S(1)} %bitcast.189, f32[256,4,128]{2,1,0:T(4,128)S(1)} %copy.286), kind=kCustom, calls=%fused_computation.20 | custom fusion | bytes 1573888 | tf_op jit(solution)/shard_map/scatter | solution.py:73
  110.6 2.9 fusion.89
  118.2 9.1 %reduce-scatter.16.cloned.1.call-done = f32[128,4]{1,0:T(8,128)} async-done(((f32[1024,4]{1,0:T(8,128)}), f32[128,4]{1,0:T(8,128)}) %reduce-scatter.16.cloned.1.call-update) | async-done | bytes 2064
  128.2 31.1 %reduce-scatter.22.cloned.1.call-done = f32[128,4]{1,0:T(8,128)} async-done(((f32[1024,4]{1,0:T(8,128)}), f32[128,4]{1,0:T(8,128)}) %reduce-scatter.22.cloned.1.call-update) | async-done | bytes 2064
  160.2 31.2 %reduce-scatter.18.cloned.1.call-done = f32[128,4]{1,0:T(8,128)} async-done(((f32[1024,4]{1,0:T(8,128)}), f32[128,4]{1,0:T(8,128)}) %reduce-scatter.18.cloned.1.call-update) | async-done | bytes 2064
  194.8 70.2 %all-reduce.11.cloned.1.call-done = (f32[1024,4,128]{2,1,0:T(4,128)}, f32[1024,4,128]{2,1,0:T(4,128)}) async-done(((f32[1024,4,128]{2,1,0:T(4,128)}, f32[1024,4,128]{2,1,0:T(4,128)}), (f32[1024,4,128]{2,1,0:T(4,128)}, f32[1024,4,128]{2,1,0:T(4,128)})) %all-reduce.11.cloned.1.call-update) | async-done | bytes 4194320
  265.0 2.4 fusion.22
  269.8 2.8 collective-permute-done.1
  273.4 2.0 fusion.51
  278.5 84.6 %all-reduce.9.cloned.1.call-done = bf16[128,4096]{1,0:T(8,128)(2,1)} async-done(((bf16[128,4096]{1,0:T(8,128)(2,1)}), bf16[128,4096]{1,0:T(8,128)(2,1)}) %all-reduce.9.cloned.1.call-update) | async-done | bytes 1048592 | tf_op jit(solution)/shard_map/psum | solution.py:243
  366.3 4.4 gather_fusion.13
  370.7 2.6 broadcast_select_fusion
  373.3 54.4 %all_to_all.10 = bf16[8,64,4096]{2,1,0:T(8,128)(2,1)S(1)} all-to-all(bf16[8,64,4096]{2,1,0:T(8,128)(2,1)S(1)} %broadcast_select_fusion), channel_id=1, replica_groups=mesh['dp'=8,'mp'=16] {'dp'}, dimensions={0} | all-to-all | bytes 8388608 | tf_op jit(solution)/shard_map/all_to_all | solution.py:266
  427.8 7.1 %fusion.13 = f32[2,8,1,64,512]{4,3,0,1,2:T(8,128)S(1)} fusion(bf16[1,2,512,4096]{3,2,1,0:T(8,128)(2,1)} %param.27, bf16[8,64,4096]{2,1,0:T(8,128)(2,1)S(1)} %all_to_all.10), kind=kOutput, calls=%fused_computation.46 | convolution fusion | flops 4294967296 | bytes 14680064 | tf_op jit(solution)/shard_map/sjcd,jkfd->ksjcf/dot_general | solution.py:269
  434.9 4.3 fusion.5
  440.2 1.7 fusion.90
  442.0 72.4 %reduce-scatter.14.cloned.1.call-done = bf16[8,1,64,256]{3,2,0,1:T(8,128)(2,1)} async-done(((bf16[8,1,64,4096]{3,2,0,1:T(8,128)(2,1)}), bf16[8,1,64,256]{3,2,0,1:T(8,128)(2,1)}) %reduce-scatter.14.cloned.1.call-update) | async-done | bytes 262160 | tf_op jit(solution)/shard_map/reduce_scatter | solution.py:276
  514.4 4.2 all-to-all-start.1
  519.4 2.8 convert_element_type.90
  522.2 4.0 all-to-all-done.1
  (240 shorter events, 58.5 us)
Async XLA Ops:
  6.5 34.9 %copy-start = (bf16[2,96,1,64,128]{4,3,2,1,0:T(8,128)(2,1)S(1)}, bf16[2,96,1,64,128]{4,3,2,1,0:T(8,128)(2,1)}, u32[]{:S(2)}) copy-start(bf16[2,96,1,64,128]{4,3,2,1,0:T(8,128)(2,1)} %param.29) | copy-start | bytes 9437188
  6.5 14.2 %copy-start.16 = (s32[1024]{0:T(1024)S(1)}, s32[1024]{0:T(1024)}, u32[]{:S(2)}) copy-start(s32[1024]{0:T(1024)} %param.31) | copy-start | bytes 12292
  6.5 9.7 %copy-start.2 = (s32[1024]{0:T(1024)S(1)}, s32[1024]{0:T(1024)}, u32[]{:S(2)}) copy-start(s32[1024]{0:T(1024)} %param.32) | copy-start | bytes 12292
  6.5 45.4 %all-gather.2.cloned.1.call-start = ((), (), s32[]{:S(2)}) async-start(), calls=%async_computation.7 | async-start | bytes 1179648 | tf_op jit(solution)/shard_map/all_gather | solution.py:128
  8.3 109.0 %reduce-scatter.20.cloned.1.call-start = ((), (), s32[]{:S(2)}) async-start(), calls=%async_computation.12 | async-start | bytes 589824
  25.8 9.7 %copy-start.17 = (s32[16,32]{1,0:T(8,128)S(1)}, s32[16,32]{1,0:T(8,128)}, u32[]{:S(2)}) copy-start(s32[16,32]{1,0:T(8,128)} %param.36) | copy-start | bytes 6148
  25.8 10.3 %copy-start.21 = (s32[64]{0:T(128)S(1)}, s32[64]{0:T(128)}, u32[]{:S(2)}) copy-start(s32[64]{0:T(128)} %param.35) | copy-start | bytes 772
  25.8 13.7 %copy-start.18 = (s32[64,4]{0,1:T(4,128)S(1)}, s32[64,4]{0,1:T(4,128)}, u32[]{:S(2)}) copy-start(s32[64,4]{0,1:T(4,128)} %param.37) | copy-start | bytes 3076
  25.8 14.6 %copy-start.15 = (s32[128,2]{0,1:T(2,128)S(1)}, s32[128,2]{0,1:T(2,128)}, u32[]{:S(2)}) copy-start(s32[128,2]{0,1:T(2,128)} %param.41) | copy-start | bytes 3076
  41.5 5.0 copy-start.3
  41.5 5.6 %copy-start.4 = (s32[64]{0:T(128)S(1)}, s32[64]{0:T(128)}, u32[]{:S(2)}) copy-start(s32[64]{0:T(128)} %param.39) | copy-start | bytes 772
  45.3 5.1 copy-start.7
  59.4 5.5 %copy-start.11 = (bf16[8,1,4,64,128]{4,3,2,0,1:T(8,128)(2,1)S(1)}, bf16[8,1,4,64,128]{4,3,2,0,1:T(8,128)(2,1)}, u32[]{:S(2)}) copy-start(bf16[8,1,4,64,128]{4,3,2,0,1:T(8,128)(2,1)} %get-tuple-element.32) | copy-start | bytes 1572868
  61.6 65.7 %reduce-scatter.16.cloned.1.call-start = ((), (), s32[]{:S(2)}) async-start(), calls=%async_computation.10 | async-start | bytes 589824
  64.8 5.4 %copy-start.10 = (bf16[2,1,32,64,128]{4,3,2,0,1:T(8,128)(2,1)S(1)}, bf16[2,1,32,64,128]{4,3,2,0,1:T(8,128)(2,1)}, u32[]{:S(2)}) copy-start(bf16[2,1,32,64,128]{4,3,2,0,1:T(8,128)(2,1)} %get-tuple-element.29) | copy-start | bytes 3145732
  64.8 94.4 %reduce-scatter.22.cloned.1.call-start = ((), (), s32[]{:S(2)}) async-start(), calls=%async_computation.13 | async-start | bytes 589824
  67.9 123.5 %reduce-scatter.18.cloned.1.call-start = ((), (), s32[]{:S(2)}) async-start(), calls=%async_computation.11 | async-start | bytes 589824
  70.2 194.9 %all-reduce.11.cloned.1.call-start = ((), (), s32[]{:S(2)}) async-start(), calls=%async_computation.14 | async-start | bytes 8388608
  101.7 8.7 %copy-start.9 = (bf16[128,512]{1,0:T(8,128)(2,1)S(1)}, bf16[128,512]{1,0:T(8,128)(2,1)}, u32[]{:S(2)}) copy-start(bf16[128,512]{1,0:T(8,128)(2,1)} %constant_dynamic-slice_fusion.1) | copy-start | bytes 393220
  101.7 8.8 %copy-start.19 = (s32[128]{0:T(128)S(1)}, s32[128]{0:T(128)}, u32[]{:S(2)}) copy-start(s32[128]{0:T(128)} %param.40) | copy-start | bytes 1540
  110.3 5.7 %copy-start.22 = (u32[128]{0:T(128)S(1)}, u32[128]{0:T(128)}, u32[]{:S(2)}) copy-start(u32[128]{0:T(128)} %constant.357) | copy-start | bytes 1540
  110.3 252.8 %all-reduce.9.cloned.1.call-start = ((), (), s32[]{:S(2)}) async-start(), calls=%async_computation.8 | async-start | bytes 2097152 | tf_op jit(solution)/shard_map/psum | solution.py:243
  192.3 76.9 %collective-permute-start = (f32[128,2]{0,1:T(2,128)S(1)}, f32[128,2]{0,1:T(2,128)S(1)}, u32[]{:S(2)}, u32[]{:S(2)}) collective-permute-start(f32[128,2]{0,1:T(2,128)S(1)} %get-tuple-element.36), channel_id=1, source_target_pairs={{0,1},{1,0},{2,3},{3,2},{4,5},{5,4},{6,7},{7,6},{8,9},{9,8},{10,11... | collective-permute-start | bytes 3080 | tf_op jit(solution)/shard_map/ppermute | solution.py:22
  194.0 75.2 %collective-permute-start.2 = (f32[128,2]{0,1:T(2,128)S(1)}, f32[128,2]{0,1:T(2,128)S(1)}, u32[]{:S(2)}, u32[]{:S(2)}) collective-permute-start(f32[128,2]{0,1:T(2,128)S(1)} %broadcast_select_fusion.6), channel_id=1, source_target_pairs={{0,1},{1,0},{2,3},{3,2},{4,5},{5,4},{6,7},{7,6},{8,9},{9,8},{10,11... | collective-permute-start | bytes 3080 | tf_op jit(solution)/shard_map/ppermute | solution.py:22
  267.5 8.0 %copy-start.12 = (bf16[128,256]{1,0:T(8,128)(2,1)S(1)}, bf16[128,256]{1,0:T(8,128)(2,1)}, u32[]{:S(2)}) copy-start(bf16[128,256]{1,0:T(8,128)(2,1)} %param.23) | copy-start | bytes 196612
  267.6 5.0 collective-permute-start.1
  275.5 89.2 %copy-start.14 = (f32[4096]{0:T(1024)S(1)}, f32[4096]{0:T(1024)}, u32[]{:S(2)}) copy-start(f32[4096]{0:T(1024)} %param.25) | copy-start | bytes 49156
  276.7 237.7 %reduce-scatter.14.cloned.1.call-start = ((), (), s32[]{:S(2)}) async-start(), calls=%async_computation.9 | async-start | bytes 4456448 | tf_op jit(solution)/shard_map/reduce_scatter | solution.py:276
  366.2 4.5 copy-start.6
  427.8 7.1 %copy-start.20 = (bf16[1,512,4096]{2,1,0:T(8,128)(2,1)S(1)}, bf16[1,512,4096]{2,1,0:T(8,128)(2,1)}, u32[]{:S(2)}) copy-start(bf16[1,512,4096]{2,1,0:T(8,128)(2,1)} %param.28) | copy-start | bytes 12582916
  440.2 90.2 %copy-start.1 = (bf16[2,96,1,64,128]{4,3,2,1,0:T(8,128)(2,1)S(1)}, bf16[2,96,1,64,128]{4,3,2,1,0:T(8,128)(2,1)}, u32[]{:S(2)}) copy-start(bf16[2,96,1,64,128]{4,3,2,1,0:T(8,128)(2,1)} %param.29) | copy-start | bytes 9437188
  514.4 11.8 %all-to-all-start.1 = ((bf16[8,64,256]{2,1,0:T(8,128)(2,1)}), bf16[8,64,256]{2,1,0:T(8,128)(2,1)S(1)}, u32[]{:S(2)}, u32[]{:S(2)}) async-start(bf16[8,64,256]{2,1,0:T(8,128)(2,1)} %bitcast.176), calls=%async_computation.2 | async-start | bytes 524288 | tf_op jit(solution)/shard_map/all_to_all | solution.py:279
  (3 other events, 5.8 us)
Sparse Core Ops, SparseCore 0:
  9.1 25.8 all-gather.1
  61.7 33.2 reduce-scatter.19
  97.5 29.7 reduce-scatter.15
  129.5 29.6 reduce-scatter.21
  161.6 29.6 reduce-scatter.17
  193.6 71.3 all-reduce.10
  276.8 86.2 all-reduce.8
  439.3 75.0 reduce-scatter.13
where the time goes:
time: 539 us; the launch traced here: 537 us
  waiting for transfers between devices  306 us (57%)
  local copies, waits for them, and re-layouts  90.4 us (17%)
  blocking collectives  54.4 us (10%)
  other arithmetic  37 us (7%)
  matrix products  26.4 us (5%)
  between operations  14.9 us (3%)
  starting transfers between devices  8.45 us (2%)
    unnamed x13, waiting for transfers between devices  142 us
    psum x1, waiting for transfers between devices, shards(): hidden = lax.psum(projected.astype(jnp.bfloat16), 'mp').astype(jnp.float32)  84.6 us
    reduce_scatter x1, waiting for transfers between devices, shards(): lax.psum_scatter(expert_partial.astype(jnp.bfloat16), 'mp', scatter_dimen...  72.4 us
    all_to_all x1, blocking collectives, shards(): lax.all_to_all(outgoing, 'dp', split_axis=0, concat_axis=0, tiled=True)  54.4 us
    scatter x2, local copies, waits for them, and re-layouts, spread_rows(): sum_rows = jnp.zeros((requests, groups, head_width), jnp.float32).at[flat...  32.3 us
  transfers between devices with their start and end apart: 12, of which 8 were waited for; matrix products, arithmetic and copies ran while one was open for 21% of the time, Pallas kernels for 0%

commit v1 on v0

v1 whole, which is shorter than its diff:
```python
import jax
import jax.numpy as jnp
from jax import lax
from jax.experimental import pallas as pl
from jax.experimental.pallas import tpu as pltpu
from jax.sharding import PartitionSpec as P

EXPERTS = 8
PAGE = 128
ROOT_DEV = 2
BR_DEV = 8
BR_CAP = 32
E_CAP = 64

MASKED_SCORE = -1e30
NORM_EPS = 1e-05

BF = jnp.bfloat16
F32 = jnp.float32
MESH = pl.DeviceIdType.MESH
ROWS = 128
PART_ROWS = ((0, 48), (48, 48), (96, 32))
AXES = ("x", "y", "z")


def place():
    dp = lax.axis_index("dp")
    mp = lax.axis_index("mp")
    return {"x": dp // 2, "c": dp % 2, "y": mp // 4, "z": mp % 4}


def device_of(at, **moved):
    at = {**at, **moved}
    return (at["x"] * 2 + at["c"], at["y"] * 4 + at["z"])


def step_along(at, axis, by):
    return device_of(at, **{axis: (at[axis] + by) % 4})


def greet(peers):
    barrier = pltpu.get_barrier_semaphore()
    for peer in peers:
        pl.semaphore_signal(barrier, inc=1, device_id=peer, device_id_type=MESH)
    pl.semaphore_wait(barrier, len(peers))


def remote(src, dst, sems, key, device):
    return pltpu.make_async_remote_copy(
        src_ref=src,
        dst_ref=dst,
        send_sem=sems[0].at[key],
        recv_sem=sems[1].at[key],
        device_id=device,
        device_id_type=MESH,
    )


def all_peers(at):
    return [step_along(at, axis, by) for axis in AXES for by in (1, 3)] + [
        device_of(at, c=1 - at["c"])
    ]


def gather_kernel(own_ref, buf_ref, local_sem, send_sem, recv_sem):
    at = place()
    sems = (send_sem, recv_sem)
    greet(all_peers(at))
    sibling = device_of(at, c=1 - at["c"])

    def slab(part, order, phase, value, half, core):
        index = {"x": at["x"], "y": at["y"], "z": at["z"]}
        for axis in order[:phase]:
            index[axis] = slice(None)
        index[order[phase]] = value
        row, rows = PART_ROWS[part]
        return buf_ref.at[
            index["x"],
            core,
            index["y"],
            index["z"],
            half,
            pl.ds(row, rows),
            :,
        ]

    both = slice(None)
    mine = buf_ref.at[at["x"], at["c"], at["y"], at["z"]]
    local = pltpu.make_async_copy(own_ref, mine, local_sem)
    local.start()
    orders = [AXES[part:] + AXES[:part] for part in range(3)]
    started = []

    def send(src, dst, key, device):
        copy = remote(src, dst, sems, key, device)
        copy.start()
        started.append(copy)

    def arrive(ref, key):
        remote(ref, ref, sems, key, sibling).wait_recv()

    core = at["c"]
    for phase in range(3):
        for part in range(3):
            order = orders[part]
            axis = order[phase]
            v = at[axis]
            key = part * 16 + phase * 4
            ref = slab(part, order, phase, v, both, core)
            if phase == 0:
                row, rows = PART_ROWS[part]
                src = own_ref.at[:, pl.ds(row, rows), :]
            else:
                src = ref
            send(src, ref, key, step_along(at, axis, 1))
            send(src, ref, key + 1, step_along(at, axis, 3))
            if phase == 2:
                send(src, ref, part * 16 + 12, sibling)
        for part in range(3):
            order = orders[part]
            axis = order[phase]
            v = at[axis]
            key = part * 16 + phase * 4
            low = slab(part, order, phase, (v + 3) % 4, both, core)
            arrive(low, key)
            first = slab(part, order, phase, (v + 3) % 4, 0, core)
            send(first, first, key + 2, step_along(at, axis, 1))
            high = slab(part, order, phase, (v + 1) % 4, both, core)
            arrive(high, key + 1)
            second = slab(part, order, phase, (v + 1) % 4, 1, core)
            send(second, second, key + 3, step_along(at, axis, 3))
            if phase == 2:
                send(low, low, part * 16 + 13, sibling)
                send(high, high, part * 16 + 14, sibling)
        if phase == 0:
            local.wait()
        for part in range(3):
            order = orders[part]
            axis = order[phase]
            v = at[axis]
            key = part * 16 + phase * 4
            far = (v + 2) % 4
            arrive(slab(part, order, phase, far, 0, core), key + 2)
            arrive(slab(part, order, phase, far, 1, core), key + 3)
            if phase == 2:
                ref = slab(part, order, phase, far, both, core)
                send(ref, ref, part * 16 + 15, sibling)
    for part in range(3):
        order = orders[part]
        v = at[order[2]]
        for key, by in ((12, 0), (13, 3), (14, 1), (15, 2)):
            arrive(slab(part, order, 2, (v + by) % 4, both, 1 - core), part * 16 + key)
    for copy in started:
        copy.wait_send()


def gather_rows(own):
    return pl.pallas_call(
        gather_kernel,
        out_shape=jax.ShapeDtypeStruct((4, 2, 4, 4, 2, ROWS, 128), BF),
        in_specs=[pl.BlockSpec(memory_space=pl.ANY)],
        out_specs=pl.BlockSpec(memory_space=pl.ANY),
        scratch_shapes=[
            pltpu.SemaphoreType.DMA,
            pltpu.SemaphoreType.DMA((48,)),
            pltpu.SemaphoreType.DMA((48,)),
        ],
        compiler_params=pltpu.CompilerParams(collective_id=1, has_side_effects=True),
        name="gather_rows",
    )(own)


FF_STEPS = 2


def expert_kernel(
    buf_ref, rank_ref, other_ref, mine_ref, gain_ref, router_ref, up_ref, down_ref,
    out_ref, rows_ref, gate_ref, total_ref, block_ref, block_sem,
):
    step = pl.program_id(0)
    cap = E_CAP

    def fetch(block, slot):
        return pltpu.make_async_copy(
            buf_ref.at[block // 2, block % 2], block_ref.at[slot], block_sem.at[slot]
        )

    @pl.when(step == 0)
    def _():
        fetch(0, 0).start()

        def body(block, _):
            slot = lax.rem(block, 2)

            @pl.when(block < 7)
            def _():
                fetch(block + 1, 1 - slot).start()

            fetch(block, slot).wait()
            pick = (
                lax.broadcasted_iota(jnp.int32, (cap, ROWS), 0) == rank_ref[pl.ds(block, 1), :]
            ).astype(BF)
            squares = jnp.zeros((cap, 1), F32)
            pieces = []
            for y in range(4):
                for z in range(4):
                    whole = jnp.concatenate([block_ref[slot, y, z, 0], block_ref[slot, y, z, 1]], axis=1)
                    piece = jnp.dot(pick, whole, preferred_element_type=F32)
                    squares += jnp.sum(piece * piece, axis=1, keepdims=True)
                    pieces.append(piece.astype(BF))
            scale = lax.rsqrt(squares / (32.0 * 128.0) + NORM_EPS)
            base = pl.multiple_of(block * cap, cap)
            for i, piece in enumerate(pieces):
                cols = pl.ds(i * 256, 256)
                rows_ref[pl.ds(base, cap), cols] = (
                    piece.astype(F32) * scale * gain_ref[0:1, cols]
                ).astype(BF)
            return 0

        lax.fori_loop(0, 8, body, 0)
        logits = jnp.dot(rows_ref[...], router_ref[...], preferred_element_type=F32)
        lane = lax.broadcasted_iota(jnp.int32, logits.shape, 1)
        here = jnp.sum(jnp.where(lane == mine_ref[0, 0], logits, 0.0), axis=1, keepdims=True)
        there = jnp.sum(jnp.where(lane == other_ref[...], logits, 0.0), axis=1, keepdims=True)
        most = jnp.maximum(here, there)
        here = jnp.exp(here - most)
        there = jnp.exp(there - most)
        gate_ref[...] = jnp.broadcast_to(here / (here + there), gate_ref.shape)

    width = up_ref.shape[1]
    contract = (((1,), (1,)), ((), ()))
    gate = lax.dot_general(rows_ref[...], up_ref[0], contract, preferred_element_type=F32)
    up = lax.dot_general(rows_ref[...], up_ref[1], contract, preferred_element_type=F32)
    hidden = (gate / (1.0 + jnp.exp(-gate)) * up).astype(BF)

    def piece(i, last):
        partial = jnp.dot(hidden, down_ref[:, i * 256 : (i + 1) * 256], preferred_element_type=F32)
        if FF_STEPS > 1:
            if last:
                partial += total_ref[i]
            else:
                total_ref[i] = partial
        if last:
            scaled = (partial * gate_ref[:, 0:1]).astype(BF)
            for half in range(2):
                out_ref[:, i, half] = scaled[:, half * 128 : (half + 1) * 128].reshape(8, cap, 128)

    for last in (False, True):
        @pl.when((step == FF_STEPS - 1) == last)
        def _():
            for i in range(16):
                piece(i, last)


def run_experts(buf, rank, other, mine, gain, router, expert_in, expert_out):
    width = expert_in.shape[1] // FF_STEPS
    deep = expert_in.shape[2]
    return pl.pallas_call(
        expert_kernel,
        grid=(FF_STEPS,),
        out_shape=jax.ShapeDtypeStruct((8, 16, 2, E_CAP, 128), BF),
        in_specs=[
            pl.BlockSpec(memory_space=pl.ANY),
            pl.BlockSpec((8, ROWS), lambda f: (0, 0)),
            pl.BlockSpec((8 * E_CAP, 1), lambda f: (0, 0)),
            pl.BlockSpec(memory_space=pltpu.SMEM),
            pl.BlockSpec((1, deep), lambda f: (0, 0)),
            pl.BlockSpec((deep, EXPERTS), lambda f: (0, 0)),
            pl.BlockSpec((2, width, deep), lambda f: (0, f, 0)),
            pl.BlockSpec((width, deep), lambda f: (f, 0)),
        ],
        out_specs=pl.BlockSpec((8, 16, 2, E_CAP, 128), lambda f: (0, 0, 0, 0, 0)),
        scratch_shapes=[
            pltpu.VMEM((8 * E_CAP, deep), BF),
            pltpu.VMEM((8 * E_CAP, 128), F32),
            pltpu.VMEM((16, 8 * E_CAP, 256), F32),
            pltpu.VMEM((2, 4, 4, 2, ROWS, 128), BF),
            pltpu.SemaphoreType.DMA((2,)),
        ],
        compiler_params=pltpu.CompilerParams(
            vmem_limit_bytes=56 * 2**20, dimension_semantics=("arbitrary",)
        ),
        cost_estimate=pl.CostEstimate(
            flops=6 * 512 * 512 * 4096, bytes_accessed=25 * 2**20, transcendentals=512 * 512
        ),
        name="run_experts",
    )(buf, rank, other, mine, gain, router, expert_in, expert_out)


def return_kernel(
    part_ref, rank_ref, kept_ref, out_ref,
    theirs_ref, sum_ref, half1, full1, half2, full2, half3, full3, sib_send, sib_recv, send_sem, recv_sem,
):
    at = place()
    greet(all_peers(at))
    sems = (send_sem, recv_sem)
    sibling = device_of(at, c=1 - at["c"])
    core = at["c"]
    cross = pltpu.make_async_remote_copy(
        src_ref=part_ref.at[:, 1 - core],
        dst_ref=theirs_ref,
        send_sem=sib_send,
        recv_sem=sib_recv,
        device_id=sibling,
        device_id_type=MESH,
    )
    cross.start()
    cross.wait()
    lane = lax.broadcasted_iota(jnp.int32, (ROWS, E_CAP), 1)
    for x in range(4):
        spread = jnp.concatenate(
            [
                (rank_ref[x, 0] == lane).astype(BF),
                (rank_ref[x, 1] == lane).astype(BF),
            ],
            axis=1,
        )

        def body(i, _):
            y, z = i // 4, lax.rem(i, 4)
            for half in range(2):
                both = jnp.concatenate(
                    [part_ref[x, core, i, half], theirs_ref[x, i, half]], axis=0
                )
                sum_ref[x, y, z, half] = jnp.dot(
                    spread, both, preferred_element_type=F32
                ).astype(BF)
            return 0

        lax.fori_loop(0, 16, body, 0)

    started = []

    def send(src, dst, key, device):
        copy = remote(src, dst, sems, key, device)
        copy.start()
        started.append(copy)

    def arrive(ref, key):
        remote(ref, ref, sems, key, sibling).wait_recv()

    def finish(row, rows, half, total):
        spot = (pl.ds(row, rows), pl.ds(half * 128, 128))
        out_ref[spot] = (kept_ref[spot] + total).astype(BF)

    ring_reduce(
        at, sum_ref, AXES, [AXES[part:] + AXES[:part] for part in range(3)], PART_ROWS,
        (half1, half2, half3), (full1, full2, full3), send, arrive, 0, finish,
    )
    for copy in started:
        copy.wait_send()


def return_rows(partial, rank, kept):
    return pl.pallas_call(
        return_kernel,
        out_shape=jax.ShapeDtypeStruct((ROWS, 256), BF),
        in_specs=[pl.BlockSpec(memory_space=pltpu.VMEM)] * 3,
        out_specs=pl.BlockSpec(memory_space=pltpu.VMEM),
        scratch_shapes=[
            pltpu.VMEM((4, 16, 2, E_CAP, 128), BF),
            pltpu.VMEM((4, 4, 4, 2, ROWS, 128), BF),
            pltpu.VMEM((2, 4, 4, ROWS, 128), BF),
            pltpu.VMEM((2, 4, 4, 2, ROWS, 128), BF),
            pltpu.VMEM((2, 4, ROWS, 128), BF),
            pltpu.VMEM((2, 4, 2, ROWS, 128), BF),
            pltpu.VMEM((2, ROWS, 128), BF),
            pltpu.VMEM((2, 2, ROWS, 128), BF),
            pltpu.SemaphoreType.DMA,
            pltpu.SemaphoreType.DMA,
            pltpu.SemaphoreType.DMA((36,)),
            pltpu.SemaphoreType.DMA((36,)),
        ],
        compiler_params=pltpu.CompilerParams(
            collective_id=2, has_side_effects=True, vmem_limit_bytes=48 * 2**20
        ),
        name="return_rows",
    )(partial, rank, kept)


LOG2E = 1.4426950408889634


def query_kernel(queries_ref, all_ref, local_sem, send_sem, recv_sem):
    at = place()
    sems = (send_sem, recv_sem)
    sibling = device_of(at, c=1 - at["c"])
    right, left = step_along(at, "x", 1), step_along(at, "x", 3)
    greet([right, left, sibling])
    x, core = at["x"], at["c"]
    kv_head = lax.axis_index("mp") // 2
    own = queries_ref.at[:, pl.ds(pl.multiple_of(kv_head * 512, 512), 512)]
    local = pltpu.make_async_copy(own, all_ref.at[x, core], local_sem)
    local.start()
    started = []

    def send(src, dst, key, device):
        copy = remote(src, dst, sems, key, device)
        copy.start()
        started.append(copy)

    def arrive(ref, key):
        remote(ref, ref, sems, key, sibling).wait_recv()

    low, high, far = (x + 3) % 4, (x + 1) % 4, (x + 2) % 4
    upper, lower = pl.ds(0, 64), pl.ds(64, 64)
    mine = all_ref.at[x, core]
    send(own, mine, 0, right)
    send(own, mine, 1, left)
    send(own, mine, 4, sibling)
    from_low, from_high = all_ref.at[low, core], all_ref.at[high, core]
    arrive(from_low, 0)
    first = all_ref.at[low, core, upper]
    send(first, first, 2, right)
    arrive(from_high, 1)
    second = all_ref.at[high, core, lower]
    send(second, second, 3, left)
    send(from_low, from_low, 5, sibling)
    send(from_high, from_high, 6, sibling)
    for key, rows in ((2, upper), (3, lower)):
        ref = all_ref.at[far, core, rows]
        arrive(ref, key)
        send(ref, ref, key + 5, sibling)
    for key, ref in (
        (4, all_ref.at[x, 1 - core]),
        (5, all_ref.at[low, 1 - core]),
        (6, all_ref.at[high, 1 - core]),
        (7, all_ref.at[far, 1 - core, upper]),
        (8, all_ref.at[far, 1 - core, lower]),
    ):
        arrive(ref, key)
    local.wait()
    for copy in started:
        copy.wait_send()


def gather_queries(queries):
    return pl.pallas_call(
        query_kernel,
        out_shape=jax.ShapeDtypeStruct((4, 2, ROWS, 512), BF),
        in_specs=[pl.BlockSpec(memory_space=pl.ANY)],
        out_specs=pl.BlockSpec(memory_space=pl.ANY),
        scratch_shapes=[
            pltpu.SemaphoreType.DMA,
            pltpu.SemaphoreType.DMA((9,)),
            pltpu.SemaphoreType.DMA((9,)),
        ],
        compiler_params=pltpu.CompilerParams(collective_id=3, has_side_effects=True),
        name="gather_queries",
    )(queries)


SCALE2 = LOG2E * 128 ** (-0.5)
BY_ROW = (((1,), (1,)), ((), ()))


def node_kernel(
    local_ref, branch_id_ref, root_pages_ref, branch_pages_ref, root_len_ref, branch_len_ref, part_ref,
    all_ref, pages_ref, code_row_ref, code_col_ref,
    sum_ref, stat_ref,
    query_ref, acc_ref, max_ref, total_ref, node_sum_ref, node_stat_ref,
):
    part = part_ref[0]
    lane = lax.broadcasted_iota(jnp.int32, (1, 128), 1)

    def pick(kind, base, count):
        wanted = lax.broadcasted_iota(jnp.int32, (count, 1024), 0) + base
        chosen = (wanted == code_row_ref[kind : kind + 1, :]).astype(BF)
        return jnp.dot(chosen, all_ref[...], preferred_element_type=F32).astype(BF)

    def put(row, rows):
        stats = jnp.zeros((rows, 128), F32)
        for h in range(4):
            span = pl.ds(h * rows, rows)
            node_sum_ref[pl.ds(row, rows), h * 128 : (h + 1) * 128] = acc_ref[span, :].astype(BF)
            stats = jnp.where(lane == h, max_ref[span, 0:1], stats)
            stats = jnp.where(lane == 4 + h, total_ref[span, 0:1], stats)
        node_stat_ref[pl.ds(row, rows), :] = stats

    chunk = 8
    for k in range(ROOT_DEV):
        root = local_ref[k]
        length = root_len_ref[root]
        picked = pick(0, k * 128, 128)
        for h in range(4):
            query_ref[h * 128 : (h + 1) * 128, :] = picked[:, h * 128 : (h + 1) * 128]
        acc_ref[...] = jnp.zeros_like(acc_ref)
        max_ref[...] = jnp.full_like(max_ref, MASKED_SCORE)
        total_ref[...] = jnp.zeros_like(total_ref)
        used = (length - part * 64 + PAGE - 1) // PAGE
        steps = (used + chunk - 1) // chunk

        def body(i, _):
            ids = [root_pages_ref[root, i * chunk + j] for j in range(chunk)]
            keys = jnp.concatenate([pages_ref[0, page] for page in ids], axis=0)
            values = jnp.concatenate([pages_ref[1, page] for page in ids], axis=0)
            spot = lax.broadcasted_iota(jnp.int32, (1, chunk * 64), 1)
            spot = (i * chunk + spot // 64) * PAGE + part * 64 + spot % 64
            usable = spot < length
            for h in range(4):
                span = pl.ds(h * 128, 128)
                scores = lax.dot_general(query_ref[span, :], keys, BY_ROW, preferred_element_type=F32)
                scores = jnp.where(usable, scores * SCALE2, MASKED_SCORE)
                old = max_ref[span, 0:1]
                new = jnp.maximum(old, jnp.max(scores, axis=1, keepdims=True))
                weights = jnp.where(usable, jnp.exp2(scores - new), 0.0)
                fade = jnp.exp2(old - new)
                total = total_ref[span, 0:1] * fade + jnp.sum(weights, axis=1, keepdims=True)
                acc_ref[span, :] = acc_ref[span, :] * fade + jnp.dot(
                    weights.astype(BF), values, preferred_element_type=F32
                )
                max_ref[span, :] = jnp.broadcast_to(new, (128, 128))
                total_ref[span, :] = jnp.broadcast_to(total, (128, 128))
            return 0

        lax.fori_loop(0, steps, body, 0)
        put(k * 128, 128)

    def branch_body(b, _):
        branch = branch_id_ref[b]
        length = branch_len_ref[branch]
        picked = pick(1, b * 32, 32)
        stacked = jnp.concatenate([picked[:, h * 128 : (h + 1) * 128] for h in range(4)], axis=0)
        ids = [branch_pages_ref[branch, j] for j in range(4)]
        keys = jnp.concatenate([pages_ref[0, page] for page in ids], axis=0)
        values = jnp.concatenate([pages_ref[1, page] for page in ids], axis=0)
        spot = lax.broadcasted_iota(jnp.int32, (1, 256), 1)
        spot = (spot // 64) * PAGE + part * 64 + spot % 64
        usable = spot < length
        scores = lax.dot_general(stacked, keys, BY_ROW, preferred_element_type=F32)
        scores = jnp.where(usable, scores * SCALE2, MASKED_SCORE)
        top = jnp.max(scores, axis=1, keepdims=True)
        weights = jnp.where(usable, jnp.exp2(scores - top), 0.0)
        total = jnp.sum(weights, axis=1, keepdims=True)
        acc = jnp.dot(weights.astype(BF), values, preferred_element_type=F32)
        row = pl.multiple_of(256 + b * 32, 32)
        stats = jnp.zeros((32, 128), F32)
        for h in range(4):
            node_sum_ref[pl.ds(row, 32), h * 128 : (h + 1) * 128] = acc[h * 32 : (h + 1) * 32].astype(BF)
            stats = jnp.where(lane == h, top[h * 32 : (h + 1) * 32], stats)
            stats = jnp.where(lane == 4 + h, total[h * 32 : (h + 1) * 32], stats)
        node_stat_ref[pl.ds(row, 32), :] = stats
        return 0

    lax.fori_loop(0, BR_DEV, branch_body, 0)

    def spread_body(block, _):
        parts = []
        wanted = lax.broadcasted_iota(jnp.int32, (ROWS, 256), 1)
        for kind in range(2):
            code = code_col_ref[block, :, kind : kind + 1]
            chosen = wanted == code
            rows = slice(kind * 256, kind * 256 + 256)
            sums = jnp.dot(chosen.astype(BF), node_sum_ref[rows, :], preferred_element_type=F32)
            stats = jnp.dot(
                chosen.astype(F32),
                node_stat_ref[rows, :],
                preferred_element_type=F32,
                precision=lax.Precision.HIGHEST,
            )
            stats = jnp.where((lane < 4) & (code < 0), MASKED_SCORE, stats)
            parts.append((sums, stats))
        merged, stats = merge_blocks(parts[0], parts[1], 4)
        sum_ref[block] = merged.astype(BF)
        stat_ref[block] = stats
        return 0

    lax.fori_loop(0, 8, spread_body, 0)


def merge_blocks(one, two, heads):
    sums_one, stats_one = one
    sums_two, stats_two = two
    lane = lax.broadcasted_iota(jnp.int32, (1, 128), 1)
    pieces = []
    stats = jnp.zeros_like(stats_one)
    for h in range(heads):
        span = slice(h * 128, (h + 1) * 128)
        top_one, top_two = stats_one[:, h : h + 1], stats_two[:, h : h + 1]
        top = jnp.maximum(top_one, top_two)
        factor_one, factor_two = jnp.exp2(top_one - top), jnp.exp2(top_two - top)
        pieces.append(
            sums_one[:, span].astype(F32) * factor_one + sums_two[:, span].astype(F32) * factor_two
        )
        total = stats_one[:, 4 + h : 5 + h] * factor_one + stats_two[:, 4 + h : 5 + h] * factor_two
        stats = jnp.where(lane == h, top, stats)
        stats = jnp.where(lane == 4 + h, total, stats)
    return jnp.concatenate(pieces, axis=1), stats


def node_partials(local_roots, local_branches, tables, part, all_queries, pages, codes):
    return pl.pallas_call(
        node_kernel,
        out_shape=(
            jax.ShapeDtypeStruct((8, ROWS, 512), BF),
            jax.ShapeDtypeStruct((8, ROWS, 128), F32),
        ),
        in_specs=[pl.BlockSpec(memory_space=pltpu.SMEM)] * 7 + [pl.BlockSpec(memory_space=pltpu.VMEM)] * 4,
        out_specs=(pl.BlockSpec(memory_space=pltpu.VMEM),) * 2,
        scratch_shapes=[
            pltpu.VMEM((512, 128), BF),
            pltpu.VMEM((512, 128), F32),
            pltpu.VMEM((512, 128), F32),
            pltpu.VMEM((512, 128), F32),
            pltpu.VMEM((512, 512), BF),
            pltpu.VMEM((512, 128), F32),
        ],
        compiler_params=pltpu.CompilerParams(vmem_limit_bytes=40 * 2**20),
        name="node_partials",
    )(local_roots, local_branches, *tables, part, all_queries, pages, codes, codes.T.reshape(8, ROWS, 2))


def attend_kernel(
    sum_ref, stat_ref, query_ref, own_query_ref, leaf_ref, leaf_len_ref, fresh_ref, weight_ref, residual_ref,
    hidden_ref, narrow_ref,
    their_sum, their_stat, run_sum, run_stat, land_sum, land_stat, last_sum, last_stat,
    leaf_sum, leaf_stat, side_sum, side_stat, give_sum,
    proj_ref, half1, full1, half2, full2, send_sem, recv_sem,
):
    at = place()
    sems = (send_sem, recv_sem)
    sibling = device_of(at, c=1 - at["c"])
    beside = {**at, "z": at["z"] + 1 - 2 * (at["z"] % 2)}
    right, left = step_along(at, "x", 1), step_along(at, "x", 3)
    greet(all_peers(at))
    x, core = at["x"], at["c"]
    part = at["z"] % 2
    started = []

    def send(src, dst, key, device):
        copy = remote(src, dst, sems, key, device)
        copy.start()
        started.append(copy)

    def arrive(ref, key):
        remote(ref, ref, sems, key, sibling).wait_recv()

    send(sum_ref.at[:, 1 - core], their_sum, 0, sibling)
    send(stat_ref.at[:, 1 - core], their_stat, 1, sibling)
    lane = lax.broadcasted_iota(jnp.int32, (1, 128), 1)

    def leaf_body(i, _):
        base = pl.multiple_of(i * 8, 8)
        span = pl.ds(base, 8)
        heads = [query_ref[span, h * 128 : (h + 1) * 128] for h in range(4)]
        stacked = jnp.concatenate(heads, axis=0)
        keys = leaf_ref[0, span].reshape(512, 128)
        values = leaf_ref[1, span].reshape(512, 128)
        scores = lax.dot_general(
            stacked.astype(BF), keys, BY_ROW, preferred_element_type=F32
        )
        row = lax.broadcasted_iota(jnp.int32, (32, 512), 0) % 8
        col = lax.broadcasted_iota(jnp.int32, (32, 512), 1)
        lengths = jnp.concatenate([leaf_len_ref[span, 0:1]] * 4, axis=0)
        usable = (row == col // 64) & (part * 64 + col % 64 < lengths)
        scores = jnp.where(usable, scores * SCALE2, MASKED_SCORE)
        top = jnp.max(scores, axis=1, keepdims=True)
        weights = jnp.where(usable, jnp.exp2(scores - top), 0.0)
        total = jnp.sum(weights, axis=1, keepdims=True)
        acc = jnp.dot(weights.astype(BF), values, preferred_element_type=F32)
        stats = jnp.zeros((8, 128), F32)
        for h in range(4):
            leaf_sum[span, h * 128 : (h + 1) * 128] = acc[h * 8 : (h + 1) * 8]
            stats = jnp.where(lane == h, top[h * 8 : (h + 1) * 8], stats)
            stats = jnp.where(lane == 4 + h, total[h * 8 : (h + 1) * 8], stats)
        leaf_stat[span, :] = stats
        return 0

    lax.fori_loop(0, 16, leaf_body, 0)
    arrive(their_sum, 0)
    arrive(their_stat, 1)

    def cross_body(i, _):
        value = lax.rem(x + 2 + i, 4)
        merged, stats = merge_blocks(
            (sum_ref[value, core], stat_ref[value, core]), (their_sum[value], their_stat[value]), 4
        )
        run_sum[value] = merged.astype(BF)
        run_stat[value] = stats
        return 0

    def cross_merge(by):
        cross_body(by - 2, 0)

    low, high, far = (x + 3) % 4, (x + 1) % 4, (x + 2) % 4
    upper, lower = pl.ds(0, 64), pl.ds(64, 64)
    cross_merge(2)
    for key, rows, device in ((2, upper, right), (4, lower, left)):
        send(run_sum.at[far, rows], land_sum.at[rows], key, device)
        send(run_stat.at[far, rows], land_stat.at[rows], key + 1, device)
    cross_merge(3)
    cross_merge(4)
    cross_merge(5)
    for key, rows, value, device, side in ((2, upper, high, right, 0), (4, lower, low, left, 1)):
        arrive(land_sum.at[rows], key)
        arrive(land_stat.at[rows], key + 1)
        merged, stats = merge_blocks(
            (run_sum[value, rows], run_stat[value, rows]), (land_sum[rows], land_stat[rows]), 4
        )
        run_sum[value, rows] = merged.astype(BF)
        run_stat[value, rows] = stats
        send(run_sum.at[value], last_sum.at[side], key + 4, device)
        send(run_stat.at[value], last_stat.at[side], key + 5, device)
    sums, stats = merge_blocks((run_sum[x], run_stat[x]), (leaf_sum[...], leaf_stat[...]), 4)
    for side, key in ((0, 6), (1, 8)):
        arrive(last_sum.at[side], key)
        arrive(last_stat.at[side], key + 1)
        sums, stats = merge_blocks((sums, stats), (last_sum[side], last_stat[side]), 4)
    first = part == 0
    give_sum[...] = jnp.where(first, sums[:, 256:], sums[:, :256]).astype(BF)
    leaf_stat[...] = stats
    send(give_sum, side_sum, 10, device_of(beside))
    send(leaf_stat, side_stat, 11, device_of(beside))
    kept = jnp.where(first, sums[:, :256], sums[:, 256:])
    fresh_key = fresh_ref[0].astype(F32)
    fresh_value = fresh_ref[1].astype(F32)
    own_scores = [
        jnp.sum(own_query_ref[:, h * 128 : (h + 1) * 128].astype(F32) * fresh_key, axis=1, keepdims=True)
        * SCALE2
        for h in range(2)
    ]
    arrive(side_sum, 10)
    arrive(side_stat, 11)
    theirs = side_stat[...]
    pieces = []
    for h in range(2):
        span = slice(h * 128, (h + 1) * 128)

        def column(from_stats, offset):
            return jnp.where(
                first,
                from_stats[:, offset + h : offset + h + 1],
                from_stats[:, offset + 2 + h : offset + 3 + h],
            )

        top_one, top_two = column(stats, 0), column(theirs, 0)
        top = jnp.maximum(jnp.maximum(top_one, top_two), own_scores[h])
        factor_one, factor_two = jnp.exp2(top_one - top), jnp.exp2(top_two - top)
        factor_own = jnp.exp2(own_scores[h] - top)
        weighted = (
            kept[:, span] * factor_one
            + side_sum[:, span].astype(F32) * factor_two
            + factor_own * fresh_value
        )
        total = column(stats, 4) * factor_one + column(theirs, 4) * factor_two + factor_own
        pieces.append((weighted / total).astype(BF))
    attended = jnp.concatenate(pieces, axis=1)
    for i in range(16):
        product = jnp.dot(
            attended, weight_ref[:, i * 256 : (i + 1) * 256], preferred_element_type=F32
        ).astype(BF)
        for half in range(2):
            proj_ref[i // 4, i % 4, half] = product[:, half * 128 : (half + 1) * 128]

    def finish(row, rows, half, total):
        cols = pl.ds(half * 128, 128)
        total += residual_ref[pl.ds(row, rows), cols].astype(F32)
        hidden_ref[pl.ds(row, rows), cols] = total
        narrow_ref[half, pl.ds(row, rows), :] = total.astype(BF)

    ring_reduce(
        at, proj_ref, ("y", "z"), (("y", "z"), ("z", "y")), ((0, 64), (64, 64)),
        (half1, half2), (full1, full2), send, arrive, 12, finish,
    )
    for copy in started:
        copy.wait_send()


def attend(sums, stats, queries, own_queries, leaf, leaf_len, fresh, out_weight, residual):
    return pl.pallas_call(
        attend_kernel,
        out_shape=(
            jax.ShapeDtypeStruct((ROWS, 256), F32),
            jax.ShapeDtypeStruct((2, ROWS, 128), BF),
        ),
        in_specs=[pl.BlockSpec(memory_space=pltpu.VMEM)] * 9,
        out_specs=(pl.BlockSpec(memory_space=pltpu.VMEM),) * 2,
        scratch_shapes=[
            pltpu.VMEM((4, ROWS, 512), BF),
            pltpu.VMEM((4, ROWS, 128), F32),
            pltpu.VMEM((4, ROWS, 512), BF),
            pltpu.VMEM((4, ROWS, 128), F32),
            pltpu.VMEM((ROWS, 512), BF),
            pltpu.VMEM((ROWS, 128), F32),
            pltpu.VMEM((2, ROWS, 512), BF),
            pltpu.VMEM((2, ROWS, 128), F32),
            pltpu.VMEM((ROWS, 512), F32),
            pltpu.VMEM((ROWS, 128), F32),
            pltpu.VMEM((ROWS, 256), BF),
            pltpu.VMEM((ROWS, 128), F32),
            pltpu.VMEM((ROWS, 256), BF),
            pltpu.VMEM((4, 4, 2, ROWS, 128), BF),
            pltpu.VMEM((2, 4, ROWS, 128), BF),
            pltpu.VMEM((2, 4, 2, ROWS, 128), BF),
            pltpu.VMEM((2, ROWS, 128), BF),
            pltpu.VMEM((2, 2, ROWS, 128), BF),
            pltpu.SemaphoreType.DMA((28,)),
            pltpu.SemaphoreType.DMA((28,)),
        ],
        compiler_params=pltpu.CompilerParams(
            collective_id=4, has_side_effects=True, vmem_limit_bytes=48 * 2**20
        ),
        name="attend",
    )(sums, stats, queries, own_queries, leaf, leaf_len, fresh, out_weight, residual)


def ring_reduce(at, sum_ref, dims, orders, part_rows, halves, fulls, send, arrive, base, finish):
    phases = len(dims)
    both = slice(None)

    def view(part, phase, value, half):
        index = dict(at)
        for axis in orders[part][phase + 1 :]:
            index[axis] = slice(None)
        index[orders[part][phase]] = value
        row, rows = part_rows[part]
        return tuple(index[axis] for axis in dims) + (half, pl.ds(row, rows), slice(None))

    def landing(part, phase, direction, half):
        row, rows = part_rows[part]
        free = (slice(None),) * (phases - 1 - phase)
        if half is None:
            return (halves[phase], (direction,) + free + (pl.ds(row, rows), slice(None)))
        return (fulls[phase], (direction,) + free + (half, pl.ds(row, rows), slice(None)))

    def accumulate(target, others):
        total = sum_ref[target].astype(F32)
        for ref, index in others:
            total += ref[index].astype(F32)
        return total

    parts = range(len(orders))
    for phase in range(phases):
        keys = [base + (part * phases + phase) * 4 for part in parts]
        for part in parts:
            axis = orders[part][phase]
            for direction, by in ((0, 1), (1, 3)):
                ref, index = landing(part, phase, direction, None)
                send(
                    sum_ref.at[view(part, phase, (at[axis] + 2) % 4, direction)],
                    ref.at[index],
                    keys[part] + direction,
                    step_along(at, axis, by),
                )
        for part in parts:
            axis = orders[part][phase]
            for direction, by in ((0, 1), (1, 3)):
                ref, index = landing(part, phase, direction, None)
                arrive(ref.at[index], keys[part] + direction)
                target = view(part, phase, (at[axis] + by) % 4, direction)
                sum_ref[target] = accumulate(target, [(ref, index)]).astype(BF)
            for direction, by in ((0, 1), (1, 3)):
                ref, index = landing(part, phase, direction, both)
                send(
                    sum_ref.at[view(part, phase, (at[axis] + by) % 4, both)],
                    ref.at[index],
                    keys[part] + 2 + direction,
                    step_along(at, axis, by),
                )
        for part in parts:
            axis = orders[part][phase]
            for direction in range(2):
                ref, index = landing(part, phase, direction, both)
                arrive(ref.at[index], keys[part] + 2 + direction)
            for half in range(2):
                target = view(part, phase, at[axis], half)
                total = accumulate(
                    target, [landing(part, phase, direction, half) for direction in range(2)]
                )
                if phase < phases - 1:
                    sum_ref[target] = total.astype(BF)
                else:
                    row, rows = part_rows[part]
                    finish(row, rows, half, total)


def owned_nodes(owner, dp_index, count):
    node = jnp.arange(owner.shape[0])
    owned = owner == dp_index
    rank = jnp.sum((owned[None, :] & (node[None, :] < node[:, None])).astype(jnp.int32), axis=1)
    chosen = owned[None, :] & (rank[None, :] == jnp.arange(count)[:, None])
    return jnp.sum(jnp.where(chosen, node[None, :], 0), axis=1), jnp.where(owned, rank, -1)


def slot_codes(slot_request, request_branch, branch_parent, root_place, branch_place):
    slots = slot_request.shape[0]
    slot = jnp.arange(slots)
    slot_branch = jnp.sum(
        jnp.where(slot_request[:, None] == slot[None, :], request_branch[None, :], 0), axis=1
    )
    rank = jnp.sum(
        ((slot_branch[:, None] == slot_branch[None, :]) & (slot[None, :] < slot[:, None])).astype(jnp.int32),
        axis=1,
    )
    branch = jnp.arange(branch_parent.shape[0])
    kid = jnp.sum(
        ((branch_parent[:, None] == branch_parent[None, :]) & (branch[None, :] < branch[:, None])).astype(
            jnp.int32
        ),
        axis=1,
    )
    parent_place = jnp.sum(
        jnp.where(branch_parent[:, None] == jnp.arange(root_place.shape[0])[None, :], root_place[None, :], 0),
        axis=1,
    )
    root_base = jnp.where(parent_place >= 0, parent_place * ROWS + kid * BR_CAP, -4096)
    branch_base = jnp.where(branch_place >= 0, branch_place * BR_CAP, -4096)
    mine = slot_branch[None, :, None] == branch[None, None, :]
    bases = jnp.sum(jnp.where(mine, jnp.stack([root_base, branch_base])[:, None, :], 0), axis=2)
    return jnp.maximum(bases + rank[None, :], -1)


def expert_phase(hidden, narrow, all_routes, norm_gain, router, expert_in, expert_out):
    dp = lax.axis_index("dp")
    names = jnp.arange(EXPERTS)
    hit = jnp.any(all_routes[:, :, :, None] == names, axis=2)
    before = jnp.tril(jnp.ones((ROWS, ROWS), F32), -1)
    rank = jnp.einsum(
        "rq,bqe->ebr", before.astype(BF), hit.astype(BF), preferred_element_type=F32
    ).astype(jnp.int32)
    rank = jnp.where(hit.transpose(2, 0, 1), rank, -1)
    mine = lax.dynamic_index_in_dim(rank, dp, 0, False)
    other = jnp.sum(all_routes, axis=2) - dp
    packed = mine[:, None, :] == jnp.arange(E_CAP)[None, :, None]
    other = jnp.sum(jnp.where(packed, other[:, None, :], 0), axis=2).reshape(-1, 1)
    core = dp % 2
    ours = lax.dynamic_index_in_dim(rank.reshape(EXPERTS, 4, 2, ROWS), core, 2, False)
    pair = jnp.stack(
        [
            lax.dynamic_index_in_dim(ours, dp, 0, False),
            lax.dynamic_index_in_dim(ours, dp + 1 - 2 * core, 0, False),
        ],
        axis=1,
    )
    buf = gather_rows(narrow)
    partial = run_experts(
        buf,
        mine,
        other,
        dp.reshape(1, 1).astype(jnp.int32),
        norm_gain[None, :],
        router,
        expert_in[0],
        expert_out[0],
    )
    return return_rows(partial.reshape(4, 2, 16, 2, E_CAP, 128), pair[..., None], hidden)


def shards(
    queries,
    new_kv,
    residual,
    out_weight,
    norm_gain,
    router,
    expert_in,
    expert_out,
    node_cache,
    leaf_cache,
    slot_request,
    request_branch,
    branch_parent,
    root_owner,
    branch_owner,
    root_pages,
    branch_pages,
    root_len,
    branch_len,
    leaf_len,
    routes,
):
    dp = lax.axis_index("dp")
    mp = lax.axis_index("mp")
    all_routes = lax.all_gather(routes, "dp", axis=0)
    local_roots, root_place = owned_nodes(root_owner, dp, ROOT_DEV)
    local_branches, branch_place = owned_nodes(branch_owner, dp, BR_DEV)
    codes = slot_codes(slot_request, request_branch, branch_parent, root_place, branch_place)
    all_queries = gather_queries(queries).reshape(8 * ROWS, 512)
    sums, stats = node_partials(
        local_roots,
        local_branches,
        (root_pages, branch_pages, root_len, branch_len),
        (mp % 2).reshape(1).astype(jnp.int32),
        all_queries,
        node_cache[:, :, 0],
        codes,
    )
    hidden, narrow = attend(
        sums.reshape(4, 2, ROWS, 512),
        stats.reshape(4, 2, ROWS, 128),
        lax.dynamic_slice_in_dim(queries, (mp // 2) * 512, 512, 1).astype(F32),
        lax.dynamic_slice_in_dim(queries, mp * 256, 256, 1),
        leaf_cache[:, :, 0],
        leaf_len[:, None],
        lax.dynamic_slice_in_dim(new_kv, (mp // 2) * 128, 128, 2),
        out_weight,
        residual,
    )
    return expert_phase(hidden, narrow, all_routes, norm_gain, router, expert_in, expert_out)


def solution(mesh):
    placed = (
        P("dp", None),
        P(None, "dp", None),
        P("dp", "mp"),
        P("mp", None),
        P(),
        P(),
        P("dp", None, "mp", None),
        P("dp", "mp", None),
        P(None, "dp", "mp", None, None),
        P(None, "dp", "mp", None, None),
        P(),
        P(),
        P(),
        P(),
        P(),
        P(),
        P(),
        P(),
        P(),
        P("dp"),
        P("dp", None),
    )
    return jax.shard_map(
        shards, mesh=mesh, in_specs=placed, out_specs=P("dp", "mp"), check_vma=False
    )
```

time: 539 us -> 228 us (0.42)
  waiting for transfers between devices: 306 us -> 0 us
  Pallas kernels: 0 us -> 191 us
  local copies, waits for them, and re-layouts: 90.4 us -> 17.2 us
  blocking collectives: 54.4 us -> 9.75 us
  other arithmetic: 37 us -> 8.19 us
  matrix products: 26.4 us -> 0.2 us
  between operations: 14.9 us -> 0.3 us
  starting transfers between devices: 8.45 us -> 0 us
    pallas_call x0 -> x6, Pallas kernels: none -> 191 us  [the longest x1 51.3 us: attend(): pl.pallas_call(attend_kernel, out_shape=(jax.ShapeDtypeStruct((ROWS, 256)...]
    unnamed x13 -> x0, waiting for transfers between devices: 142 us -> none
    psum x1 -> x0, waiting for transfers between devices: 84.6 us -> none  [shards(): hidden = lax.psum(projected.astype(jnp.bfloat16), 'mp').astype(jnp.float32)]
    reduce_scatter x1 -> x0, waiting for transfers between devices: 72.4 us -> none  [shards(): lax.psum_scatter(expert_partial.astype(jnp.bfloat16), 'mp', scatter_dimen...]
    all_to_all x1 -> x0, blocking collectives: 54.4 us -> none  [shards(): lax.all_to_all(outgoing, 'dp', split_axis=0, concat_axis=0, tiled=True)]
    scatter x7 -> x0, local copies, waits for them, and re-layouts: 41.8 us -> none  [the longest x2 32.3 us: spread_rows(): sum_rows = jnp.zeros((requests, groups, head_width), jnp.float32).at[flat...]
    gather x20 -> x0, local copies, waits for them, and re-layouts: 28.9 us -> none  [the longest x2 8.66 us: shards(): jnp.take(branch_order, spots)]
    dot_general x11 -> x1, matrix products: 26.4 us -> 0.2 us  [expert_phase(): jnp.einsum('rq,bqe->ebr', before.astype(BF), hit.astype(BF), preferred_el...]
  transfers between devices with their start and end apart: 12 -> 0, of which waited for: 8 -> 0; matrix products, arithmetic and copies ran while one was open for 21% -> 0% of each run, Pallas kernels for 0% -> 0%
where the time goes in v1:
time: 228 us; the launch traced here: 227 us
  Pallas kernels  191 us (84%)
  local copies, waits for them, and re-layouts  17.2 us (8%)
  blocking collectives  9.75 us (4%)
  other arithmetic  8.19 us (4%)
    pallas_call x1, Pallas kernels, attend(): pl.pallas_call(attend_kernel, out_shape=(jax.ShapeDtypeStruct((ROWS, 256)...  51.3 us
    pallas_call x1, Pallas kernels, return_rows(): pl.pallas_call(return_kernel, out_shape=jax.ShapeDtypeStruct((ROWS, 256),...  50.4 us
    pallas_call x1, Pallas kernels, gather_rows(): pl.pallas_call(gather_kernel, out_shape=jax.ShapeDtypeStruct((4, 2, 4, 4,...  36.8 us
    pallas_call x1, Pallas kernels, run_experts(): pl.pallas_call(expert_kernel, grid=(FF_STEPS,), out_shape=jax.ShapeDtypeS...  22.6 us
    pallas_call x1, Pallas kernels, node_partials(): pl.pallas_call(node_kernel, out_shape=(jax.ShapeDtypeStruct((8, ROWS, 512...  17.8 us
    unnamed x39, local copies, waits for them, and re-layouts  14.8 us
    pallas_call x1, Pallas kernels, gather_queries(): pl.pallas_call(query_kernel, out_shape=jax.ShapeDtypeStruct((4, 2, ROWS,...  12.6 us
    all_gather x1, blocking collectives, shards(): all_routes = lax.all_gather(routes, 'dp', axis=0)  9.75 us

profile of v1, /device:TPU:0, one launch (start us, length us, event | category | flops | bytes accessed | tf_op | source)
XLA Modules:
  0.0 227.1 jit_solution(6859400830249665943)
XLA Ops:
  0.0 0.7 broadcast_compare_fusion.1
  0.8 0.7 broadcast_select_fusion
  1.5 0.7 select_reduce_fusion.3
  2.2 0.7 broadcast_compare_fusion
  3.0 0.9 convert_reduce_fusion.1
  3.9 0.7 fusion.14
  4.6 1.5 select_reduce_fusion
  6.3 0.5 convert_reduce_fusion
  7.3 12.6 %gather_queries.1 = bf16[4,2,128,512]{3,2,1,0:T(8,128)(2,1)} custom-call(bf16[128,4096]{1,0:T(8,128)(2,1)} %queries_ref.1), custom_call_target="tpu_custom_call" | custom-call | tf_op jit(solution)/shard_map/gather_queries/pallas_call | solution.py:438
  19.9 0.8 copy.37.branch_pages_ref
  20.7 1.2 copy-done.2
  21.9 1.9 copy-done.3
  23.8 0.7 copy-done.11
  24.5 0.7 copy-done.12
  25.1 0.7 copy-done.13
  25.8 17.8 %node_partials.1 = (bf16[8,128,512]{2,1,0:T(8,128)(2,1)S(1)}, f32[8,128,128]{2,1,0:T(8,128)S(1)}) custom-call(s32[2]{0:T(128)S(1)} %fusion.13.local_ref, s32[8]{0:T(128)S(1)} %select_reduce_fusion.4.branch_id_ref, s32[16,32]{1,0:T(8,128)S(1)} %copy-done.11, s32[64,4]{1,0:T(8,128)S(1)} %copy.37.branch_pages_ref, s32[16]{0:T(128)S(1)} %copy-done.12, ...), custom_call_target="tpu_custom_call" | custom-call | tf_op jit(solution)/shard_map/node_partials/pallas_call | solution.py:592
  43.6 1.0 copy-done.5
  44.6 0.8 copy-done.7
  45.4 0.9 dynamic-slice_convert_fusion.query_ref
  46.4 0.8 constant_dynamic-slice_fusion.2.own_query_ref
  47.4 1.2 copy-done.6
  48.6 1.0 copy-done.8
  49.7 51.3 %attend.1 = (f32[128,256]{1,0:T(8,128)S(1)}, bf16[2,128,128]{2,1,0:T(8,128)(2,1)S(1)}) custom-call(bf16[4,2,128,512]{3,2,1,0:T(8,128)(2,1)S(1)} %bitcast.44, f32[4,2,128,128]{3,2,1,0:T(8,128)S(1)} %bitcast.45, f32[128,512]{1,0:T(8,128)S(1)} %dynamic-slice_convert_fusion.query_ref, bf16[128,256]{1,0:T(8,128)(2,1)S(1)} %constant_dynamic-slice_fusion.2.own_query_ref, ...), custom_call_target="tpu_custom_call" | custom-call | tf_op jit(solution)/shard_map/attend/pallas_call | solution.py:770
  101.0 0.6 copy-done.10
  101.6 36.8 %gather_rows.1.buf_ref = bf16[4,2,4,4,2,128,128]{6,5,4,3,2,1,0:T(8,128)(2,1)} custom-call(bf16[2,128,128]{2,1,0:T(8,128)(2,1)} %copy-done.10), custom_call_target="tpu_custom_call" | custom-call | tf_op jit(solution)/shard_map/gather_rows/pallas_call | solution.py:158
  138.5 9.8 %all-gather = s32[1024,2]{0,1:T(2,128)S(1)} all-gather(s32[128,2]{0,1:T(2,128)S(1)} %copy-done.16), channel_id=2, replica_groups=mesh['dp'=8,'mp'=16] {'dp'}, dimensions={0}, use_global_device_ids=true | all-gather | bytes 9216 | tf_op jit(solution)/shard_map/all_gather | solution.py:974
  148.8 0.9 reshape.120.other_ref
  149.7 1.4 copy.41.router_ref
  151.1 22.6 %run_experts.1 = bf16[8,16,2,64,128]{4,3,2,1,0:T(8,128)(2,1)} custom-call(bf16[4,2,4,4,2,128,128]{6,5,4,3,2,1,0:T(8,128)(2,1)} %gather_rows.1.buf_ref, s32[8,128]{1,0:T(8,128)} %bitcast.51, s32[512,1]{1,0:T(8,128)} %reshape.120.other_ref, s32[1,1]{1,0:T(1,128)} %bitcast.17.mine_ref, f32[1,4096]{1,0:T(1,128)} %bitcast.52, bf16[4096,8]{1,0:T(8,128)(2,1)} %copy.41.router_ref, ...), custom_call_target="tpu_custom_call" | custom-call | flops 6442450944 | bytes 26214400 | tf_op jit(solution)/shard_map/run_experts/pallas_call | solution.py:258
  174.0 2.2 copy-done.1
  176.1 50.4 %return_rows.1 = bf16[128,256]{1,0:T(8,128)(2,1)S(1)} custom-call(bf16[4,2,16,2,64,128]{5,4,3,2,1,0:T(8,128)(2,1)S(1)} %bitcast.40, s32[4,2,128,1]{3,2,1,0:T(8,128)S(1)} %copy.42.rank_ref, f32[128,256]{1,0:T(8,128)S(1)} %get-tuple-element.12.kept_ref), custom_call_target="tpu_custom_call" | custom-call | tf_op jit(solution)/shard_map/return_rows/pallas_call | solution.py:355
  226.5 0.6 copy.44
  (47 shorter events, 1.8 us)
Async XLA Ops:
  0.0 46.4 %copy-start = (bf16[2,128,1024]{2,1,0:T(8,128)(2,1)S(1)}, bf16[2,128,1024]{2,1,0:T(8,128)(2,1)}, u32[]{:S(2)}) copy-start(bf16[2,128,1024]{2,1,0:T(8,128)(2,1)} %param.22) | copy-start | bytes 1572868
  0.7 46.5 %copy-start.17 = (s32[128]{0:T(128)S(1)}, s32[128]{0:T(128)}, u32[]{:S(2)}) copy-start(s32[128]{0:T(128)} %param.40) | copy-start | bytes 1540
  6.1 41.3 %copy-start.4 = (bf16[256,4096]{1,0:T(8,128)(2,1)S(1)}, bf16[256,4096]{1,0:T(8,128)(2,1)}, u32[]{:S(2)}) copy-start(bf16[256,4096]{1,0:T(8,128)(2,1)} %weight_ref.1) | copy-start | bytes 6291460
  6.1 41.3 %copy-start.9 = (bf16[128,256]{1,0:T(8,128)(2,1)S(1)}, bf16[128,256]{1,0:T(8,128)(2,1)}, u32[]{:S(2)}) copy-start(bf16[128,256]{1,0:T(8,128)(2,1)} %residual_ref.1) | copy-start | bytes 196612
  20.7 1.2 copy-start.2
  21.9 1.9 copy-start.3
  23.8 0.7 copy-start.11
  24.5 0.7 copy-start.12
  25.1 0.7 copy-start.13
  43.6 1.0 copy-start.5
  44.6 0.8 copy-start.7
  47.4 1.2 copy-start.6
  48.6 1.0 copy-start.8
  101.0 0.6 copy-start.10
  101.6 36.8 %copy-start.16 = (s32[128,2]{0,1:T(2,128)S(1)}, s32[128,2]{0,1:T(2,128)}, u32[]{:S(2)}) copy-start(s32[128,2]{0,1:T(2,128)} %param.41) | copy-start | bytes 3076
  101.6 48.0 %copy-start.14 = (bf16[4096,8]{0,1:T(8,128)(2,1)S(1)}, bf16[4096,8]{0,1:T(8,128)(2,1)}, u32[]{:S(2)}) copy-start(bf16[4096,8]{0,1:T(8,128)(2,1)} %param.26) | copy-start | bytes 196612
  148.5 2.6 %copy-start.15 = (s32[1,8,128]{2,0,1:T(1,128)}, s32[1,8,128]{2,0,1:T(1,128)S(1)}, u32[]{:S(2)}) copy-start(s32[1,8,128]{2,0,1:T(1,128)S(1)} %constant_dynamic-slice_fusion) | copy-start | bytes 12292
  173.9 2.2 copy-start.1

commit v2 on v1

--- a/solution.py
+++ b/solution.py
@@ -21,6 +21,7 @@
 ROWS = 128
 PART_ROWS = ((0, 48), (48, 48), (96, 32))
 AXES = ("x", "y", "z")
+ORDERS = tuple(AXES[part:] + AXES[:part] for part in range(3))
 
 
 def place():
@@ -57,370 +58,379 @@
 
 
 def all_peers(at):
-    return [step_along(at, axis, by) for axis in AXES for by in (1, 3)] + [
+    return [step_along(at, axis, by) for axis in AXES for by in (1, 2, 3)] + [
         device_of(at, c=1 - at["c"])
     ]
 
 
-def gather_kernel(own_ref, buf_ref, local_sem, send_sem, recv_sem):
-    at = place()
-    sems = (send_sem, recv_sem)
-    greet(all_peers(at))
-    sibling = device_of(at, c=1 - at["c"])
-
-    def slab(part, order, phase, value, half, core):
+class Link:
+    def __init__(self, at, sems):
+        self.sems = sems
+        self.sibling = device_of(at, c=1 - at["c"])
+        self.started = []
+
+    def send(self, src, dst, key, device):
+        copy = remote(src, dst, self.sems, key, device)
+        copy.start()
+        self.started.append(copy)
+
+    def arrive(self, ref, key):
+        remote(ref, ref, self.sems, key, self.sibling).wait_recv()
+
+    def finish(self):
+        for copy in self.started:
+            copy.wait_send()
+
+
+def gather_all(at, link, own_ref, buf_ref, local_sem, base):
+    both = slice(None)
+    core = at["c"]
+
+    def slab(part, phase, value, half, plane):
         index = {"x": at["x"], "y": at["y"], "z": at["z"]}
-        for axis in order[:phase]:
+        for axis in ORDERS[part][:phase]:
             index[axis] = slice(None)
-        index[order[phase]] = value
+        index[ORDERS[part][phase]] = value
         row, rows = PART_ROWS[part]
-        return buf_ref.at[
-            index["x"],
-            core,
-            index["y"],
-            index["z"],
-            half,
-            pl.ds(row, rows),
-            :,
-        ]
-
-    both = slice(None)
-    mine = buf_ref.at[at["x"], at["c"], at["y"], at["z"]]
-    local = pltpu.make_async_copy(own_ref, mine, local_sem)
+        return buf_ref.at[index["x"], plane, index["y"], index["z"], half, pl.ds(row, rows), :]
+
+    local = pltpu.make_async_copy(own_ref, buf_ref.at[at["x"], core, at["y"], at["z"]], local_sem)
     local.start()
-    orders = [AXES[part:] + AXES[:part] for part in range(3)]
-    started = []
-
-    def send(src, dst, key, device):
-        copy = remote(src, dst, sems, key, device)
-        copy.start()
-        started.append(copy)
-
-    def arrive(ref, key):
-        remote(ref, ref, sems, key, sibling).wait_recv()
-
-    core = at["c"]
-    for phase in range(3):
+    for phase in range(2):
         for part in range(3):
-            order = orders[part]
-            axis = order[phase]
-            v = at[axis]
-            key = part * 16 + phase * 4
-            ref = slab(part, order, phase, v, both, core)
+            axis = ORDERS[part][phase]
+            ref = slab(part, phase, at[axis], both, core)
+            src = ref
             if phase == 0:
                 row, rows = PART_ROWS[part]
                 src = own_ref.at[:, pl.ds(row, rows), :]
-            else:
-                src = ref
-            send(src, ref, key, step_along(at, axis, 1))
-            send(src, ref, key + 1, step_along(at, axis, 3))
-            if phase == 2:
-                send(src, ref, part * 16 + 12, sibling)
-        for part in range(3):
-            order = orders[part]
-            axis = order[phase]
-            v = at[axis]
-            key = part * 16 + phase * 4
-            low = slab(part, order, phase, (v + 3) % 4, both, core)
-            arrive(low, key)
-            first = slab(part, order, phase, (v + 3) % 4, 0, core)
-            send(first, first, key + 2, step_along(at, axis, 1))
-            high = slab(part, order, phase, (v + 1) % 4, both, core)
-            arrive(high, key + 1)
-            second = slab(part, order, phase, (v + 1) % 4, 1, core)
-            send(second, second, key + 3, step_along(at, axis, 3))
-            if phase == 2:
-                send(low, low, part * 16 + 13, sibling)
-                send(high, high, part * 16 + 14, sibling)
+            for by in (2, 1, 3):
+                link.send(src, ref, base + (part * 2 + phase) * 3 + by - 1, step_along(at, axis, by))
         if phase == 0:
             local.wait()
         for part in range(3):
-            order = orders[part]
-            axis = order[phase]
-            v = at[axis]
-            key = part * 16 + phase * 4
-            far = (v + 2) % 4
-            arrive(slab(part, order, phase, far, 0, core), key + 2)
-            arrive(slab(part, order, phase, far, 1, core), key + 3)
-            if phase == 2:
-                ref = slab(part, order, phase, far, both, core)
-                send(ref, ref, part * 16 + 15, sibling)
+            axis = ORDERS[part][phase]
+            for by in (1, 3, 2):
+                ref = slab(part, phase, (at[axis] - by) % 4, both, core)
+                link.arrive(ref, base + (part * 2 + phase) * 3 + by - 1)
+    base += 18
     for part in range(3):
-        order = orders[part]
-        v = at[order[2]]
-        for key, by in ((12, 0), (13, 3), (14, 1), (15, 2)):
-            arrive(slab(part, order, 2, (v + by) % 4, both, 1 - core), part * 16 + key)
-    for copy in started:
-        copy.wait_send()
-
-
-def gather_rows(own):
-    return pl.pallas_call(
-        gather_kernel,
-        out_shape=jax.ShapeDtypeStruct((4, 2, 4, 4, 2, ROWS, 128), BF),
-        in_specs=[pl.BlockSpec(memory_space=pl.ANY)],
-        out_specs=pl.BlockSpec(memory_space=pl.ANY),
-        scratch_shapes=[
-            pltpu.SemaphoreType.DMA,
-            pltpu.SemaphoreType.DMA((48,)),
-            pltpu.SemaphoreType.DMA((48,)),
-        ],
-        compiler_params=pltpu.CompilerParams(collective_id=1, has_side_effects=True),
-        name="gather_rows",
-    )(own)
-
-
-FF_STEPS = 2
+        axis = ORDERS[part][2]
+        key = base + part * 8
+        ref = slab(part, 2, at[axis], both, core)
+        link.send(ref, ref, key, step_along(at, axis, 1))
+        link.send(ref, ref, key + 1, step_along(at, axis, 3))
+        link.send(ref, ref, key + 4, link.sibling)
+    for part in range(3):
+        axis = ORDERS[part][2]
+        key = base + part * 8
+        for side, by in ((0, 3), (1, 1)):
+            value = (at[axis] + by) % 4
+            ref = slab(part, 2, value, both, core)
+            link.arrive(ref, key + side)
+            half = slab(part, 2, value, side, core)
+            link.send(half, half, key + 2 + side, step_along(at, axis, 1 + 2 * side))
+            link.send(ref, ref, key + 5 + side, link.sibling)
+    for part in range(3):
+        axis = ORDERS[part][2]
+        key = base + part * 8
+        far = (at[axis] + 2) % 4
+        for side in range(2):
+            link.arrive(slab(part, 2, far, side, core), key + 2 + side)
+        ref = slab(part, 2, far, both, core)
+        link.send(ref, ref, key + 7, link.sibling)
+
+    def others():
+        for part in range(3):
+            v = at[ORDERS[part][2]]
+            for i, by in enumerate((0, 3, 1, 2)):
+                link.arrive(slab(part, 2, (v + by) % 4, both, 1 - core), base + part * 8 + 4 + i)
+
+    return others
+
+
+GATHER_KEYS = 18 + 24
+
+
+def ring_reduce(at, link, sum_ref, dims, orders, part_rows, relay, lands, base, finish):
+    phases = len(dims)
+    both = slice(None)
+    parts = range(len(orders))
+
+    def view(part, phase, value, half):
+        index = dict(at)
+        for axis in orders[part][phase + 1 :]:
+            index[axis] = slice(None)
+        index[orders[part][phase]] = value
+        row, rows = part_rows[part]
+        return tuple(index[axis] for axis in dims) + (half, pl.ds(row, rows), slice(None))
+
+    def spot(part, phase, slot, *half):
+        row, rows = part_rows[part]
+        return (slot,) + (slice(None),) * (phases - 1 - phase) + half + (pl.ds(row, rows), slice(None))
+
+    def accumulate(target, others):
+        total = sum_ref[target].astype(F32)
+        for ref, index in others:
+            total += ref[index].astype(F32)
+        return total
+
+    for phase in range(phases):
+        keys = [base + (part * phases + phase) * 4 for part in parts]
+        if phase < relay:
+            halves, fulls = lands[phase]
+            for part in parts:
+                axis = orders[part][phase]
+                for side, by in ((0, 1), (1, 3)):
+                    link.send(
+                        sum_ref.at[view(part, phase, (at[axis] + 2) % 4, side)],
+                        halves.at[spot(part, phase, side)],
+                        keys[part] + side,
+                        step_along(at, axis, by),
+                    )
+            for part in parts:
+                axis = orders[part][phase]
+                for side, by in ((0, 1), (1, 3)):
+                    index = spot(part, phase, side)
+                    link.arrive(halves.at[index], keys[part] + side)
+                    target = view(part, phase, (at[axis] + by) % 4, side)
+                    sum_ref[target] = accumulate(target, [(halves, index)]).astype(BF)
+                    link.send(
+                        sum_ref.at[view(part, phase, (at[axis] + by) % 4, both)],
+                        fulls.at[spot(part, phase, side, both)],
+                        keys[part] + 2 + side,
+                        step_along(at, axis, by),
+                    )
+            slots, first = 2, 2
+        else:
+            fulls = lands[phase]
+            for part in parts:
+                axis = orders[part][phase]
+                for by in (2, 1, 3):
+                    link.send(
+                        sum_ref.at[view(part, phase, (at[axis] + by) % 4, both)],
+                        fulls.at[spot(part, phase, by - 1, both)],
+                        keys[part] + by - 1,
+                        step_along(at, axis, by),
+                    )
+            slots, first = 3, 0
+        for part in parts:
+            axis = orders[part][phase]
+            for slot in range(slots):
+                link.arrive(fulls.at[spot(part, phase, slot, both)], keys[part] + first + slot)
+            for half in range(2):
+                target = view(part, phase, at[axis], half)
+                total = accumulate(target, [(fulls, spot(part, phase, slot, half)) for slot in range(slots)])
+                if phase < phases - 1:
+                    sum_ref[target] = total.astype(BF)
+                else:
+                    finish(*part_rows[part], half, total)
 
 
 def expert_kernel(
-    buf_ref, rank_ref, other_ref, mine_ref, gain_ref, router_ref, up_ref, down_ref,
-    out_ref, rows_ref, gate_ref, total_ref, block_ref, block_sem,
+    own_ref, kept_ref, pick_ref, other_ref, spread_ref, gain_ref, router_ref, up_hbm, down_hbm,
+    out_ref,
+    buf_ref, rows_ref, gate_ref, up_ref, down_ref, act_ref, give_ref, theirs_ref, sum_ref,
+    half0, full0, full1, full2,
+    local_sem, up_sem, down_sem, send_sem, recv_sem,
 ):
-    step = pl.program_id(0)
-    cap = E_CAP
-
-    def fetch(block, slot):
-        return pltpu.make_async_copy(
-            buf_ref.at[block // 2, block % 2], block_ref.at[slot], block_sem.at[slot]
+    at = place()
+    loads = [pltpu.make_async_copy(up_hbm, up_ref, up_sem), pltpu.make_async_copy(down_hbm, down_ref, down_sem)]
+    for load in loads:
+        load.start()
+    greet(all_peers(at))
+    link = Link(at, (send_sem, recv_sem))
+    core = at["c"]
+    mine = lax.axis_index("dp")
+    others = gather_all(at, link, own_ref, buf_ref, local_sem, 0)
+
+    def compact(plane):
+        base = pl.multiple_of(plane * 256, 256)
+        wanted = lax.broadcasted_iota(jnp.int32, (128, 256), 0)
+        picks = [(wanted == pick_ref[plane, pair]).astype(BF) for pair in range(2)]
+
+        def fill(y, squares):
+            for z in range(4):
+                pieces = []
+                for pair in range(2):
+                    whole = jnp.concatenate(
+                        [
+                            jnp.concatenate([buf_ref[2 * pair + k, plane, y, z, h] for h in range(2)], axis=1)
+                            for k in range(2)
+                        ],
+                        axis=0,
+                    )
+                    pieces.append(jnp.dot(picks[pair], whole, preferred_element_type=F32))
+                piece = jnp.concatenate(pieces, axis=0)
+                cols = pl.ds(pl.multiple_of((y * 4 + z) * 256, 256), 256)
+                rows_ref[pl.ds(base, 256), cols] = piece.astype(BF)
+                piece = piece * piece
+                squares += piece[:, :128] + piece[:, 128:]
+            return squares
+
+        squares = lax.fori_loop(0, 4, fill, jnp.zeros((256, 128), F32))
+        scale = lax.rsqrt(jnp.sum(squares, axis=1, keepdims=True) / 4096.0 + NORM_EPS)
+
+        def norm(y, _):
+            for z in range(4):
+                cols = pl.ds(pl.multiple_of((y * 4 + z) * 256, 256), 256)
+                normed = rows_ref[pl.ds(base, 256), cols].astype(F32) * scale * gain_ref[y * 4 + z]
+                rows_ref[pl.ds(base, 256), cols] = normed.astype(BF)
+            return 0
+
+        lax.fori_loop(0, 4, norm, 0)
+        logits = jnp.dot(rows_ref[pl.ds(base, 256), :], router_ref[...], preferred_element_type=F32)
+        lane = lax.broadcasted_iota(jnp.int32, logits.shape, 1)
+        here = jnp.sum(jnp.where(lane == mine, logits, 0.0), axis=1, keepdims=True)
+        there = jnp.sum(
+            jnp.where(lane == other_ref[pl.ds(base, 256), 0:1], logits, 0.0), axis=1, keepdims=True
         )
-
-    @pl.when(step == 0)
-    def _():
-        fetch(0, 0).start()
-
-        def body(block, _):
-            slot = lax.rem(block, 2)
-
-            @pl.when(block < 7)
-            def _():
-                fetch(block + 1, 1 - slot).start()
-
-            fetch(block, slot).wait()
-            pick = (
-                lax.broadcasted_iota(jnp.int32, (cap, ROWS), 0) == rank_ref[pl.ds(block, 1), :]
-            ).astype(BF)
-            squares = jnp.zeros((cap, 1), F32)
-            pieces = []
-            for y in range(4):
-                for z in range(4):
-                    whole = jnp.concatenate([block_ref[slot, y, z, 0], block_ref[slot, y, z, 1]], axis=1)
-                    piece = jnp.dot(pick, whole, preferred_element_type=F32)
-                    squares += jnp.sum(piece * piece, axis=1, keepdims=True)
-                    pieces.append(piece.astype(BF))
-            scale = lax.rsqrt(squares / (32.0 * 128.0) + NORM_EPS)
-            base = pl.multiple_of(block * cap, cap)
-            for i, piece in enumerate(pieces):
-                cols = pl.ds(i * 256, 256)
-                rows_ref[pl.ds(base, cap), cols] = (
-                    piece.astype(F32) * scale * gain_ref[0:1, cols]
-                ).astype(BF)
-            return 0
-
-        lax.fori_loop(0, 8, body, 0)
-        logits = jnp.dot(rows_ref[...], router_ref[...], preferred_element_type=F32)
-        lane = lax.broadcasted_iota(jnp.int32, logits.shape, 1)
-        here = jnp.sum(jnp.where(lane == mine_ref[0, 0], logits, 0.0), axis=1, keepdims=True)
-        there = jnp.sum(jnp.where(lane == other_ref[...], logits, 0.0), axis=1, keepdims=True)
         most = jnp.maximum(here, there)
         here = jnp.exp(here - most)
         there = jnp.exp(there - most)
-        gate_ref[...] = jnp.broadcast_to(here / (here + there), gate_ref.shape)
-
-    width = up_ref.shape[1]
-    contract = (((1,), (1,)), ((), ()))
-    gate = lax.dot_general(rows_ref[...], up_ref[0], contract, preferred_element_type=F32)
-    up = lax.dot_general(rows_ref[...], up_ref[1], contract, preferred_element_type=F32)
-    hidden = (gate / (1.0 + jnp.exp(-gate)) * up).astype(BF)
-
-    def piece(i, last):
-        partial = jnp.dot(hidden, down_ref[:, i * 256 : (i + 1) * 256], preferred_element_type=F32)
-        if FF_STEPS > 1:
-            if last:
-                partial += total_ref[i]
-            else:
-                total_ref[i] = partial
-        if last:
-            scaled = (partial * gate_ref[:, 0:1]).astype(BF)
-            for half in range(2):
-                out_ref[:, i, half] = scaled[:, half * 128 : (half + 1) * 128].reshape(8, cap, 128)
-
-    for last in (False, True):
-        @pl.when((step == FF_STEPS - 1) == last)
-        def _():
-            for i in range(16):
-                piece(i, last)
-
-
-def run_experts(buf, rank, other, mine, gain, router, expert_in, expert_out):
-    width = expert_in.shape[1] // FF_STEPS
-    deep = expert_in.shape[2]
-    return pl.pallas_call(
-        expert_kernel,
-        grid=(FF_STEPS,),
-        out_shape=jax.ShapeDtypeStruct((8, 16, 2, E_CAP, 128), BF),
-        in_specs=[
-            pl.BlockSpec(memory_space=pl.ANY),
-            pl.BlockSpec((8, ROWS), lambda f: (0, 0)),
-            pl.BlockSpec((8 * E_CAP, 1), lambda f: (0, 0)),
-            pl.BlockSpec(memory_space=pltpu.SMEM),
-            pl.BlockSpec((1, deep), lambda f: (0, 0)),
-            pl.BlockSpec((deep, EXPERTS), lambda f: (0, 0)),
-            pl.BlockSpec((2, width, deep), lambda f: (0, f, 0)),
-            pl.BlockSpec((width, deep), lambda f: (f, 0)),
-        ],
-        out_specs=pl.BlockSpec((8, 16, 2, E_CAP, 128), lambda f: (0, 0, 0, 0, 0)),
-        scratch_shapes=[
-            pltpu.VMEM((8 * E_CAP, deep), BF),
-            pltpu.VMEM((8 * E_CAP, 128), F32),
-            pltpu.VMEM((16, 8 * E_CAP, 256), F32),
-            pltpu.VMEM((2, 4, 4, 2, ROWS, 128), BF),
-            pltpu.SemaphoreType.DMA((2,)),
-        ],
-        compiler_params=pltpu.CompilerParams(
-            vmem_limit_bytes=56 * 2**20, dimension_semantics=("arbitrary",)
-        ),
-        cost_estimate=pl.CostEstimate(
-            flops=6 * 512 * 512 * 4096, bytes_accessed=25 * 2**20, transcendentals=512 * 512
-        ),
-        name="run_experts",
-    )(buf, rank, other, mine, gain, router, expert_in, expert_out)
-
-
-def return_kernel(
-    part_ref, rank_ref, kept_ref, out_ref,
-    theirs_ref, sum_ref, half1, full1, half2, full2, half3, full3, sib_send, sib_recv, send_sem, recv_sem,
-):
-    at = place()
-    greet(all_peers(at))
-    sems = (send_sem, recv_sem)
-    sibling = device_of(at, c=1 - at["c"])
-    core = at["c"]
-    cross = pltpu.make_async_remote_copy(
-        src_ref=part_ref.at[:, 1 - core],
-        dst_ref=theirs_ref,
-        send_sem=sib_send,
-        recv_sem=sib_recv,
-        device_id=sibling,
-        device_id_type=MESH,
-    )
-    cross.start()
-    cross.wait()
-    lane = lax.broadcasted_iota(jnp.int32, (ROWS, E_CAP), 1)
-    for x in range(4):
-        spread = jnp.concatenate(
-            [
-                (rank_ref[x, 0] == lane).astype(BF),
-                (rank_ref[x, 1] == lane).astype(BF),
-            ],
-            axis=1,
+        gate_ref[pl.ds(base, 256), :] = jnp.broadcast_to(here / (here + there), (256, 128))
+
+    compact(core)
+    others()
+    compact(1 - core)
+    for load in loads:
+        load.wait()
+
+    for j in range(2):
+        span = slice(j * 256, (j + 1) * 256)
+        gate, up = [
+            lax.dot_general(rows_ref[...], up_ref[k, span, :], BY_ROW, preferred_element_type=F32)
+            for k in range(2)
+        ]
+        act_ref[:, span] = (gate / (1.0 + jnp.exp(-gate)) * up).astype(BF)
+
+    def project(plane, i):
+        base = pl.multiple_of(plane * 256, 256)
+        cols = pl.ds(pl.multiple_of(i * 256, 256), 256)
+        product = jnp.dot(act_ref[pl.ds(base, 256), :], down_ref[:, cols], preferred_element_type=F32)
+        return (product * gate_ref[pl.ds(base, 256), 0:1]).astype(BF)
+
+    for group in range(4):
+
+        def hand(k, _):
+            i = group * 4 + k
+            give_ref[i] = project(1 - core, i)
+            return 0
+
+        lax.fori_loop(0, 4, hand, 0)
+        link.send(
+            give_ref.at[pl.ds(group * 4, 4)], theirs_ref.at[pl.ds(group * 4, 4)], GATHER_KEYS + group, link.sibling
         )
-
-        def body(i, _):
-            y, z = i // 4, lax.rem(i, 4)
-            for half in range(2):
-                both = jnp.concatenate(
-                    [part_ref[x, core, i, half], theirs_ref[x, i, half]], axis=0
-                )
-                sum_ref[x, y, z, half] = jnp.dot(
-                    spread, both, preferred_element_type=F32
-                ).astype(BF)
+    spreads = []
+    for pair in range(2):
+        lane = lax.broadcasted_iota(jnp.int32, (256, 128), 1)
+        spreads.append(
+            jnp.concatenate([(spread_ref[pair, :, k : k + 1] == lane).astype(BF) for k in range(2)], axis=1)
+        )
+    for group in range(4):
+        link.arrive(theirs_ref.at[pl.ds(group * 4, 4)], GATHER_KEYS + group)
+
+        def merge(k, _):
+            i = group * 4 + k
+            ours = project(core, i)
+            for pair in range(2):
+                rows = slice(pair * 128, (pair + 1) * 128)
+                stacked = jnp.concatenate([ours[rows], theirs_ref[i, rows]], axis=0)
+                spread = jnp.dot(spreads[pair], stacked, preferred_element_type=F32).astype(BF)
+                for x in range(2):
+                    for half in range(2):
+                        sum_ref[2 * pair + x, group, k, half] = spread[
+                            x * 128 : (x + 1) * 128, half * 128 : (half + 1) * 128
+                        ]
             return 0
 
-        lax.fori_loop(0, 16, body, 0)
-
-    started = []
-
-    def send(src, dst, key, device):
-        copy = remote(src, dst, sems, key, device)
-        copy.start()
-        started.append(copy)
-
-    def arrive(ref, key):
-        remote(ref, ref, sems, key, sibling).wait_recv()
+        lax.fori_loop(0, 4, merge, 0)
 
     def finish(row, rows, half, total):
         spot = (pl.ds(row, rows), pl.ds(half * 128, 128))
         out_ref[spot] = (kept_ref[spot] + total).astype(BF)
 
     ring_reduce(
-        at, sum_ref, AXES, [AXES[part:] + AXES[:part] for part in range(3)], PART_ROWS,
-        (half1, half2, half3), (full1, full2, full3), send, arrive, 0, finish,
-    )
-    for copy in started:
-        copy.wait_send()
-
-
-def return_rows(partial, rank, kept):
+        at, link, sum_ref, AXES, ORDERS, PART_ROWS, 1, ((half0, full0), full1, full2), GATHER_KEYS + 4, finish
+    )
+    link.finish()
+
+
+def run_experts(own, kept, pick, other, spread, gain, router, expert_in, expert_out):
+    keys = GATHER_KEYS + 4 + 36
+    vmem, hbm = pl.BlockSpec(memory_space=pltpu.VMEM), pl.BlockSpec(memory_space=pl.ANY)
     return pl.pallas_call(
-        return_kernel,
+        expert_kernel,
         out_shape=jax.ShapeDtypeStruct((ROWS, 256), BF),
-        in_specs=[pl.BlockSpec(memory_space=pltpu.VMEM)] * 3,
-        out_specs=pl.BlockSpec(memory_space=pltpu.VMEM),
+        in_specs=[vmem] * 7 + [hbm] * 2,
+        out_specs=vmem,
         scratch_shapes=[
-            pltpu.VMEM((4, 16, 2, E_CAP, 128), BF),
+            pltpu.VMEM((4, 2, 4, 4, 2, ROWS, 128), BF),
+            pltpu.VMEM((512, 4096), BF),
+            pltpu.VMEM((512, 128), F32),
+            pltpu.VMEM(expert_in.shape, BF),
+            pltpu.VMEM(expert_out.shape, BF),
+            pltpu.VMEM((512, 512), BF),
+            pltpu.VMEM((16, 256, 256), BF),
+            pltpu.VMEM((16, 256, 256), BF),
             pltpu.VMEM((4, 4, 4, 2, ROWS, 128), BF),
             pltpu.VMEM((2, 4, 4, ROWS, 128), BF),
             pltpu.VMEM((2, 4, 4, 2, ROWS, 128), BF),
-            pltpu.VMEM((2, 4, ROWS, 128), BF),
-            pltpu.VMEM((2, 4, 2, ROWS, 128), BF),
-            pltpu.VMEM((2, ROWS, 128), BF),
-            pltpu.VMEM((2, 2, ROWS, 128), BF),
+            pltpu.VMEM((3, 4, 2, ROWS, 128), BF),
+            pltpu.VMEM((3, 2, ROWS, 128), BF),
             pltpu.SemaphoreType.DMA,
             pltpu.SemaphoreType.DMA,
-            pltpu.SemaphoreType.DMA((36,)),
-            pltpu.SemaphoreType.DMA((36,)),
+            pltpu.SemaphoreType.DMA,
+            pltpu.SemaphoreType.DMA((keys,)),
+            pltpu.SemaphoreType.DMA((keys,)),
         ],
         compiler_params=pltpu.CompilerParams(
-            collective_id=2, has_side_effects=True, vmem_limit_bytes=48 * 2**20
+            collective_id=1, has_side_effects=True, vmem_limit_bytes=60 * 2**20
         ),
-        name="return_rows",
-    )(partial, rank, kept)
+        name="run_experts",
+    )(own, kept, pick, other, spread, gain, router, expert_in, expert_out)
 
 
 LOG2E = 1.4426950408889634
 
 
-def query_kernel(queries_ref, all_ref, local_sem, send_sem, recv_sem):
+def query_kernel(queries_ref, routes_ref, all_ref, all_routes_ref, local_sem, route_sem, send_sem, recv_sem):
     at = place()
-    sems = (send_sem, recv_sem)
-    sibling = device_of(at, c=1 - at["c"])
+    link = Link(at, (send_sem, recv_sem))
+    sibling = link.sibling
     right, left = step_along(at, "x", 1), step_along(at, "x", 3)
-    greet([right, left, sibling])
     x, core = at["x"], at["c"]
+    peers = [(by, device_of(at, x=(x + by // 2) % 4, c=(core + by) % 2)) for by in range(1, 8)]
+    greet([device for _, device in peers])
     kv_head = lax.axis_index("mp") // 2
     own = queries_ref.at[:, pl.ds(pl.multiple_of(kv_head * 512, 512), 512)]
-    local = pltpu.make_async_copy(own, all_ref.at[x, core], local_sem)
-    local.start()
-    started = []
-
-    def send(src, dst, key, device):
-        copy = remote(src, dst, sems, key, device)
+    mine = all_ref.at[x, core]
+    link.send(own, mine, 0, right)
+    link.send(own, mine, 1, left)
+    link.send(own, mine, 4, sibling)
+    local = [
+        pltpu.make_async_copy(own, mine, local_sem),
+        pltpu.make_async_copy(routes_ref, all_routes_ref.at[x, core], route_sem),
+    ]
+    for copy in local:
         copy.start()
-        started.append(copy)
-
-    def arrive(ref, key):
-        remote(ref, ref, sems, key, sibling).wait_recv()
-
+    for by, device in peers:
+        link.send(routes_ref, all_routes_ref.at[x, core], 8 + by, device)
     low, high, far = (x + 3) % 4, (x + 1) % 4, (x + 2) % 4
     upper, lower = pl.ds(0, 64), pl.ds(64, 64)
-    mine = all_ref.at[x, core]
-    send(own, mine, 0, right)
-    send(own, mine, 1, left)
-    send(own, mine, 4, sibling)
     from_low, from_high = all_ref.at[low, core], all_ref.at[high, core]
-    arrive(from_low, 0)
+    link.arrive(from_low, 0)
     first = all_ref.at[low, core, upper]
-    send(first, first, 2, right)
-    arrive(from_high, 1)
+    link.send(first, first, 2, right)
+    link.arrive(from_high, 1)
     second = all_ref.at[high, core, lower]
-    send(second, second, 3, left)
-    send(from_low, from_low, 5, sibling)
-    send(from_high, from_high, 6, sibling)
+    link.send(second, second, 3, left)
+    link.send(from_low, from_low, 5, sibling)
+    link.send(from_high, from_high, 6, sibling)
     for key, rows in ((2, upper), (3, lower)):
         ref = all_ref.at[far, core, rows]
-        arrive(ref, key)
-        send(ref, ref, key + 5, sibling)
+        link.arrive(ref, key)
+        link.send(ref, ref, key + 5, sibling)
     for key, ref in (
         (4, all_ref.at[x, 1 - core]),
         (5, all_ref.at[low, 1 - core]),
@@ -428,26 +438,33 @@
         (7, all_ref.at[far, 1 - core, upper]),
         (8, all_ref.at[far, 1 - core, lower]),
     ):
-        arrive(ref, key)
-    local.wait()
-    for copy in started:
-        copy.wait_send()
-
-
-def gather_queries(queries):
+        link.arrive(ref, key)
+    for by in range(1, 8):
+        giver = all_routes_ref.at[(x + 4 - by // 2) % 4, (core + by) % 2]
+        link.arrive(giver, 8 + by)
+    for copy in local:
+        copy.wait()
+    link.finish()
+
+
+def gather_queries(queries, routes):
     return pl.pallas_call(
         query_kernel,
-        out_shape=jax.ShapeDtypeStruct((4, 2, ROWS, 512), BF),
-        in_specs=[pl.BlockSpec(memory_space=pl.ANY)],
-        out_specs=pl.BlockSpec(memory_space=pl.ANY),
+        out_shape=(
+            jax.ShapeDtypeStruct((4, 2, ROWS, 512), BF),
+            jax.ShapeDtypeStruct((4, 2, 8, ROWS), jnp.int32),
+        ),
+        in_specs=[pl.BlockSpec(memory_space=pl.ANY)] * 2,
+        out_specs=(pl.BlockSpec(memory_space=pl.ANY),) * 2,
         scratch_shapes=[
             pltpu.SemaphoreType.DMA,
-            pltpu.SemaphoreType.DMA((9,)),
-            pltpu.SemaphoreType.DMA((9,)),
+            pltpu.SemaphoreType.DMA,
+            pltpu.SemaphoreType.DMA((16,)),
+            pltpu.SemaphoreType.DMA((16,)),
         ],
         compiler_params=pltpu.CompilerParams(collective_id=3, has_side_effects=True),
         name="gather_queries",
-    )(queries)
+    )(queries, routes)
 
 
 SCALE2 = LOG2E * 128 ** (-0.5)
@@ -615,26 +632,16 @@
     hidden_ref, narrow_ref,
     their_sum, their_stat, run_sum, run_stat, land_sum, land_stat, last_sum, last_stat,
     leaf_sum, leaf_stat, side_sum, side_stat, give_sum,
-    proj_ref, half1, full1, half2, full2, send_sem, recv_sem,
+    proj_ref, full1, full2, send_sem, recv_sem,
 ):
     at = place()
-    sems = (send_sem, recv_sem)
-    sibling = device_of(at, c=1 - at["c"])
+    link = Link(at, (send_sem, recv_sem))
+    send, arrive, sibling = link.send, link.arrive, link.sibling
     beside = {**at, "z": at["z"] + 1 - 2 * (at["z"] % 2)}
     right, left = step_along(at, "x", 1), step_along(at, "x", 3)
     greet(all_peers(at))
     x, core = at["x"], at["c"]
     part = at["z"] % 2
-    started = []
-
-    def send(src, dst, key, device):
-        copy = remote(src, dst, sems, key, device)
-        copy.start()
-        started.append(copy)
-
-    def arrive(ref, key):
-        remote(ref, ref, sems, key, sibling).wait_recv()
-
     send(sum_ref.at[:, 1 - core], their_sum, 0, sibling)
     send(stat_ref.at[:, 1 - core], their_stat, 1, sibling)
     lane = lax.broadcasted_iota(jnp.int32, (1, 128), 1)
@@ -759,11 +766,10 @@
         narrow_ref[half, pl.ds(row, rows), :] = total.astype(BF)
 
     ring_reduce(
-        at, proj_ref, ("y", "z"), (("y", "z"), ("z", "y")), ((0, 64), (64, 64)),
-        (half1, half2), (full1, full2), send, arrive, 12, finish,
-    )
-    for copy in started:
-        copy.wait_send()
+        at, link, proj_ref, ("y", "z"), (("y", "z"), ("z", "y")), ((0, 64), (64, 64)), 0,
+        (full1, full2), 12, finish,
+    )
+    link.finish()
 
 
 def attend(sums, stats, queries, own_queries, leaf, leaf_len, fresh, out_weight, residual):
@@ -790,10 +796,8 @@
             pltpu.VMEM((ROWS, 128), F32),
             pltpu.VMEM((ROWS, 256), BF),
             pltpu.VMEM((4, 4, 2, ROWS, 128), BF),
-            pltpu.VMEM((2, 4, ROWS, 128), BF),
-            pltpu.VMEM((2, 4, 2, ROWS, 128), BF),
-            pltpu.VMEM((2, ROWS, 128), BF),
-            pltpu.VMEM((2, 2, ROWS, 128), BF),
+            pltpu.VMEM((3, 4, 2, ROWS, 128), BF),
+            pltpu.VMEM((3, 2, ROWS, 128), BF),
             pltpu.SemaphoreType.DMA((28,)),
             pltpu.SemaphoreType.DMA((28,)),
         ],
@@ -804,76 +808,6 @@
     )(sums, stats, queries, own_queries, leaf, leaf_len, fresh, out_weight, residual)
 
 
-def ring_reduce(at, sum_ref, dims, orders, part_rows, halves, fulls, send, arrive, base, finish):
-    phases = len(dims)
-    both = slice(None)
-
-    def view(part, phase, value, half):
-        index = dict(at)
-        for axis in orders[part][phase + 1 :]:
-            index[axis] = slice(None)
-        index[orders[part][phase]] = value
-        row, rows = part_rows[part]
-        return tuple(index[axis] for axis in dims) + (half, pl.ds(row, rows), slice(None))
-
-    def landing(part, phase, direction, half):
-        row, rows = part_rows[part]
-        free = (slice(None),) * (phases - 1 - phase)
-        if half is None:
-            return (halves[phase], (direction,) + free + (pl.ds(row, rows), slice(None)))
-        return (fulls[phase], (direction,) + free + (half, pl.ds(row, rows), slice(None)))
-
-    def accumulate(target, others):
-        total = sum_ref[target].astype(F32)
-        for ref, index in others:
-            total += ref[index].astype(F32)
-        return total
-
-    parts = range(len(orders))
-    for phase in range(phases):
-        keys = [base + (part * phases + phase) * 4 for part in parts]
-        for part in parts:
-            axis = orders[part][phase]
-            for direction, by in ((0, 1), (1, 3)):
-                ref, index = landing(part, phase, direction, None)
-                send(
-                    sum_ref.at[view(part, phase, (at[axis] + 2) % 4, direction)],
-                    ref.at[index],
-                    keys[part] + direction,
-                    step_along(at, axis, by),
-                )
-        for part in parts:
-            axis = orders[part][phase]
-            for direction, by in ((0, 1), (1, 3)):
-                ref, index = landing(part, phase, direction, None)
-                arrive(ref.at[index], keys[part] + direction)
-                target = view(part, phase, (at[axis] + by) % 4, direction)
-                sum_ref[target] = accumulate(target, [(ref, index)]).astype(BF)
-            for direction, by in ((0, 1), (1, 3)):
-                ref, index = landing(part, phase, direction, both)
-                send(
-                    sum_ref.at[view(part, phase, (at[axis] + by) % 4, both)],
-                    ref.at[index],
-                    keys[part] + 2 + direction,
-                    step_along(at, axis, by),
-                )
-        for part in parts:
-            axis = orders[part][phase]
-            for direction in range(2):
-                ref, index = landing(part, phase, direction, both)
-                arrive(ref.at[index], keys[part] + 2 + direction)
-            for half in range(2):
-                target = view(part, phase, at[axis], half)
-                total = accumulate(
-                    target, [landing(part, phase, direction, half) for direction in range(2)]
-                )
-                if phase < phases - 1:
-                    sum_ref[target] = total.astype(BF)
-                else:
-                    row, rows = part_rows[part]
-                    finish(row, rows, half, total)
-
-
 def owned_nodes(owner, dp_index, count):
     node = jnp.arange(owner.shape[0])
     owned = owner == dp_index
@@ -910,8 +844,9 @@
     return jnp.maximum(bases + rank[None, :], -1)
 
 
-def expert_phase(hidden, narrow, all_routes, norm_gain, router, expert_in, expert_out):
+def expert_tables(all_routes):
     dp = lax.axis_index("dp")
+    core = dp % 2
     names = jnp.arange(EXPERTS)
     hit = jnp.any(all_routes[:, :, :, None] == names, axis=2)
     before = jnp.tril(jnp.ones((ROWS, ROWS), F32), -1)
@@ -922,28 +857,24 @@
     mine = lax.dynamic_index_in_dim(rank, dp, 0, False)
     other = jnp.sum(all_routes, axis=2) - dp
     packed = mine[:, None, :] == jnp.arange(E_CAP)[None, :, None]
-    other = jnp.sum(jnp.where(packed, other[:, None, :], 0), axis=2).reshape(-1, 1)
-    core = dp % 2
+    other = jnp.sum(jnp.where(packed, other[:, None, :], 0), axis=2)
+    other = other.reshape(4, 2, E_CAP).transpose(1, 0, 2).reshape(-1, 1)
+    shift = (jnp.arange(4) % 2 * E_CAP)[:, None]
+
+    def coded(ranks):
+        return jnp.where(ranks >= 0, ranks + shift, -1)
+
+    mine = mine.reshape(4, 2, ROWS)
+    pick = jnp.stack([coded(mine[:, c]).reshape(2, 1, 256) for c in range(2)])
     ours = lax.dynamic_index_in_dim(rank.reshape(EXPERTS, 4, 2, ROWS), core, 2, False)
-    pair = jnp.stack(
+    spread = jnp.stack(
         [
-            lax.dynamic_index_in_dim(ours, dp, 0, False),
-            lax.dynamic_index_in_dim(ours, dp + 1 - 2 * core, 0, False),
+            coded(lax.dynamic_index_in_dim(ours, dp, 0, False)).reshape(2, 256),
+            coded(lax.dynamic_index_in_dim(ours, dp + 1 - 2 * core, 0, False)).reshape(2, 256),
         ],
-        axis=1,
-    )
-    buf = gather_rows(narrow)
-    partial = run_experts(
-        buf,
-        mine,
-        other,
-        dp.reshape(1, 1).astype(jnp.int32),
-        norm_gain[None, :],
-        router,
-        expert_in[0],
-        expert_out[0],
-    )
-    return return_rows(partial.reshape(4, 2, 16, 2, E_CAP, 128), pair[..., None], hidden)
+        axis=2,
+    )
+    return pick, other, spread
 
 
 def shards(
@@ -971,11 +902,12 @@
 ):
     dp = lax.axis_index("dp")
     mp = lax.axis_index("mp")
-    all_routes = lax.all_gather(routes, "dp", axis=0)
     local_roots, root_place = owned_nodes(root_owner, dp, ROOT_DEV)
     local_branches, branch_place = owned_nodes(branch_owner, dp, BR_DEV)
     codes = slot_codes(slot_request, request_branch, branch_parent, root_place, branch_place)
-    all_queries = gather_queries(queries).reshape(8 * ROWS, 512)
+    all_queries, all_routes = gather_queries(queries, jnp.pad(routes.T, ((0, 6), (0, 0))))
+    all_queries = all_queries.reshape(8 * ROWS, 512)
+    pick, other, spread = expert_tables(all_routes.reshape(8, 8, ROWS)[:, :2].transpose(0, 2, 1))
     sums, stats = node_partials(
         local_roots,
         local_branches,
@@ -996,7 +928,17 @@
         out_weight,
         residual,
     )
-    return expert_phase(hidden, narrow, all_routes, norm_gain, router, expert_in, expert_out)
+    return run_experts(
+        narrow,
+        hidden,
+        pick,
+        other,
+        spread,
+        norm_gain.reshape(16, 1, 256),
+        router,
+        expert_in[0],
+        expert_out[0],
+    )
 
 
 def solution(mesh):

time: 228 us -> 186 us (0.82)
  Pallas kernels: 191 us -> 157 us
  blocking collectives: 9.75 us -> 0 us
    pallas_call x4 -> x2, Pallas kernels: 122 us -> 93.1 us  [the longest x1 79.5 us: run_experts(): pl.pallas_call(expert_kernel, out_shape=jax.ShapeDtypeStruct((ROWS, 256),...]
    all_gather x1 -> x0, blocking collectives: 9.75 us -> none  [shards(): all_routes = lax.all_gather(routes, 'dp', axis=0)]
    pallas_call x1, Pallas kernels: 51.3 us -> 46.2 us  [attend(): pl.pallas_call(attend_kernel, out_shape=(jax.ShapeDtypeStruct((ROWS, 256)...]
    unnamed x39 -> x37, local copies, waits for them, and re-layouts: 14.8 us -> 13.4 us
where the time goes in v2:
time: 186 us; the launch traced here: 185 us
  Pallas kernels  157 us (84%)
  local copies, waits for them, and re-layouts  17.6 us (9%)
  other arithmetic  9.72 us (5%)
    pallas_call x1, Pallas kernels, run_experts(): pl.pallas_call(expert_kernel, out_shape=jax.ShapeDtypeStruct((ROWS, 256),...  79.5 us
    pallas_call x1, Pallas kernels, attend(): pl.pallas_call(attend_kernel, out_shape=(jax.ShapeDtypeStruct((ROWS, 256)...  46.2 us
    pallas_call x1, Pallas kernels, node_partials(): pl.pallas_call(node_kernel, out_shape=(jax.ShapeDtypeStruct((8, ROWS, 512...  18 us
    pallas_call x1, Pallas kernels, gather_queries(): pl.pallas_call(query_kernel, out_shape=(jax.ShapeDtypeStruct((4, 2, ROWS,...  13.5 us
    unnamed x37, local copies, waits for them, and re-layouts  13.4 us

profile of v2, /device:TPU:0, one launch (start us, length us, event | category | flops | bytes accessed | tf_op | source)
XLA Modules:
  0.0 185.0 jit_solution(10988329339282760126)
XLA Ops:
  0.0 0.7 broadcast_compare_fusion.1
  1.0 0.7 broadcast_compare_fusion
  1.9 0.8 copy.57.branch_pages_ref
  2.7 1.3 pad.4.routes_ref
  3.9 13.5 %gather_queries.1 = (bf16[4,2,128,512]{3,2,1,0:T(8,128)(2,1)}, s32[4,2,8,128]{3,2,1,0:T(8,128)}) custom-call(bf16[128,4096]{1,0:T(8,128)(2,1)} %queries_ref.1, s32[8,128]{1,0:T(8,128)} %pad.4.routes_ref), custom_call_target="tpu_custom_call" | custom-call | tf_op jit(solution)/shard_map/gather_queries/pallas_call | solution.py:451
  17.5 0.7 broadcast_select_fusion
  18.1 0.7 select_reduce_fusion.3
  18.9 0.9 convert_reduce_fusion.1
  19.8 0.7 fusion.15
  20.5 1.5 select_reduce_fusion
  22.1 0.5 convert_reduce_fusion
  22.7 0.2 copy.56
  22.9 1.9 %copy-done.1 = bf16[2,96,1,64,128]{4,3,2,1,0:T(8,128)(2,1)S(1)} copy-done((bf16[2,96,1,64,128]{4,3,2,1,0:T(8,128)(2,1)S(1)}, bf16[2,96,1,64,128]{4,3,2,1,0:T(8,128)(2,1)}, u32[]{:S(2)}) %copy-start.1) | copy-done | bytes 3145752
  24.8 1.2 copy-done.3
  26.0 0.7 copy-done.11
  26.7 0.7 copy-done.12
  27.4 0.7 copy-done.13
  28.0 18.0 %node_partials.1 = (bf16[8,128,512]{2,1,0:T(8,128)(2,1)S(1)}, f32[8,128,128]{2,1,0:T(8,128)S(1)}) custom-call(s32[2]{0:T(128)S(1)} %fusion.13.local_ref, s32[8]{0:T(128)S(1)} %select_reduce_fusion.4.branch_id_ref, s32[16,32]{1,0:T(8,128)S(1)} %copy-done.11, s32[64,4]{1,0:T(8,128)S(1)} %copy.57.branch_pages_ref, s32[16]{0:T(128)S(1)} %copy-done.12, ...), custom_call_target="tpu_custom_call" | custom-call | tf_op jit(solution)/shard_map/node_partials/pallas_call | solution.py:609
  46.1 1.0 copy-done.4
  47.0 0.8 copy-done.6
  47.9 0.9 dynamic-slice_convert_fusion.query_ref
  48.8 0.8 constant_dynamic-slice_fusion.4.own_query_ref
  49.8 1.2 copy-done.5
  51.1 1.0 copy-done.7
  52.1 46.2 %attend.1 = (f32[128,256]{1,0:T(8,128)S(1)}, bf16[2,128,128]{2,1,0:T(8,128)(2,1)S(1)}) custom-call(bf16[4,2,128,512]{3,2,1,0:T(8,128)(2,1)S(1)} %bitcast.51, f32[4,2,128,128]{3,2,1,0:T(8,128)S(1)} %bitcast.52, f32[128,512]{1,0:T(8,128)S(1)} %dynamic-slice_convert_fusion.query_ref, bf16[128,256]{1,0:T(8,128)(2,1)S(1)} %constant_dynamic-slice_fusion.4.own_query_ref, ...), custom_call_target="tpu_custom_call" | custom-call | tf_op jit(solution)/shard_map/attend/pallas_call | solution.py:776
  98.3 0.6 copy-done.8
  99.3 0.6 pad_add_fusion.1.pick_ref
  100.2 0.9 reshape.271.other_ref
  101.8 0.9 pad_add_fusion.spread_ref
  102.7 1.3 copy.69.router_ref
  104.0 79.5 %run_experts.1 = bf16[128,256]{1,0:T(8,128)(2,1)} custom-call(bf16[2,128,128]{2,1,0:T(8,128)(2,1)} %copy-done.10, f32[128,256]{1,0:T(8,128)} %copy-done.8, s32[2,2,1,256]{3,2,1,0:T(1,128)} %pad_add_fusion.1.pick_ref, s32[512,1]{1,0:T(8,128)} %reshape.271.other_ref, s32[2,256,2]{2,1,0:T(8,128)} %pad_add_fusion.spread_ref, f32[16,1,256]{2,1,0:T(1,128)} %bitcast.59, ...), custom_call_target="tpu_custom_call" | custom-call | tf_op jit(solution)/shard_map/run_experts/pallas_call | solution.py:362
  183.6 1.5 copy.73
  (53 shorter events, 2.1 us)
Async XLA Ops:
  0.0 49.8 %copy-start = (bf16[2,128,1024]{2,1,0:T(8,128)(2,1)S(1)}, bf16[2,128,1024]{2,1,0:T(8,128)(2,1)}, u32[]{:S(2)}) copy-start(bf16[2,128,1024]{2,1,0:T(8,128)(2,1)} %param.22) | copy-start | bytes 1572868
  0.0 49.6 %copy-start.16 = (s32[128]{0:T(128)S(1)}, s32[128]{0:T(128)}, u32[]{:S(2)}) copy-start(s32[128]{0:T(128)} %param.40) | copy-start | bytes 1540
  0.0 49.8 %copy-start.9 = (bf16[128,256]{1,0:T(8,128)(2,1)S(1)}, bf16[128,256]{1,0:T(8,128)(2,1)}, u32[]{:S(2)}) copy-start(bf16[128,256]{1,0:T(8,128)(2,1)} %residual_ref.1) | copy-start | bytes 196612
  22.9 1.9 %copy-start.1 = (bf16[2,96,1,64,128]{4,3,2,1,0:T(8,128)(2,1)S(1)}, bf16[2,96,1,64,128]{4,3,2,1,0:T(8,128)(2,1)}, u32[]{:S(2)}) copy-start(bf16[2,96,1,64,128]{4,3,2,1,0:T(8,128)(2,1)} %param.29) | copy-start | bytes 9437188
  24.8 1.2 copy-start.3
  26.0 0.7 copy-start.11
  26.7 0.7 copy-start.12
  27.4 0.7 copy-start.13
  28.0 21.8 %copy-start.2 = (bf16[256,4096]{1,0:T(8,128)(2,1)S(1)}, bf16[256,4096]{1,0:T(8,128)(2,1)}, u32[]{:S(2)}) copy-start(bf16[256,4096]{1,0:T(8,128)(2,1)} %weight_ref.1) | copy-start | bytes 6291460
  46.1 1.0 copy-start.4
  47.0 0.8 copy-start.6
  49.8 1.2 copy-start.5
  51.1 1.0 copy-start.7
  52.1 46.9 %copy-start.15 = (s32[4,2,8,128]{3,2,1,0:T(8,128)S(1)}, s32[4,2,8,128]{3,2,1,0:T(8,128)}, u32[]{:S(2)}) copy-start(s32[4,2,8,128]{3,2,1,0:T(8,128)} %get-tuple-element.16) | copy-start | bytes 98308
  52.1 50.6 %copy-start.14 = (bf16[4096,8]{0,1:T(8,128)(2,1)S(1)}, bf16[4096,8]{0,1:T(8,128)(2,1)}, u32[]{:S(2)}) copy-start(bf16[4096,8]{0,1:T(8,128)(2,1)} %param.26) | copy-start | bytes 196612
  98.3 0.6 copy-start.8
  98.9 5.1 %copy-start.10 = (bf16[2,128,128]{2,1,0:T(8,128)(2,1)}, bf16[2,128,128]{2,1,0:T(8,128)(2,1)S(1)}, u32[]{:S(2)}) copy-start(bf16[2,128,128]{2,1,0:T(8,128)(2,1)S(1)} %get-tuple-element.14.own_ref) | copy-start | bytes 196612

commit v3 on v2

--- a/solution.py
+++ b/solution.py
@@ -82,7 +82,7 @@
             copy.wait_send()
 
 
-def gather_all(at, link, own_ref, buf_ref, local_sem, base):
+def gather_all(at, link, own_ref, buf_ref, local_sem, base, meanwhile):
     both = slice(None)
     core = at["c"]
 
@@ -108,6 +108,8 @@
                 link.send(src, ref, base + (part * 2 + phase) * 3 + by - 1, step_along(at, axis, by))
         if phase == 0:
             local.wait()
+        else:
+            meanwhile()
         for part in range(3):
             axis = ORDERS[part][phase]
             for by in (1, 3, 2):
@@ -228,9 +230,9 @@
 
 
 def expert_kernel(
-    own_ref, kept_ref, pick_ref, other_ref, spread_ref, gain_ref, router_ref, up_hbm, down_hbm,
+    own_ref, kept_ref, routes_ref, gain_ref, router_ref, up_hbm, down_hbm,
     out_ref,
-    buf_ref, rows_ref, gate_ref, up_ref, down_ref, act_ref, give_ref, theirs_ref, sum_ref,
+    buf_ref, code_ref, other_ref, rows_ref, gate_ref, up_ref, down_ref, act_ref, give_ref, theirs_ref, sum_ref,
     half0, full0, full1, full2,
     local_sem, up_sem, down_sem, send_sem, recv_sem,
 ):
@@ -242,12 +244,44 @@
     link = Link(at, (send_sem, recv_sem))
     core = at["c"]
     mine = lax.axis_index("dp")
-    others = gather_all(at, link, own_ref, buf_ref, local_sem, 0)
+    row_index = lax.broadcasted_iota(jnp.int32, (ROWS, ROWS), 0)
+    lane_index = lax.broadcasted_iota(jnp.int32, (ROWS, ROWS), 1)
+    upright = []
+
+    def tables():
+        unit = (row_index == lane_index).astype(BF)
+        later = (row_index < lane_index).astype(BF)
+        earlier = (lane_index < row_index).astype(BF)
+        first = jnp.concatenate([routes_ref[b // 2, b % 2, 0:1, :] for b in range(8)], axis=0)
+        second = jnp.concatenate([routes_ref[b // 2, b % 2, 1:2, :] for b in range(8)], axis=0)
+        shift = (lax.broadcasted_iota(jnp.int32, (8, ROWS), 0) // 2) % 2 * E_CAP
+        hit = ((first == mine) | (second == mine)).astype(F32)
+        rank = jnp.dot(hit.astype(BF), later, preferred_element_type=F32).astype(jnp.int32)
+        code_ref[0:8, :] = jnp.where(hit > 0.5, rank + shift, -1)
+        other_ref[...] = first + second - mine
+        for expert in (mine, mine + 1 - 2 * core):
+            hit = ((first == expert) | (second == expert)).astype(BF)
+            there = lax.dot_general(unit, hit, BY_ROW, preferred_element_type=F32)
+            rank = lax.dot_general(earlier, hit, BY_ROW, preferred_element_type=F32)
+            codes = jnp.where(there > 0.5, rank, -1.0)
+            upright.append(
+                [jnp.where(core == 0, codes[:, 2 * b : 2 * b + 1], codes[:, 2 * b + 1 : 2 * b + 2]) for b in range(4)]
+            )
+
+    others = gather_all(at, link, own_ref, buf_ref, local_sem, 0, tables)
 
     def compact(plane):
         base = pl.multiple_of(plane * 256, 256)
         wanted = lax.broadcasted_iota(jnp.int32, (128, 256), 0)
-        picks = [(wanted == pick_ref[plane, pair]).astype(BF) for pair in range(2)]
+        picks, answers = [], []
+        for pair in range(2):
+            blocks = [pl.ds(4 * pair + 2 * k + plane, 1) for k in range(2)]
+            code = jnp.concatenate([code_ref[b, :] for b in blocks], axis=1)
+            other = jnp.concatenate([other_ref[b, :] for b in blocks], axis=1)
+            chosen = wanted == code
+            picks.append(chosen.astype(BF))
+            answers.append(jnp.sum(jnp.where(chosen, other, 0), axis=1, keepdims=True))
+        answer = jnp.concatenate(answers, axis=0)
 
         def fill(y, squares):
             for z in range(4):
@@ -283,7 +317,7 @@
         lane = lax.broadcasted_iota(jnp.int32, logits.shape, 1)
         here = jnp.sum(jnp.where(lane == mine, logits, 0.0), axis=1, keepdims=True)
         there = jnp.sum(
-            jnp.where(lane == other_ref[pl.ds(base, 256), 0:1], logits, 0.0), axis=1, keepdims=True
+            jnp.where(lane == answer, logits, 0.0), axis=1, keepdims=True
         )
         most = jnp.maximum(here, there)
         here = jnp.exp(here - most)
@@ -323,9 +357,17 @@
         )
     spreads = []
     for pair in range(2):
-        lane = lax.broadcasted_iota(jnp.int32, (256, 128), 1)
+        corners = []
+        for k in range(2):
+            empty = jnp.zeros((ROWS, E_CAP), BF)
+            lane = lax.broadcasted_iota(jnp.int32, (ROWS, E_CAP), 1).astype(F32)
+            for codes in upright:
+                hit = (codes[2 * pair + k] == lane).astype(BF)
+                corners.append(jnp.concatenate([hit, empty] if k == 0 else [empty, hit], axis=1))
         spreads.append(
-            jnp.concatenate([(spread_ref[pair, :, k : k + 1] == lane).astype(BF) for k in range(2)], axis=1)
+            jnp.concatenate(
+                [jnp.concatenate(corners[0:2], axis=1), jnp.concatenate(corners[2:4], axis=1)], axis=0
+            )
         )
     for group in range(4):
         link.arrive(theirs_ref.at[pl.ds(group * 4, 4)], GATHER_KEYS + group)
@@ -356,16 +398,18 @@
     link.finish()
 
 
-def run_experts(own, kept, pick, other, spread, gain, router, expert_in, expert_out):
+def run_experts(own, kept, routes, gain, router, expert_in, expert_out):
     keys = GATHER_KEYS + 4 + 36
     vmem, hbm = pl.BlockSpec(memory_space=pltpu.VMEM), pl.BlockSpec(memory_space=pl.ANY)
     return pl.pallas_call(
         expert_kernel,
         out_shape=jax.ShapeDtypeStruct((ROWS, 256), BF),
-        in_specs=[vmem] * 7 + [hbm] * 2,
+        in_specs=[vmem] * 5 + [hbm] * 2,
         out_specs=vmem,
         scratch_shapes=[
             pltpu.VMEM((4, 2, 4, 4, 2, ROWS, 128), BF),
+            pltpu.VMEM((8, ROWS), jnp.int32),
+            pltpu.VMEM((8, ROWS), jnp.int32),
             pltpu.VMEM((512, 4096), BF),
             pltpu.VMEM((512, 128), F32),
             pltpu.VMEM(expert_in.shape, BF),
@@ -388,7 +432,7 @@
             collective_id=1, has_side_effects=True, vmem_limit_bytes=60 * 2**20
         ),
         name="run_experts",
-    )(own, kept, pick, other, spread, gain, router, expert_in, expert_out)
+    )(own, kept, routes, gain, router, expert_in, expert_out)
 
 
 LOG2E = 1.4426950408889634
@@ -579,7 +623,7 @@
             parts.append((sums, stats))
         merged, stats = merge_blocks(parts[0], parts[1], 4)
         sum_ref[block] = merged.astype(BF)
-        stat_ref[block] = stats
+        stat_ref[block] = stats.T[0:8]
         return 0
 
     lax.fori_loop(0, 8, spread_body, 0)
@@ -610,7 +654,7 @@
         node_kernel,
         out_shape=(
             jax.ShapeDtypeStruct((8, ROWS, 512), BF),
-            jax.ShapeDtypeStruct((8, ROWS, 128), F32),
+            jax.ShapeDtypeStruct((8, 8, ROWS), F32),
         ),
         in_specs=[pl.BlockSpec(memory_space=pltpu.SMEM)] * 7 + [pl.BlockSpec(memory_space=pltpu.VMEM)] * 4,
         out_specs=(pl.BlockSpec(memory_space=pltpu.VMEM),) * 2,
@@ -628,28 +672,64 @@
 
 
 def attend_kernel(
-    sum_ref, stat_ref, query_ref, own_query_ref, leaf_ref, leaf_len_ref, fresh_ref, weight_ref, residual_ref,
+    sum_hbm, stat_hbm, query_hbm, leaf_hbm, leaf_len_ref, fresh_hbm, weight_hbm, residual_ref,
     hidden_ref, narrow_ref,
-    their_sum, their_stat, run_sum, run_stat, land_sum, land_stat, last_sum, last_stat,
-    leaf_sum, leaf_stat, side_sum, side_stat, give_sum,
-    proj_ref, full1, full2, send_sem, recv_sem,
+    own_sum, own_stat, their_sum, their_stat, run_sum, run_stat, land_sum, land_stat,
+    query_ref, wide_query, own_query_ref, leaf_ref, length_ref, fresh_ref, weight_ref,
+    leaf_sum, leaf_stat, give_stat, side_sum, side_stat, give_sum,
+    proj_ref, full1, full2, load_sem, send_sem, recv_sem,
 ):
     at = place()
     link = Link(at, (send_sem, recv_sem))
     send, arrive, sibling = link.send, link.arrive, link.sibling
     beside = {**at, "z": at["z"] + 1 - 2 * (at["z"] % 2)}
-    right, left = step_along(at, "x", 1), step_along(at, "x", 3)
-    greet(all_peers(at))
     x, core = at["x"], at["c"]
     part = at["z"] % 2
-    send(sum_ref.at[:, 1 - core], their_sum, 0, sibling)
-    send(stat_ref.at[:, 1 - core], their_stat, 1, sibling)
+    mp = lax.axis_index("mp")
+    kv_head = mp // 2
+
+    def columns(ref, width, index):
+        return ref.at[:, pl.ds(pl.multiple_of(index * width, width), width)]
+
+    loads = [
+        pltpu.make_async_copy(src, dst, load_sem.at[i])
+        for i, (src, dst) in enumerate(
+            (
+                (columns(query_hbm, 512, kv_head), query_ref),
+                (leaf_hbm.at[:, :, 0], leaf_ref),
+                (sum_hbm.at[:, core], own_sum),
+                (stat_hbm.at[:, core], own_stat),
+                (columns(query_hbm, 256, mp), own_query_ref),
+                (columns(fresh_hbm.at[0], 128, kv_head), fresh_ref.at[0]),
+                (columns(fresh_hbm.at[1], 128, kv_head), fresh_ref.at[1]),
+                (weight_hbm, weight_ref),
+            )
+        )
+    ]
+    for load in loads:
+        load.start()
+    greet(all_peers(at))
+    send(sum_hbm.at[:, 1 - core], their_sum, 0, sibling)
+    send(stat_hbm.at[:, 1 - core], their_stat, 1, sibling)
     lane = lax.broadcasted_iota(jnp.int32, (1, 128), 1)
-
-    def leaf_body(i, _):
-        base = pl.multiple_of(i * 8, 8)
+    unit = lax.broadcasted_iota(jnp.int32, (ROWS, ROWS), 0) == lax.broadcasted_iota(
+        jnp.int32, (ROWS, ROWS), 1
+    )
+    lengths_row = jnp.broadcast_to(leaf_len_ref[...], (ROWS, ROWS))
+    length_ref[...] = jnp.broadcast_to(
+        jnp.sum(jnp.where(unit, lengths_row, 0), axis=1, keepdims=True), (ROWS, ROWS)
+    )
+
+    def upright(stats):
+        return jnp.concatenate([stats, jnp.zeros((ROWS - 8, ROWS), F32)], axis=0).T
+
+    loads[0].wait()
+    loads[1].wait()
+    wide_query[...] = query_ref[...].astype(F32)
+
+    def leaf_group(base):
         span = pl.ds(base, 8)
-        heads = [query_ref[span, h * 128 : (h + 1) * 128] for h in range(4)]
+        heads = [wide_query[span, h * 128 : (h + 1) * 128] for h in range(4)]
         stacked = jnp.concatenate(heads, axis=0)
         keys = leaf_ref[0, span].reshape(512, 128)
         values = leaf_ref[1, span].reshape(512, 128)
@@ -658,7 +738,7 @@
         )
         row = lax.broadcasted_iota(jnp.int32, (32, 512), 0) % 8
         col = lax.broadcasted_iota(jnp.int32, (32, 512), 1)
-        lengths = jnp.concatenate([leaf_len_ref[span, 0:1]] * 4, axis=0)
+        lengths = jnp.concatenate([length_ref[span, 0:1]] * 4, axis=0)
         usable = (row == col // 64) & (part * 64 + col % 64 < lengths)
         scores = jnp.where(usable, scores * SCALE2, MASKED_SCORE)
         top = jnp.max(scores, axis=1, keepdims=True)
@@ -671,54 +751,33 @@
             stats = jnp.where(lane == h, top[h * 8 : (h + 1) * 8], stats)
             stats = jnp.where(lane == 4 + h, total[h * 8 : (h + 1) * 8], stats)
         leaf_stat[span, :] = stats
+
+    def leaf_body(i, _):
+        for k in range(4):
+            leaf_group(pl.multiple_of(i * 32 + k * 8, 8))
         return 0
 
-    lax.fori_loop(0, 16, leaf_body, 0)
+    lax.fori_loop(0, 4, leaf_body, 0)
+    loads[2].wait()
+    loads[3].wait()
     arrive(their_sum, 0)
     arrive(their_stat, 1)
-
-    def cross_body(i, _):
-        value = lax.rem(x + 2 + i, 4)
+    for by in (2, 1, 3):
+        value = (x + by) % 4
         merged, stats = merge_blocks(
-            (sum_ref[value, core], stat_ref[value, core]), (their_sum[value], their_stat[value]), 4
+            (own_sum[value], upright(own_stat[value])), (their_sum[value], upright(their_stat[value])), 4
         )
-        run_sum[value] = merged.astype(BF)
-        run_stat[value] = stats
-        return 0
-
-    def cross_merge(by):
-        cross_body(by - 2, 0)
-
-    low, high, far = (x + 3) % 4, (x + 1) % 4, (x + 2) % 4
-    upper, lower = pl.ds(0, 64), pl.ds(64, 64)
-    cross_merge(2)
-    for key, rows, device in ((2, upper, right), (4, lower, left)):
-        send(run_sum.at[far, rows], land_sum.at[rows], key, device)
-        send(run_stat.at[far, rows], land_stat.at[rows], key + 1, device)
-    cross_merge(3)
-    cross_merge(4)
-    cross_merge(5)
-    for key, rows, value, device, side in ((2, upper, high, right, 0), (4, lower, low, left, 1)):
-        arrive(land_sum.at[rows], key)
-        arrive(land_stat.at[rows], key + 1)
-        merged, stats = merge_blocks(
-            (run_sum[value, rows], run_stat[value, rows]), (land_sum[rows], land_stat[rows]), 4
-        )
-        run_sum[value, rows] = merged.astype(BF)
-        run_stat[value, rows] = stats
-        send(run_sum.at[value], last_sum.at[side], key + 4, device)
-        send(run_stat.at[value], last_stat.at[side], key + 5, device)
-    sums, stats = merge_blocks((run_sum[x], run_stat[x]), (leaf_sum[...], leaf_stat[...]), 4)
-    for side, key in ((0, 6), (1, 8)):
-        arrive(last_sum.at[side], key)
-        arrive(last_stat.at[side], key + 1)
-        sums, stats = merge_blocks((sums, stats), (last_sum[side], last_stat[side]), 4)
-    first = part == 0
-    give_sum[...] = jnp.where(first, sums[:, 256:], sums[:, :256]).astype(BF)
-    leaf_stat[...] = stats
-    send(give_sum, side_sum, 10, device_of(beside))
-    send(leaf_stat, side_stat, 11, device_of(beside))
-    kept = jnp.where(first, sums[:, :256], sums[:, 256:])
+        run_sum[by - 1] = merged.astype(BF)
+        run_stat[by - 1] = stats.T[0:8]
+        device = step_along(at, "x", by)
+        send(run_sum.at[by - 1], land_sum.at[by - 1], 2 * by, device)
+        send(run_stat.at[by - 1], land_stat.at[by - 1], 2 * by + 1, device)
+    sums, stats = merge_blocks(
+        (own_sum[x], upright(own_stat[x])), (their_sum[x], upright(their_stat[x])), 4
+    )
+    sums, stats = merge_blocks((sums, stats), (leaf_sum[...], leaf_stat[...]), 4)
+    for load in loads[4:]:
+        load.wait()
     fresh_key = fresh_ref[0].astype(F32)
     fresh_value = fresh_ref[1].astype(F32)
     own_scores = [
@@ -726,9 +785,19 @@
         * SCALE2
         for h in range(2)
     ]
+    for by in (1, 3, 2):
+        arrive(land_sum.at[by - 1], 2 * by)
+        arrive(land_stat.at[by - 1], 2 * by + 1)
+        sums, stats = merge_blocks((sums, stats), (land_sum[by - 1], upright(land_stat[by - 1])), 4)
+    first = part == 0
+    give_sum[...] = jnp.where(first, sums[:, 256:], sums[:, :256]).astype(BF)
+    give_stat[...] = stats.T[0:8]
+    send(give_sum, side_sum, 10, device_of(beside))
+    send(give_stat, side_stat, 11, device_of(beside))
+    kept = jnp.where(first, sums[:, :256], sums[:, 256:])
     arrive(side_sum, 10)
     arrive(side_stat, 11)
-    theirs = side_stat[...]
+    theirs = upright(side_stat[...])
     pieces = []
     for h in range(2):
         span = slice(h * 128, (h + 1) * 128)
@@ -772,32 +841,42 @@
     link.finish()
 
 
-def attend(sums, stats, queries, own_queries, leaf, leaf_len, fresh, out_weight, residual):
+def attend(sums, stats, queries, leaf, leaf_len, fresh, out_weight, residual):
+    vmem, hbm = pl.BlockSpec(memory_space=pltpu.VMEM), pl.BlockSpec(memory_space=pl.ANY)
     return pl.pallas_call(
         attend_kernel,
         out_shape=(
             jax.ShapeDtypeStruct((ROWS, 256), F32),
             jax.ShapeDtypeStruct((2, ROWS, 128), BF),
         ),
-        in_specs=[pl.BlockSpec(memory_space=pltpu.VMEM)] * 9,
-        out_specs=(pl.BlockSpec(memory_space=pltpu.VMEM),) * 2,
+        in_specs=[hbm, hbm, hbm, hbm, vmem, hbm, hbm, vmem],
+        out_specs=(vmem, vmem),
         scratch_shapes=[
             pltpu.VMEM((4, ROWS, 512), BF),
-            pltpu.VMEM((4, ROWS, 128), F32),
+            pltpu.VMEM((4, 8, ROWS), F32),
             pltpu.VMEM((4, ROWS, 512), BF),
-            pltpu.VMEM((4, ROWS, 128), F32),
+            pltpu.VMEM((4, 8, ROWS), F32),
+            pltpu.VMEM((3, ROWS, 512), BF),
+            pltpu.VMEM((3, 8, ROWS), F32),
+            pltpu.VMEM((3, ROWS, 512), BF),
+            pltpu.VMEM((3, 8, ROWS), F32),
             pltpu.VMEM((ROWS, 512), BF),
-            pltpu.VMEM((ROWS, 128), F32),
-            pltpu.VMEM((2, ROWS, 512), BF),
-            pltpu.VMEM((2, ROWS, 128), F32),
+            pltpu.VMEM((ROWS, 512), F32),
+            pltpu.VMEM((ROWS, 256), BF),
+            pltpu.VMEM((2, ROWS, 64, 128), BF),
+            pltpu.VMEM((ROWS, ROWS), jnp.int32),
+            pltpu.VMEM((2, ROWS, 128), BF),
+            pltpu.VMEM((256, 4096), BF),
             pltpu.VMEM((ROWS, 512), F32),
             pltpu.VMEM((ROWS, 128), F32),
+            pltpu.VMEM((8, ROWS), F32),
             pltpu.VMEM((ROWS, 256), BF),
-            pltpu.VMEM((ROWS, 128), F32),
+            pltpu.VMEM((8, ROWS), F32),
             pltpu.VMEM((ROWS, 256), BF),
             pltpu.VMEM((4, 4, 2, ROWS, 128), BF),
             pltpu.VMEM((3, 4, 2, ROWS, 128), BF),
             pltpu.VMEM((3, 2, ROWS, 128), BF),
+            pltpu.SemaphoreType.DMA((8,)),
             pltpu.SemaphoreType.DMA((28,)),
             pltpu.SemaphoreType.DMA((28,)),
         ],
@@ -805,7 +884,7 @@
             collective_id=4, has_side_effects=True, vmem_limit_bytes=48 * 2**20
         ),
         name="attend",
-    )(sums, stats, queries, own_queries, leaf, leaf_len, fresh, out_weight, residual)
+    )(sums, stats, queries, leaf, leaf_len, fresh, out_weight, residual)
 
 
 def owned_nodes(owner, dp_index, count):
@@ -842,39 +921,6 @@
     mine = slot_branch[None, :, None] == branch[None, None, :]
     bases = jnp.sum(jnp.where(mine, jnp.stack([root_base, branch_base])[:, None, :], 0), axis=2)
     return jnp.maximum(bases + rank[None, :], -1)
-
-
-def expert_tables(all_routes):
-    dp = lax.axis_index("dp")
-    core = dp % 2
-    names = jnp.arange(EXPERTS)
-    hit = jnp.any(all_routes[:, :, :, None] == names, axis=2)
-    before = jnp.tril(jnp.ones((ROWS, ROWS), F32), -1)
-    rank = jnp.einsum(
-        "rq,bqe->ebr", before.astype(BF), hit.astype(BF), preferred_element_type=F32
-    ).astype(jnp.int32)
-    rank = jnp.where(hit.transpose(2, 0, 1), rank, -1)
-    mine = lax.dynamic_index_in_dim(rank, dp, 0, False)
-    other = jnp.sum(all_routes, axis=2) - dp
-    packed = mine[:, None, :] == jnp.arange(E_CAP)[None, :, None]
-    other = jnp.sum(jnp.where(packed, other[:, None, :], 0), axis=2)
-    other = other.reshape(4, 2, E_CAP).transpose(1, 0, 2).reshape(-1, 1)
-    shift = (jnp.arange(4) % 2 * E_CAP)[:, None]
-
-    def coded(ranks):
-        return jnp.where(ranks >= 0, ranks + shift, -1)
-
-    mine = mine.reshape(4, 2, ROWS)
-    pick = jnp.stack([coded(mine[:, c]).reshape(2, 1, 256) for c in range(2)])
-    ours = lax.dynamic_index_in_dim(rank.reshape(EXPERTS, 4, 2, ROWS), core, 2, False)
-    spread = jnp.stack(
-        [
-            coded(lax.dynamic_index_in_dim(ours, dp, 0, False)).reshape(2, 256),
-            coded(lax.dynamic_index_in_dim(ours, dp + 1 - 2 * core, 0, False)).reshape(2, 256),
-        ],
-        axis=2,
-    )
-    return pick, other, spread
 
 
 def shards(
@@ -907,7 +953,6 @@
     codes = slot_codes(slot_request, request_branch, branch_parent, root_place, branch_place)
     all_queries, all_routes = gather_queries(queries, jnp.pad(routes.T, ((0, 6), (0, 0))))
     all_queries = all_queries.reshape(8 * ROWS, 512)
-    pick, other, spread = expert_tables(all_routes.reshape(8, 8, ROWS)[:, :2].transpose(0, 2, 1))
     sums, stats = node_partials(
         local_roots,
         local_branches,
@@ -919,25 +964,16 @@
     )
     hidden, narrow = attend(
         sums.reshape(4, 2, ROWS, 512),
-        stats.reshape(4, 2, ROWS, 128),
-        lax.dynamic_slice_in_dim(queries, (mp // 2) * 512, 512, 1).astype(F32),
-        lax.dynamic_slice_in_dim(queries, mp * 256, 256, 1),
-        leaf_cache[:, :, 0],
-        leaf_len[:, None],
-        lax.dynamic_slice_in_dim(new_kv, (mp // 2) * 128, 128, 2),
+        stats.reshape(4, 2, 8, ROWS),
+        queries,
+        leaf_cache,
+        leaf_len[None, :],
+        new_kv,
         out_weight,
         residual,
     )
     return run_experts(
-        narrow,
-        hidden,
-        pick,
-        other,
-        spread,
-        norm_gain.reshape(16, 1, 256),
-        router,
-        expert_in[0],
-        expert_out[0],
+        narrow, hidden, all_routes, norm_gain.reshape(16, 1, 256), router, expert_in[0], expert_out[0]
     )
 
 

time: 186 us -> 172 us (0.925)
  local copies, waits for them, and re-layouts: 17.6 us -> 11.5 us
  Pallas kernels: 157 us -> 153 us
  other arithmetic: 9.72 us -> 7.08 us
    pallas_call x1, Pallas kernels: 46.2 us -> 41.7 us  [attend(): pl.pallas_call(attend_kernel, out_shape=(jax.ShapeDtypeStruct((ROWS, 256)...]
    unnamed x37 -> x29, local copies, waits for them, and re-layouts: 13.4 us -> 9.99 us
where the time goes in v3:
time: 172 us; the launch traced here: 171 us
  Pallas kernels  153 us (89%)
  local copies, waits for them, and re-layouts  11.5 us (7%)
  other arithmetic  7.08 us (4%)
    pallas_call x1, Pallas kernels, run_experts(): pl.pallas_call(expert_kernel, out_shape=jax.ShapeDtypeStruct((ROWS, 256),...  79 us
    pallas_call x1, Pallas kernels, attend(): pl.pallas_call(attend_kernel, out_shape=(jax.ShapeDtypeStruct((ROWS, 256)...  41.7 us
    pallas_call x1, Pallas kernels, node_partials(): pl.pallas_call(node_kernel, out_shape=(jax.ShapeDtypeStruct((8, ROWS, 512...  18.4 us
    pallas_call x1, Pallas kernels, gather_queries(): pl.pallas_call(query_kernel, out_shape=(jax.ShapeDtypeStruct((4, 2, ROWS,...  13.6 us
    unnamed x29, local copies, waits for them, and re-layouts  9.99 us

profile of v3, /device:TPU:0, one launch (start us, length us, event | category | flops | bytes accessed | tf_op | source)
XLA Modules:
  0.0 171.3 jit_solution(5280349249528662524)
XLA Ops:
  0.0 0.8 broadcast_compare_fusion.1
  0.8 0.1 convert_reduce_fusion.3
  0.9 0.7 broadcast_select_fusion
  1.6 0.7 select_reduce_fusion.2
  2.3 0.7 broadcast_compare_fusion
  3.0 0.1 convert_reduce_fusion.2
  3.1 0.9 convert_reduce_fusion.1
  4.0 0.7 fusion.6
  4.7 1.5 select_reduce_fusion
  6.2 0.1 select_reduce_fusion.1
  6.3 0.5 convert_reduce_fusion
  6.9 0.2 copy.25
  7.1 0.1 select_reduce_fusion.3.branch_id_ref
  7.2 0.1 fusion.5.local_ref
  7.4 1.3 pad.4.routes_ref
  8.6 13.6 %gather_queries.1 = (bf16[4,2,128,512]{3,2,1,0:T(8,128)(2,1)}, s32[4,2,8,128]{3,2,1,0:T(8,128)}) custom-call(bf16[128,4096]{1,0:T(8,128)(2,1)} %query_hbm.1, s32[8,128]{1,0:T(8,128)} %pad.4.routes_ref), custom_call_target="tpu_custom_call" | custom-call | tf_op jit(solution)/shard_map/gather_queries/pallas_call | solution.py:495
  22.2 0.8 copy.26.branch_pages_ref
  23.0 1.9 %copy-done.1 = bf16[2,96,1,64,128]{4,3,2,1,0:T(8,128)(2,1)S(1)} copy-done((bf16[2,96,1,64,128]{4,3,2,1,0:T(8,128)(2,1)S(1)}, bf16[2,96,1,64,128]{4,3,2,1,0:T(8,128)(2,1)}, u32[]{:S(2)}) %copy-start.1) | copy-done | bytes 3145752
  24.9 1.2 copy-done.3
  26.1 0.7 copy-done.8
  26.8 0.7 copy-done.9
  27.5 0.7 copy-done.10
  28.1 18.4 %node_partials.1 = (bf16[8,128,512]{2,1,0:T(8,128)(2,1)S(1)}, f32[8,8,128]{2,1,0:T(8,128)S(1)}) custom-call(s32[2]{0:T(128)S(1)} %fusion.5.local_ref, s32[8]{0:T(128)S(1)} %select_reduce_fusion.3.branch_id_ref, s32[16,32]{1,0:T(8,128)S(1)} %copy-done.8, s32[64,4]{1,0:T(8,128)S(1)} %copy.26.branch_pages_ref, s32[16]{0:T(128)S(1)} %copy-done.9, ...), custom_call_target="tpu_custom_call" | custom-call | tf_op jit(solution)/shard_map/node_partials/pallas_call | solution.py:653
  46.5 0.0 copy-done
  46.5 0.0 copy-done.11
  46.5 0.0 copy-start.12
  46.5 41.7 %attend.1 = (f32[128,256]{1,0:T(8,128)S(1)}, bf16[2,128,128]{2,1,0:T(8,128)(2,1)S(1)}) custom-call(bf16[4,2,128,512]{3,2,1,0:T(8,128)(2,1)S(1)} %bitcast.19, f32[4,2,8,128]{3,2,1,0:T(8,128)S(1)} %bitcast.21, bf16[128,4096]{1,0:T(8,128)(2,1)S(1)} %copy-done, bf16[2,128,1,64,128]{4,3,2,1,0:T(8,128)(2,1)} %leaf_hbm.1, s32[1,128]{1,0:T(1,128)S(1)} %bitcast.22, ...), custom_call_target="tpu_custom_call" | custom-call | tf_op jit(solution)/shard_map/attend/pallas_call | solution.py:846
  88.2 0.6 copy-done.5
  88.9 0.6 copy-done.7
  89.5 1.3 copy.27.router_ref
  90.8 79.0 %run_experts.1 = bf16[128,256]{1,0:T(8,128)(2,1)} custom-call(bf16[2,128,128]{2,1,0:T(8,128)(2,1)} %copy-done.7, f32[128,256]{1,0:T(8,128)} %copy-done.5, s32[4,2,8,128]{3,2,1,0:T(8,128)} %get-tuple-element.16.routes_ref, f32[16,1,256]{2,1,0:T(1,128)} %bitcast.25, bf16[4096,8]{1,0:T(8,128)(2,1)} %copy.27.router_ref, bf16[2,512,4096]{2,1,0:T(8,128)(2,1)} %bitcast.23, ...), custom_call_target="tpu_custom_call" | custom-call | tf_op jit(solution)/shard_map/run_experts/pallas_call | solution.py:404
  169.8 1.5 copy.29
  (20 shorter events, 0.1 us)
Async XLA Ops:
  0.0 46.5 %copy-start = (bf16[128,4096]{1,0:T(8,128)(2,1)S(1)}, bf16[128,4096]{1,0:T(8,128)(2,1)}, u32[]{:S(2)}) copy-start(bf16[128,4096]{1,0:T(8,128)(2,1)} %query_hbm.1) | copy-start | bytes 3145732
  0.0 46.5 %copy-start.11 = (s32[128]{0:T(128)S(1)}, s32[128]{0:T(128)}, u32[]{:S(2)}) copy-start(s32[128]{0:T(128)} %param.40) | copy-start | bytes 1540
  0.0 46.5 %copy-start.4 = (bf16[2,128,1024]{2,1,0:T(8,128)(2,1)S(1)}, bf16[2,128,1024]{2,1,0:T(8,128)(2,1)}, u32[]{:S(2)}) copy-start(bf16[2,128,1024]{2,1,0:T(8,128)(2,1)} %fresh_hbm.1) | copy-start | bytes 1572868
  0.0 46.5 %copy-start.6 = (bf16[128,256]{1,0:T(8,128)(2,1)S(1)}, bf16[128,256]{1,0:T(8,128)(2,1)}, u32[]{:S(2)}) copy-start(bf16[128,256]{1,0:T(8,128)(2,1)} %residual_ref.1) | copy-start | bytes 196612
  23.0 1.9 %copy-start.1 = (bf16[2,96,1,64,128]{4,3,2,1,0:T(8,128)(2,1)S(1)}, bf16[2,96,1,64,128]{4,3,2,1,0:T(8,128)(2,1)}, u32[]{:S(2)}) copy-start(bf16[2,96,1,64,128]{4,3,2,1,0:T(8,128)(2,1)} %param.29) | copy-start | bytes 9437188
  24.9 1.2 copy-start.3
  26.1 0.7 copy-start.8
  26.8 0.7 copy-start.9
  27.4 0.7 copy-start.10
  28.1 18.4 %copy-start.2 = (bf16[256,4096]{1,0:T(8,128)(2,1)S(1)}, bf16[256,4096]{1,0:T(8,128)(2,1)}, u32[]{:S(2)}) copy-start(bf16[256,4096]{1,0:T(8,128)(2,1)} %weight_hbm.1) | copy-start | bytes 6291460
  46.5 43.0 %copy-start.12 = (bf16[4096,8]{0,1:T(8,128)(2,1)S(1)}, bf16[4096,8]{0,1:T(8,128)(2,1)}, u32[]{:S(2)}) copy-start(bf16[4096,8]{0,1:T(8,128)(2,1)} %param.26) | copy-start | bytes 196612
  88.2 0.6 copy-start.5
  88.9 0.6 copy-start.7

commit v4 on v3

--- a/solution.py
+++ b/solution.py
@@ -230,17 +230,13 @@
 
 
 def expert_kernel(
-    own_ref, kept_ref, routes_ref, gain_ref, router_ref, up_hbm, down_hbm,
-    out_ref,
+    at, loads, tables_in,
+    out_ref, kept_ref, own_ref,
+    routes_ref, gain_ref, router_ref,
     buf_ref, code_ref, other_ref, rows_ref, gate_ref, up_ref, down_ref, act_ref, give_ref, theirs_ref, sum_ref,
     half0, full0, full1, full2,
-    local_sem, up_sem, down_sem, send_sem, recv_sem,
+    local_sem, send_sem, recv_sem,
 ):
-    at = place()
-    loads = [pltpu.make_async_copy(up_hbm, up_ref, up_sem), pltpu.make_async_copy(down_hbm, down_ref, down_sem)]
-    for load in loads:
-        load.start()
-    greet(all_peers(at))
     link = Link(at, (send_sem, recv_sem))
     core = at["c"]
     mine = lax.axis_index("dp")
@@ -249,6 +245,8 @@
     upright = []
 
     def tables():
+        for load in tables_in:
+            load.wait()
         unit = (row_index == lane_index).astype(BF)
         later = (row_index < lane_index).astype(BF)
         earlier = (lane_index < row_index).astype(BF)
@@ -313,7 +311,9 @@
             return 0
 
         lax.fori_loop(0, 4, norm, 0)
-        logits = jnp.dot(rows_ref[pl.ds(base, 256), :], router_ref[...], preferred_element_type=F32)
+        logits = lax.dot_general(
+            rows_ref[pl.ds(base, 256), :], router_ref[...], BY_ROW, preferred_element_type=F32
+        )
         lane = lax.broadcasted_iota(jnp.int32, logits.shape, 1)
         here = jnp.sum(jnp.where(lane == mine, logits, 0.0), axis=1, keepdims=True)
         there = jnp.sum(
@@ -398,47 +398,54 @@
     link.finish()
 
 
-def run_experts(own, kept, routes, gain, router, expert_in, expert_out):
-    keys = GATHER_KEYS + 4 + 36
-    vmem, hbm = pl.BlockSpec(memory_space=pltpu.VMEM), pl.BlockSpec(memory_space=pl.ANY)
-    return pl.pallas_call(
-        expert_kernel,
-        out_shape=jax.ShapeDtypeStruct((ROWS, 256), BF),
-        in_specs=[vmem] * 5 + [hbm] * 2,
-        out_specs=vmem,
-        scratch_shapes=[
-            pltpu.VMEM((4, 2, 4, 4, 2, ROWS, 128), BF),
-            pltpu.VMEM((8, ROWS), jnp.int32),
-            pltpu.VMEM((8, ROWS), jnp.int32),
-            pltpu.VMEM((512, 4096), BF),
-            pltpu.VMEM((512, 128), F32),
-            pltpu.VMEM(expert_in.shape, BF),
-            pltpu.VMEM(expert_out.shape, BF),
-            pltpu.VMEM((512, 512), BF),
-            pltpu.VMEM((16, 256, 256), BF),
-            pltpu.VMEM((16, 256, 256), BF),
-            pltpu.VMEM((4, 4, 4, 2, ROWS, 128), BF),
-            pltpu.VMEM((2, 4, 4, ROWS, 128), BF),
-            pltpu.VMEM((2, 4, 4, 2, ROWS, 128), BF),
-            pltpu.VMEM((3, 4, 2, ROWS, 128), BF),
-            pltpu.VMEM((3, 2, ROWS, 128), BF),
-            pltpu.SemaphoreType.DMA,
-            pltpu.SemaphoreType.DMA,
-            pltpu.SemaphoreType.DMA,
-            pltpu.SemaphoreType.DMA((keys,)),
-            pltpu.SemaphoreType.DMA((keys,)),
-        ],
-        compiler_params=pltpu.CompilerParams(
-            collective_id=1, has_side_effects=True, vmem_limit_bytes=60 * 2**20
-        ),
-        name="run_experts",
-    )(own, kept, routes, gain, router, expert_in, expert_out)
-
-
 LOG2E = 1.4426950408889634
 
 
-def query_kernel(queries_ref, routes_ref, all_ref, all_routes_ref, local_sem, route_sem, send_sem, recv_sem):
+def member_codes(request_ref, request_branch_ref, parent_ref, root_owner_ref, branch_owner_ref, code_ref, dp):
+    def grid(shape, dim):
+        return lax.broadcasted_iota(jnp.int32, shape, dim)
+
+    def wide(ref):
+        return jnp.broadcast_to(ref[...], (8, ref.shape[1]))
+
+    def stand(matrix, row):
+        return lax.dot_general(matrix.astype(BF), row.astype(BF), BY_ROW, preferred_element_type=F32)[:, 0:1]
+
+    roots, branches, slots = root_owner_ref.shape[1], parent_ref.shape[1], request_ref.shape[1]
+    square = (branches, branches)
+    unit = grid(square, 0) == grid(square, 1)
+    earlier = grid(square, 1) < grid(square, 0)
+    owned = (wide(branch_owner_ref) == dp).astype(F32)
+    branch_owned, branch_place = stand(unit, owned), stand(earlier, owned)
+    parent = stand(unit, wide(parent_ref).astype(F32)).astype(jnp.int32)
+    kid = jnp.sum(jnp.where((parent == parent_ref[...]) & earlier, 1.0, 0.0), axis=1, keepdims=True)
+    root_owned = (wide(root_owner_ref) == dp).astype(F32)
+    before = grid((roots, roots), 0) < grid((roots, roots), 1)
+    root_place = jnp.dot(root_owned.astype(BF), before.astype(BF), preferred_element_type=F32)
+    chosen = parent == grid((branches, roots), 1)
+    parent_place = jnp.sum(jnp.where(chosen, root_place[0:1], 0.0), axis=1, keepdims=True)
+    parent_owned = jnp.sum(jnp.where(chosen, root_owned[0:1], 0.0), axis=1, keepdims=True)
+    root_base = jnp.where(parent_owned > 0.5, parent_place * ROWS + kid * BR_CAP, -4096.0)
+    branch_base = jnp.where(branch_owned > 0.5, branch_place * BR_CAP, -4096.0)
+    branch_row = wide(request_branch_ref).astype(F32).astype(BF)
+    later = (grid((ROWS, ROWS), 0) < grid((ROWS, ROWS), 1)).astype(BF)
+    count = jnp.zeros((branches, 1), F32)
+    for block in range(slots // ROWS):
+        span = slice(block * ROWS, (block + 1) * ROWS)
+        asked = (grid((slots, ROWS), 0) == request_ref[0:1, span]).astype(BF)
+        branch = jnp.dot(branch_row, asked, preferred_element_type=F32).astype(jnp.int32)[0:1]
+        member = grid((branches, ROWS), 0) == branch
+        rank = jnp.dot(member.astype(BF), later, preferred_element_type=F32) + count
+        count += jnp.sum(jnp.where(member, 1.0, 0.0), axis=1, keepdims=True)
+        for kind, base in enumerate((root_base, branch_base)):
+            code = jnp.sum(jnp.where(member, base + rank, 0.0), axis=0, keepdims=True)
+            code_ref[kind : kind + 1, span] = jnp.maximum(code, -1.0).astype(jnp.int32)
+
+
+def query_kernel(
+    queries_ref, routes_ref, request_ref, request_branch_ref, parent_ref, root_owner_ref, branch_owner_ref,
+    all_ref, all_routes_ref, code_ref, local_sem, route_sem, send_sem, recv_sem,
+):
     at = place()
     link = Link(at, (send_sem, recv_sem))
     sibling = link.sibling
@@ -460,6 +467,10 @@
         copy.start()
     for by, device in peers:
         link.send(routes_ref, all_routes_ref.at[x, core], 8 + by, device)
+    code_ref[...] = jnp.full_like(code_ref, -1)
+    member_codes(
+        request_ref, request_branch_ref, parent_ref, root_owner_ref, branch_owner_ref, code_ref, lax.axis_index("dp")
+    )
     low, high, far = (x + 3) % 4, (x + 1) % 4, (x + 2) % 4
     upper, lower = pl.ds(0, 64), pl.ds(64, 64)
     from_low, from_high = all_ref.at[low, core], all_ref.at[high, core]
@@ -491,15 +502,16 @@
     link.finish()
 
 
-def gather_queries(queries, routes):
+def gather_queries(queries, routes, *tables):
     return pl.pallas_call(
         query_kernel,
         out_shape=(
             jax.ShapeDtypeStruct((4, 2, ROWS, 512), BF),
-            jax.ShapeDtypeStruct((4, 2, 8, ROWS), jnp.int32),
+            jax.ShapeDtypeStruct((4, 2, 2, ROWS), jnp.int32),
+            jax.ShapeDtypeStruct((8, 1024), jnp.int32),
         ),
-        in_specs=[pl.BlockSpec(memory_space=pl.ANY)] * 2,
-        out_specs=(pl.BlockSpec(memory_space=pl.ANY),) * 2,
+        in_specs=[pl.BlockSpec(memory_space=pl.ANY)] * 2 + [pl.BlockSpec(memory_space=pltpu.VMEM)] * 5,
+        out_specs=(pl.BlockSpec(memory_space=pl.ANY),) * 2 + (pl.BlockSpec(memory_space=pltpu.VMEM),),
         scratch_shapes=[
             pltpu.SemaphoreType.DMA,
             pltpu.SemaphoreType.DMA,
@@ -508,21 +520,44 @@
         ],
         compiler_params=pltpu.CompilerParams(collective_id=3, has_side_effects=True),
         name="gather_queries",
-    )(queries, routes)
-
-
+    )(queries, routes, *(table[None, :] for table in tables))
+
+
+HEAD_STEPS = 2
 SCALE2 = LOG2E * 128 ** (-0.5)
 BY_ROW = (((1,), (1,)), ((), ()))
 
 
 def node_kernel(
-    local_ref, branch_id_ref, root_pages_ref, branch_pages_ref, root_len_ref, branch_len_ref, part_ref,
-    all_ref, pages_ref, code_row_ref, code_col_ref,
+    root_owner_ref, branch_owner_ref, root_pages_ref, branch_pages_ref, root_len_ref, branch_len_ref,
+    all_hbm, pages_hbm, code_row_ref,
     sum_ref, stat_ref,
-    query_ref, acc_ref, max_ref, total_ref, node_sum_ref, node_stat_ref,
+    query_ref, acc_ref, max_ref, total_ref, node_sum_ref, node_stat_ref, all_ref, pages_ref,
+    root_id_ref, branch_id_ref, load_sem,
 ):
-    part = part_ref[0]
+    loads = [
+        pltpu.make_async_copy(all_hbm, all_ref, load_sem.at[0]),
+        pltpu.make_async_copy(pages_hbm, pages_ref, load_sem.at[1]),
+    ]
+    for load in loads:
+        load.start()
+    dp = lax.axis_index("dp")
+    part = lax.axis_index("mp") % 2
     lane = lax.broadcasted_iota(jnp.int32, (1, 128), 1)
+    for owner_ref, id_ref in ((root_owner_ref, root_id_ref), (branch_owner_ref, branch_id_ref)):
+
+        def scan(i, found):
+            owned = owner_ref[i] == dp
+
+            @pl.when(owned)
+            def _():
+                id_ref[found] = i
+
+            return found + owned.astype(jnp.int32)
+
+        lax.fori_loop(0, owner_ref.shape[0], scan, 0)
+    loads[0].wait()
+    loads[1].wait()
 
     def pick(kind, base, count):
         wanted = lax.broadcasted_iota(jnp.int32, (count, 1024), 0) + base
@@ -540,7 +575,7 @@
 
     chunk = 8
     for k in range(ROOT_DEV):
-        root = local_ref[k]
+        root = root_id_ref[k]
         length = root_len_ref[root]
         picked = pick(0, k * 128, 128)
         for h in range(4):
@@ -558,20 +593,19 @@
             spot = lax.broadcasted_iota(jnp.int32, (1, chunk * 64), 1)
             spot = (i * chunk + spot // 64) * PAGE + part * 64 + spot % 64
             usable = spot < length
-            for h in range(4):
-                span = pl.ds(h * 128, 128)
+            for h in range(HEAD_STEPS):
+                span = pl.ds(h * (512 // HEAD_STEPS), 512 // HEAD_STEPS)
                 scores = lax.dot_general(query_ref[span, :], keys, BY_ROW, preferred_element_type=F32)
                 scores = jnp.where(usable, scores * SCALE2, MASKED_SCORE)
-                old = max_ref[span, 0:1]
+                old = max_ref[span, :]
                 new = jnp.maximum(old, jnp.max(scores, axis=1, keepdims=True))
-                weights = jnp.where(usable, jnp.exp2(scores - new), 0.0)
+                weights = jnp.exp2(scores - new[:, 0:1])
                 fade = jnp.exp2(old - new)
-                total = total_ref[span, 0:1] * fade + jnp.sum(weights, axis=1, keepdims=True)
+                total_ref[span, :] = total_ref[span, :] * fade + jnp.sum(weights, axis=1, keepdims=True)
                 acc_ref[span, :] = acc_ref[span, :] * fade + jnp.dot(
                     weights.astype(BF), values, preferred_element_type=F32
                 )
-                max_ref[span, :] = jnp.broadcast_to(new, (128, 128))
-                total_ref[span, :] = jnp.broadcast_to(total, (128, 128))
+                max_ref[span, :] = new
             return 0
 
         lax.fori_loop(0, steps, body, 0)
@@ -582,7 +616,7 @@
         length = branch_len_ref[branch]
         picked = pick(1, b * 32, 32)
         stacked = jnp.concatenate([picked[:, h * 128 : (h + 1) * 128] for h in range(4)], axis=0)
-        ids = [branch_pages_ref[branch, j] for j in range(4)]
+        ids = [branch_pages_ref[j, branch] for j in range(4)]
         keys = jnp.concatenate([pages_ref[0, page] for page in ids], axis=0)
         values = jnp.concatenate([pages_ref[1, page] for page in ids], axis=0)
         spot = lax.broadcasted_iota(jnp.int32, (1, 256), 1)
@@ -605,11 +639,16 @@
 
     lax.fori_loop(0, BR_DEV, branch_body, 0)
 
+    unit = lax.broadcasted_iota(jnp.int32, (ROWS, ROWS), 0) == lax.broadcasted_iota(jnp.int32, (ROWS, ROWS), 1)
+    unit = unit.astype(BF)
+
     def spread_body(block, _):
         parts = []
         wanted = lax.broadcasted_iota(jnp.int32, (ROWS, 256), 1)
+        row = code_row_ref[:, pl.ds(pl.multiple_of(block * ROWS, ROWS), ROWS)].astype(F32).astype(BF)
+        codes = lax.dot_general(unit, row, BY_ROW, preferred_element_type=F32).astype(jnp.int32)
         for kind in range(2):
-            code = code_col_ref[block, :, kind : kind + 1]
+            code = codes[:, kind : kind + 1]
             chosen = wanted == code
             rows = slice(kind * 256, kind * 256 + 256)
             sums = jnp.dot(chosen.astype(BF), node_sum_ref[rows, :], preferred_element_type=F32)
@@ -649,15 +688,16 @@
     return jnp.concatenate(pieces, axis=1), stats
 
 
-def node_partials(local_roots, local_branches, tables, part, all_queries, pages, codes):
+def node_partials(tables, all_queries, pages, codes):
+    vmem, hbm = pl.BlockSpec(memory_space=pltpu.VMEM), pl.BlockSpec(memory_space=pl.ANY)
     return pl.pallas_call(
         node_kernel,
         out_shape=(
             jax.ShapeDtypeStruct((8, ROWS, 512), BF),
             jax.ShapeDtypeStruct((8, 8, ROWS), F32),
         ),
-        in_specs=[pl.BlockSpec(memory_space=pltpu.SMEM)] * 7 + [pl.BlockSpec(memory_space=pltpu.VMEM)] * 4,
-        out_specs=(pl.BlockSpec(memory_space=pltpu.VMEM),) * 2,
+        in_specs=[pl.BlockSpec(memory_space=pltpu.SMEM)] * 6 + [hbm, hbm, vmem],
+        out_specs=(vmem, vmem),
         scratch_shapes=[
             pltpu.VMEM((512, 128), BF),
             pltpu.VMEM((512, 128), F32),
@@ -665,13 +705,19 @@
             pltpu.VMEM((512, 128), F32),
             pltpu.VMEM((512, 512), BF),
             pltpu.VMEM((512, 128), F32),
+            pltpu.VMEM(all_queries.shape, BF),
+            pltpu.VMEM(pages.shape, BF),
+            pltpu.SMEM((ROOT_DEV,), jnp.int32),
+            pltpu.SMEM((BR_DEV,), jnp.int32),
+            pltpu.SemaphoreType.DMA((2,)),
         ],
-        compiler_params=pltpu.CompilerParams(vmem_limit_bytes=40 * 2**20),
+        compiler_params=pltpu.CompilerParams(vmem_limit_bytes=62 * 2**20),
         name="node_partials",
-    )(local_roots, local_branches, *tables, part, all_queries, pages, codes, codes.T.reshape(8, ROWS, 2))
+    )(*tables, all_queries, pages, codes)
 
 
 def attend_kernel(
+    at, begin,
     sum_hbm, stat_hbm, query_hbm, leaf_hbm, leaf_len_ref, fresh_hbm, weight_hbm, residual_ref,
     hidden_ref, narrow_ref,
     own_sum, own_stat, their_sum, their_stat, run_sum, run_stat, land_sum, land_stat,
@@ -679,7 +725,6 @@
     leaf_sum, leaf_stat, give_stat, side_sum, side_stat, give_sum,
     proj_ref, full1, full2, load_sem, send_sem, recv_sem,
 ):
-    at = place()
     link = Link(at, (send_sem, recv_sem))
     send, arrive, sibling = link.send, link.arrive, link.sibling
     beside = {**at, "z": at["z"] + 1 - 2 * (at["z"] % 2)}
@@ -725,6 +770,7 @@
 
     loads[0].wait()
     loads[1].wait()
+    begin()
     wide_query[...] = query_ref[...].astype(F32)
 
     def leaf_group(base):
@@ -841,16 +887,41 @@
     link.finish()
 
 
-def attend(sums, stats, queries, leaf, leaf_len, fresh, out_weight, residual):
+def layer_kernel(*refs):
+    ins, out_ref = refs[:13], refs[13]
+    attend_refs = refs[14 : 14 + ATTEND_SCRATCH]
+    hidden_ref, narrow_ref, tables_sem, weight_sem = refs[14 + ATTEND_SCRATCH : 18 + ATTEND_SCRATCH]
+    expert_refs = refs[18 + ATTEND_SCRATCH :]
+    at = place()
+    tables = [
+        pltpu.make_async_copy(ins[8 + i], expert_refs[i], tables_sem.at[i]) for i in range(3)
+    ]
+    loads = [
+        pltpu.make_async_copy(ins[11 + i], expert_refs[EXPERT_WEIGHTS + i], weight_sem.at[i]) for i in range(2)
+    ]
+
+    def begin():
+        for load in tables + loads:
+            load.start()
+
+    attend_kernel(at, begin, *ins[:8], hidden_ref, narrow_ref, *attend_refs)
+    expert_kernel(at, loads, tables, out_ref, hidden_ref, narrow_ref, *expert_refs)
+
+
+ATTEND_SCRATCH = 27
+EXPERT_WEIGHTS = 8
+
+
+def attend_and_route(
+    sums, stats, queries, leaf, leaf_len, fresh, out_weight, residual, routes, gain, router, expert_in, expert_out
+):
+    keys = GATHER_KEYS + 4 + 36
     vmem, hbm = pl.BlockSpec(memory_space=pltpu.VMEM), pl.BlockSpec(memory_space=pl.ANY)
     return pl.pallas_call(
-        attend_kernel,
-        out_shape=(
-            jax.ShapeDtypeStruct((ROWS, 256), F32),
-            jax.ShapeDtypeStruct((2, ROWS, 128), BF),
-        ),
-        in_specs=[hbm, hbm, hbm, hbm, vmem, hbm, hbm, vmem],
-        out_specs=(vmem, vmem),
+        layer_kernel,
+        out_shape=jax.ShapeDtypeStruct((ROWS, 256), BF),
+        in_specs=[hbm, hbm, hbm, hbm, vmem, hbm, hbm, vmem] + [hbm] * 5,
+        out_specs=vmem,
         scratch_shapes=[
             pltpu.VMEM((4, ROWS, 512), BF),
             pltpu.VMEM((4, 8, ROWS), F32),
@@ -879,48 +950,37 @@
             pltpu.SemaphoreType.DMA((8,)),
             pltpu.SemaphoreType.DMA((28,)),
             pltpu.SemaphoreType.DMA((28,)),
+            pltpu.VMEM((ROWS, 256), F32),
+            pltpu.VMEM((2, ROWS, 128), BF),
+            pltpu.SemaphoreType.DMA((3,)),
+            pltpu.SemaphoreType.DMA((2,)),
+            pltpu.VMEM(routes.shape, jnp.int32),
+            pltpu.VMEM(gain.shape, F32),
+            pltpu.VMEM(router.shape, BF),
+            pltpu.VMEM((4, 2, 4, 4, 2, ROWS, 128), BF),
+            pltpu.VMEM((8, ROWS), jnp.int32),
+            pltpu.VMEM((8, ROWS), jnp.int32),
+            pltpu.VMEM((512, 4096), BF),
+            pltpu.VMEM((512, 128), F32),
+            pltpu.VMEM(expert_in.shape, BF),
+            pltpu.VMEM(expert_out.shape, BF),
+            pltpu.VMEM((512, 512), BF),
+            pltpu.VMEM((16, 256, 256), BF),
+            pltpu.VMEM((16, 256, 256), BF),
+            pltpu.VMEM((4, 4, 4, 2, ROWS, 128), BF),
+            pltpu.VMEM((2, 4, 4, ROWS, 128), BF),
+            pltpu.VMEM((2, 4, 4, 2, ROWS, 128), BF),
+            pltpu.VMEM((3, 4, 2, ROWS, 128), BF),
+            pltpu.VMEM((3, 2, ROWS, 128), BF),
+            pltpu.SemaphoreType.DMA,
+            pltpu.SemaphoreType.DMA((keys,)),
+            pltpu.SemaphoreType.DMA((keys,)),
         ],
         compiler_params=pltpu.CompilerParams(
-            collective_id=4, has_side_effects=True, vmem_limit_bytes=48 * 2**20
+            collective_id=1, has_side_effects=True, vmem_limit_bytes=62 * 2**20
         ),
-        name="attend",
-    )(sums, stats, queries, leaf, leaf_len, fresh, out_weight, residual)
-
-
-def owned_nodes(owner, dp_index, count):
-    node = jnp.arange(owner.shape[0])
-    owned = owner == dp_index
-    rank = jnp.sum((owned[None, :] & (node[None, :] < node[:, None])).astype(jnp.int32), axis=1)
-    chosen = owned[None, :] & (rank[None, :] == jnp.arange(count)[:, None])
-    return jnp.sum(jnp.where(chosen, node[None, :], 0), axis=1), jnp.where(owned, rank, -1)
-
-
-def slot_codes(slot_request, request_branch, branch_parent, root_place, branch_place):
-    slots = slot_request.shape[0]
-    slot = jnp.arange(slots)
-    slot_branch = jnp.sum(
-        jnp.where(slot_request[:, None] == slot[None, :], request_branch[None, :], 0), axis=1
-    )
-    rank = jnp.sum(
-        ((slot_branch[:, None] == slot_branch[None, :]) & (slot[None, :] < slot[:, None])).astype(jnp.int32),
-        axis=1,
-    )
-    branch = jnp.arange(branch_parent.shape[0])
-    kid = jnp.sum(
-        ((branch_parent[:, None] == branch_parent[None, :]) & (branch[None, :] < branch[:, None])).astype(
-            jnp.int32
-        ),
-        axis=1,
-    )
-    parent_place = jnp.sum(
-        jnp.where(branch_parent[:, None] == jnp.arange(root_place.shape[0])[None, :], root_place[None, :], 0),
-        axis=1,
-    )
-    root_base = jnp.where(parent_place >= 0, parent_place * ROWS + kid * BR_CAP, -4096)
-    branch_base = jnp.where(branch_place >= 0, branch_place * BR_CAP, -4096)
-    mine = slot_branch[None, :, None] == branch[None, None, :]
-    bases = jnp.sum(jnp.where(mine, jnp.stack([root_base, branch_base])[:, None, :], 0), axis=2)
-    return jnp.maximum(bases + rank[None, :], -1)
+        name="attend_and_route",
+    )(sums, stats, queries, leaf, leaf_len, fresh, out_weight, residual, routes, gain, router, expert_in, expert_out)
 
 
 def shards(
@@ -946,23 +1006,22 @@
     leaf_len,
     routes,
 ):
-    dp = lax.axis_index("dp")
-    mp = lax.axis_index("mp")
-    local_roots, root_place = owned_nodes(root_owner, dp, ROOT_DEV)
-    local_branches, branch_place = owned_nodes(branch_owner, dp, BR_DEV)
-    codes = slot_codes(slot_request, request_branch, branch_parent, root_place, branch_place)
-    all_queries, all_routes = gather_queries(queries, jnp.pad(routes.T, ((0, 6), (0, 0))))
-    all_queries = all_queries.reshape(8 * ROWS, 512)
+    all_queries, all_routes, codes = gather_queries(
+        queries,
+        routes.T,
+        slot_request,
+        request_branch,
+        branch_parent,
+        root_owner,
+        branch_owner,
+    )
     sums, stats = node_partials(
-        local_roots,
-        local_branches,
-        (root_pages, branch_pages, root_len, branch_len),
-        (mp % 2).reshape(1).astype(jnp.int32),
-        all_queries,
+        (root_owner, branch_owner, root_pages, branch_pages.T, root_len, branch_len),
+        all_queries.reshape(8 * ROWS, 512),
         node_cache[:, :, 0],
         codes,
     )
-    hidden, narrow = attend(
+    return attend_and_route(
         sums.reshape(4, 2, ROWS, 512),
         stats.reshape(4, 2, 8, ROWS),
         queries,
@@ -971,9 +1030,11 @@
         new_kv,
         out_weight,
         residual,
-    )
-    return run_experts(
-        narrow, hidden, all_routes, norm_gain.reshape(16, 1, 256), router, expert_in[0], expert_out[0]
+        all_routes,
+        norm_gain.reshape(16, 1, 256),
+        router.T,
+        expert_in[0],
+        expert_out[0],
     )
 
 

time: 172 us -> 157 us (0.913)
  local copies, waits for them, and re-layouts: 11.5 us -> 1.47 us
  other arithmetic: 7.08 us -> 0 us
  Pallas kernels: 153 us -> 155 us
    unnamed x29 -> x1, local copies, waits for them, and re-layouts: 9.99 us -> 1.47 us
    pallas_call x1, Pallas kernels: 18.4 us -> 22.8 us  [node_partials(): pl.pallas_call(node_kernel, out_shape=(jax.ShapeDtypeStruct((8, ROWS, 512...]
    reduce_sum x9 -> x0, other arithmetic: 4.24 us -> none  [the longest x1 1.46 us: slot_codes(): jnp.sum(jnp.where(slot_request[:, None] == slot[None, :], request_branch[...]
    pallas_call x2 -> x1, Pallas kernels: 121 us -> 117 us  [attend_and_route(): pl.pallas_call(layer_kernel, out_shape=jax.ShapeDtypeStruct((ROWS, 256),...]
where the time goes in v4:
time: 157 us
  Pallas kernels  155 us (99%)
    pallas_call x1, Pallas kernels, attend_and_route(): pl.pallas_call(layer_kernel, out_shape=jax.ShapeDtypeStruct((ROWS, 256),...  117 us
    pallas_call x1, Pallas kernels, node_partials(): pl.pallas_call(node_kernel, out_shape=(jax.ShapeDtypeStruct((8, ROWS, 512...  22.8 us
    pallas_call x1, Pallas kernels, gather_queries(): pl.pallas_call(query_kernel, out_shape=(jax.ShapeDtypeStruct((4, 2, ROWS,...  14.7 us

profile of v4, /device:TPU:0, one launch (start us, length us, event | category | flops | bytes accessed | tf_op | source)
XLA Modules:
  0.0 156.5 jit_solution(17237481598784464041)
XLA Ops:
  0.0 14.7 %gather_queries.1 = (bf16[4,2,128,512]{3,2,1,0:T(8,128)(2,1)}, s32[4,2,2,128]{3,2,1,0:T(2,128)}, s32[8,1024]{1,0:T(8,128)}) custom-call(bf16[128,4096]{1,0:T(8,128)(2,1)} %refs_2_.1, s32[2,128]{1,0:T(2,128)} %bitcast.29, s32[1,1024]{1,0:T(1,128)} %bitcast.24, s32[1,1024]{1,0:T(1,128)} %bitcast.25, s32[1,64]{1,0:T(1,128)} %bitcast.31, s32[1,16]{1,0:T(1,128)} %bitcast.27, ...), custom_call_target="tpu_custom_call" | custom-call | tf_op jit(solution)/shard_map/gather_queries/pallas_call | solution.py:506
  14.8 22.8 %node_partials.1 = (bf16[8,128,512]{2,1,0:T(8,128)(2,1)}, f32[8,8,128]{2,1,0:T(8,128)}) custom-call(s32[16]{0:T(128)} %root_owner_ref.1, s32[64]{0:T(128)} %branch_owner_ref.1, s32[16,32]{1,0:T(8,128)} %root_pages_ref.1, s32[4,64]{1,0:T(4,128)} %bitcast.26, s32[16]{0:T(128)} %root_len_ref.1, s32[64]{0:T(128)} %branch_len_ref.1, bf16[1024,512]{1,0:T(8,128)(2,1)} %bitcast.19, ...), custom_call_target="tpu_custom_call" | custom-call | tf_op jit(solution)/shard_map/node_partials/pallas_call | solution.py:693
  37.6 117.5 %attend_and_route.1 = bf16[128,256]{1,0:T(8,128)(2,1)} custom-call(bf16[4,2,128,512]{3,2,1,0:T(8,128)(2,1)} %bitcast.20, f32[4,2,8,128]{3,2,1,0:T(8,128)} %bitcast.22, bf16[128,4096]{1,0:T(8,128)(2,1)} %refs_2_.1, bf16[2,128,1,64,128]{4,3,2,1,0:T(8,128)(2,1)} %refs_3_.1, s32[1,128]{1,0:T(1,128)} %bitcast.30, bf16[2,128,1024]{2,1,0:T(8,128)(2,1)} %refs_5_.1, ...), custom_call_target="tpu_custom_call" | custom-call | tf_op jit(solution)/shard_map/attend_and_route/pallas_call | solution.py:920
  155.1 1.5 copy.23

commit v5 on v4

--- a/solution.py
+++ b/solution.py
@@ -324,19 +324,25 @@
         there = jnp.exp(there - most)
         gate_ref[pl.ds(base, 256), :] = jnp.broadcast_to(here / (here + there), (256, 128))
 
+    def activate(plane):
+        base = pl.multiple_of(plane * 256, 256)
+        for j in range(2):
+            span = slice(j * 256, (j + 1) * 256)
+            gate, up = [
+                lax.dot_general(
+                    rows_ref[pl.ds(base, 256), :], up_ref[k, span, :], BY_ROW, preferred_element_type=F32
+                )
+                for k in range(2)
+            ]
+            act_ref[pl.ds(base, 256), span] = (gate / (1.0 + jnp.exp(-gate)) * up).astype(BF)
+
     compact(core)
+    for load in loads:
+        load.wait()
+    activate(core)
     others()
     compact(1 - core)
-    for load in loads:
-        load.wait()
-
-    for j in range(2):
-        span = slice(j * 256, (j + 1) * 256)
-        gate, up = [
-            lax.dot_general(rows_ref[...], up_ref[k, span, :], BY_ROW, preferred_element_type=F32)
-            for k in range(2)
-        ]
-        act_ref[:, span] = (gate / (1.0 + jnp.exp(-gate)) * up).astype(BF)
+    activate(1 - core)
 
     def project(plane, i):
         base = pl.multiple_of(plane * 256, 256)
@@ -523,7 +529,7 @@
     )(queries, routes, *(table[None, :] for table in tables))
 
 
-HEAD_STEPS = 2
+HEAD_STEPS = 1
 SCALE2 = LOG2E * 128 ** (-0.5)
 BY_ROW = (((1,), (1,)), ((), ()))
 
@@ -532,7 +538,7 @@
     root_owner_ref, branch_owner_ref, root_pages_ref, branch_pages_ref, root_len_ref, branch_len_ref,
     all_hbm, pages_hbm, code_row_ref,
     sum_ref, stat_ref,
-    query_ref, acc_ref, max_ref, total_ref, node_sum_ref, node_stat_ref, all_ref, pages_ref,
+    query_ref, acc_ref, max_ref, total_ref, node_sum_ref, node_stat_ref, picked_ref, all_ref, pages_ref,
     root_id_ref, branch_id_ref, load_sem,
 ):
     loads = [
@@ -559,10 +565,18 @@
     loads[0].wait()
     loads[1].wait()
 
-    def pick(kind, base, count):
-        wanted = lax.broadcasted_iota(jnp.int32, (count, 1024), 0) + base
+    for kind in range(2):
+        wanted = lax.broadcasted_iota(jnp.int32, (256, 1024), 0)
         chosen = (wanted == code_row_ref[kind : kind + 1, :]).astype(BF)
-        return jnp.dot(chosen, all_ref[...], preferred_element_type=F32).astype(BF)
+        picked_ref[kind * 256 : kind * 256 + 256, :] = jnp.dot(
+            chosen, all_ref[...], preferred_element_type=F32
+        ).astype(BF)
+
+    def keep_stats(row, rows, stats):
+        for i in range(3):
+            piece = stats.astype(BF)
+            node_stat_ref[i, pl.ds(row, rows), :] = piece
+            stats = stats - piece.astype(F32)
 
     def put(row, rows):
         stats = jnp.zeros((rows, 128), F32)
@@ -571,15 +585,14 @@
             node_sum_ref[pl.ds(row, rows), h * 128 : (h + 1) * 128] = acc_ref[span, :].astype(BF)
             stats = jnp.where(lane == h, max_ref[span, 0:1], stats)
             stats = jnp.where(lane == 4 + h, total_ref[span, 0:1], stats)
-        node_stat_ref[pl.ds(row, rows), :] = stats
+        keep_stats(row, rows, stats)
 
     chunk = 8
     for k in range(ROOT_DEV):
         root = root_id_ref[k]
         length = root_len_ref[root]
-        picked = pick(0, k * 128, 128)
         for h in range(4):
-            query_ref[h * 128 : (h + 1) * 128, :] = picked[:, h * 128 : (h + 1) * 128]
+            query_ref[h * 128 : (h + 1) * 128, :] = picked_ref[k * 128 : (k + 1) * 128, h * 128 : (h + 1) * 128]
         acc_ref[...] = jnp.zeros_like(acc_ref)
         max_ref[...] = jnp.full_like(max_ref, MASKED_SCORE)
         total_ref[...] = jnp.zeros_like(total_ref)
@@ -611,10 +624,11 @@
         lax.fori_loop(0, steps, body, 0)
         put(k * 128, 128)
 
-    def branch_body(b, _):
+    def branch_work(b):
         branch = branch_id_ref[b]
         length = branch_len_ref[branch]
-        picked = pick(1, b * 32, 32)
+        row = pl.multiple_of(256 + b * 32, 32)
+        picked = picked_ref[pl.ds(row, 32), :]
         stacked = jnp.concatenate([picked[:, h * 128 : (h + 1) * 128] for h in range(4)], axis=0)
         ids = [branch_pages_ref[j, branch] for j in range(4)]
         keys = jnp.concatenate([pages_ref[0, page] for page in ids], axis=0)
@@ -628,21 +642,24 @@
         weights = jnp.where(usable, jnp.exp2(scores - top), 0.0)
         total = jnp.sum(weights, axis=1, keepdims=True)
         acc = jnp.dot(weights.astype(BF), values, preferred_element_type=F32)
-        row = pl.multiple_of(256 + b * 32, 32)
         stats = jnp.zeros((32, 128), F32)
         for h in range(4):
             node_sum_ref[pl.ds(row, 32), h * 128 : (h + 1) * 128] = acc[h * 32 : (h + 1) * 32].astype(BF)
             stats = jnp.where(lane == h, top[h * 32 : (h + 1) * 32], stats)
             stats = jnp.where(lane == 4 + h, total[h * 32 : (h + 1) * 32], stats)
-        node_stat_ref[pl.ds(row, 32), :] = stats
+        keep_stats(row, 32, stats)
+
+    def branch_body(i, _):
+        for k in range(4):
+            branch_work(i * 4 + k)
         return 0
 
-    lax.fori_loop(0, BR_DEV, branch_body, 0)
+    lax.fori_loop(0, BR_DEV // 4, branch_body, 0)
 
     unit = lax.broadcasted_iota(jnp.int32, (ROWS, ROWS), 0) == lax.broadcasted_iota(jnp.int32, (ROWS, ROWS), 1)
     unit = unit.astype(BF)
 
-    def spread_body(block, _):
+    def spread_work(block):
         parts = []
         wanted = lax.broadcasted_iota(jnp.int32, (ROWS, 256), 1)
         row = code_row_ref[:, pl.ds(pl.multiple_of(block * ROWS, ROWS), ROWS)].astype(F32).astype(BF)
@@ -652,39 +669,39 @@
             chosen = wanted == code
             rows = slice(kind * 256, kind * 256 + 256)
             sums = jnp.dot(chosen.astype(BF), node_sum_ref[rows, :], preferred_element_type=F32)
-            stats = jnp.dot(
-                chosen.astype(F32),
-                node_stat_ref[rows, :],
-                preferred_element_type=F32,
-                precision=lax.Precision.HIGHEST,
+            stats = sum(
+                jnp.dot(chosen.astype(BF), node_stat_ref[i, rows, :], preferred_element_type=F32)
+                for i in (2, 1, 0)
             )
             stats = jnp.where((lane < 4) & (code < 0), MASKED_SCORE, stats)
             parts.append((sums, stats))
         merged, stats = merge_blocks(parts[0], parts[1], 4)
         sum_ref[block] = merged.astype(BF)
         stat_ref[block] = stats.T[0:8]
+
+    def spread_body(i, _):
+        for k in range(2):
+            spread_work(i * 2 + k)
         return 0
 
-    lax.fori_loop(0, 8, spread_body, 0)
+    lax.fori_loop(0, 4, spread_body, 0)
 
 
 def merge_blocks(one, two, heads):
     sums_one, stats_one = one
     sums_two, stats_two = two
     lane = lax.broadcasted_iota(jnp.int32, (1, 128), 1)
+    top = jnp.maximum(stats_one, stats_two)
+    factor_one, factor_two = jnp.exp2(stats_one - top), jnp.exp2(stats_two - top)
+    total = stats_one * pltpu.roll(factor_one, 4, 1) + stats_two * pltpu.roll(factor_two, 4, 1)
+    stats = jnp.where(lane < 4, top, jnp.where(lane < 8, total, 0.0))
     pieces = []
-    stats = jnp.zeros_like(stats_one)
     for h in range(heads):
         span = slice(h * 128, (h + 1) * 128)
-        top_one, top_two = stats_one[:, h : h + 1], stats_two[:, h : h + 1]
-        top = jnp.maximum(top_one, top_two)
-        factor_one, factor_two = jnp.exp2(top_one - top), jnp.exp2(top_two - top)
         pieces.append(
-            sums_one[:, span].astype(F32) * factor_one + sums_two[:, span].astype(F32) * factor_two
+            sums_one[:, span].astype(F32) * factor_one[:, h : h + 1]
+            + sums_two[:, span].astype(F32) * factor_two[:, h : h + 1]
         )
-        total = stats_one[:, 4 + h : 5 + h] * factor_one + stats_two[:, 4 + h : 5 + h] * factor_two
-        stats = jnp.where(lane == h, top, stats)
-        stats = jnp.where(lane == 4 + h, total, stats)
     return jnp.concatenate(pieces, axis=1), stats
 
 
@@ -704,7 +721,8 @@
             pltpu.VMEM((512, 128), F32),
             pltpu.VMEM((512, 128), F32),
             pltpu.VMEM((512, 512), BF),
-            pltpu.VMEM((512, 128), F32),
+            pltpu.VMEM((3, 512, 128), BF),
+            pltpu.VMEM((512, 512), BF),
             pltpu.VMEM(all_queries.shape, BF),
             pltpu.VMEM(pages.shape, BF),
             pltpu.SMEM((ROOT_DEV,), jnp.int32),

time: 157 us -> 147 us (0.936)
  Pallas kernels: 155 us -> 145 us
    pallas_call x1, Pallas kernels: 22.8 us -> 16.8 us  [node_partials(): pl.pallas_call(node_kernel, out_shape=(jax.ShapeDtypeStruct((8, ROWS, 512...]
    pallas_call x1, Pallas kernels: 117 us -> 114 us  [attend_and_route(): pl.pallas_call(layer_kernel, out_shape=jax.ShapeDtypeStruct((ROWS, 256),...]
where the time goes in v5:
time: 147 us
  Pallas kernels  145 us (99%)
  local copies, waits for them, and re-layouts  1.47 us (1%)
    pallas_call x1, Pallas kernels, attend_and_route(): pl.pallas_call(layer_kernel, out_shape=jax.ShapeDtypeStruct((ROWS, 256),...  114 us
    pallas_call x1, Pallas kernels, node_partials(): pl.pallas_call(node_kernel, out_shape=(jax.ShapeDtypeStruct((8, ROWS, 512...  16.8 us
    pallas_call x1, Pallas kernels, gather_queries(): pl.pallas_call(query_kernel, out_shape=(jax.ShapeDtypeStruct((4, 2, ROWS,...  14.7 us

profile of v5, /device:TPU:0, one launch (start us, length us, event | category | flops | bytes accessed | tf_op | source)
XLA Modules:
  0.0 146.6 jit_solution(6782560127507031428)
XLA Ops:
  0.0 14.7 %gather_queries.1 = (bf16[4,2,128,512]{3,2,1,0:T(8,128)(2,1)}, s32[4,2,2,128]{3,2,1,0:T(2,128)}, s32[8,1024]{1,0:T(8,128)}) custom-call(bf16[128,4096]{1,0:T(8,128)(2,1)} %refs_2_.1, s32[2,128]{1,0:T(2,128)} %bitcast.29, s32[1,1024]{1,0:T(1,128)} %bitcast.24, s32[1,1024]{1,0:T(1,128)} %bitcast.25, s32[1,64]{1,0:T(1,128)} %bitcast.31, s32[1,16]{1,0:T(1,128)} %bitcast.27, ...), custom_call_target="tpu_custom_call" | custom-call | tf_op jit(solution)/shard_map/gather_queries/pallas_call | solution.py:512
  14.8 16.8 %node_partials.1 = (bf16[8,128,512]{2,1,0:T(8,128)(2,1)}, f32[8,8,128]{2,1,0:T(8,128)}) custom-call(s32[16]{0:T(128)} %root_owner_ref.1, s32[64]{0:T(128)} %branch_owner_ref.1, s32[16,32]{1,0:T(8,128)} %root_pages_ref.1, s32[4,64]{1,0:T(4,128)} %bitcast.26, s32[16]{0:T(128)} %root_len_ref.1, s32[64]{0:T(128)} %branch_len_ref.1, bf16[1024,512]{1,0:T(8,128)(2,1)} %bitcast.19, ...), custom_call_target="tpu_custom_call" | custom-call | tf_op jit(solution)/shard_map/node_partials/pallas_call | solution.py:710
  31.5 113.5 %attend_and_route.1 = bf16[128,256]{1,0:T(8,128)(2,1)} custom-call(bf16[4,2,128,512]{3,2,1,0:T(8,128)(2,1)} %bitcast.20, f32[4,2,8,128]{3,2,1,0:T(8,128)} %bitcast.22, bf16[128,4096]{1,0:T(8,128)(2,1)} %refs_2_.1, bf16[2,128,1,64,128]{4,3,2,1,0:T(8,128)(2,1)} %refs_3_.1, s32[1,128]{1,0:T(1,128)} %bitcast.30, bf16[2,128,1024]{2,1,0:T(8,128)(2,1)} %refs_5_.1, ...), custom_call_target="tpu_custom_call" | custom-call | tf_op jit(solution)/shard_map/attend_and_route/pallas_call | solution.py:938
  145.1 1.5 %copy.23 = bf16[128,256]{1,0:T(8,128)(2,1)} copy(bf16[128,256]{1,0:T(8,128)(2,1)} %attend_and_route.1) | data formatting | bytes 131072

commit v6 on v5

--- a/solution.py
+++ b/solution.py
@@ -473,10 +473,6 @@
         copy.start()
     for by, device in peers:
         link.send(routes_ref, all_routes_ref.at[x, core], 8 + by, device)
-    code_ref[...] = jnp.full_like(code_ref, -1)
-    member_codes(
-        request_ref, request_branch_ref, parent_ref, root_owner_ref, branch_owner_ref, code_ref, lax.axis_index("dp")
-    )
     low, high, far = (x + 3) % 4, (x + 1) % 4, (x + 2) % 4
     upper, lower = pl.ds(0, 64), pl.ds(64, 64)
     from_low, from_high = all_ref.at[low, core], all_ref.at[high, core]
@@ -488,6 +484,10 @@
     link.send(second, second, 3, left)
     link.send(from_low, from_low, 5, sibling)
     link.send(from_high, from_high, 6, sibling)
+    code_ref[...] = jnp.full_like(code_ref, -1)
+    member_codes(
+        request_ref, request_branch_ref, parent_ref, root_owner_ref, branch_owner_ref, code_ref, lax.axis_index("dp")
+    )
     for key, rows in ((2, upper), (3, lower)):
         ref = all_ref.at[far, core, rows]
         link.arrive(ref, key)
@@ -680,11 +680,11 @@
         stat_ref[block] = stats.T[0:8]
 
     def spread_body(i, _):
-        for k in range(2):
-            spread_work(i * 2 + k)
+        for k in range(4):
+            spread_work(i * 4 + k)
         return 0
 
-    lax.fori_loop(0, 4, spread_body, 0)
+    lax.fori_loop(0, 2, spread_body, 0)
 
 
 def merge_blocks(one, two, heads):
@@ -786,11 +786,6 @@
     def upright(stats):
         return jnp.concatenate([stats, jnp.zeros((ROWS - 8, ROWS), F32)], axis=0).T
 
-    loads[0].wait()
-    loads[1].wait()
-    begin()
-    wide_query[...] = query_ref[...].astype(F32)
-
     def leaf_group(base):
         span = pl.ds(base, 8)
         heads = [wide_query[span, h * 128 : (h + 1) * 128] for h in range(4)]
@@ -821,7 +816,6 @@
             leaf_group(pl.multiple_of(i * 32 + k * 8, 8))
         return 0
 
-    lax.fori_loop(0, 4, leaf_body, 0)
     loads[2].wait()
     loads[3].wait()
     arrive(their_sum, 0)
@@ -836,6 +830,11 @@
         device = step_along(at, "x", by)
         send(run_sum.at[by - 1], land_sum.at[by - 1], 2 * by, device)
         send(run_stat.at[by - 1], land_stat.at[by - 1], 2 * by + 1, device)
+    loads[0].wait()
+    loads[1].wait()
+    begin()
+    wide_query[...] = query_ref[...].astype(F32)
+    lax.fori_loop(0, 4, leaf_body, 0)
     sums, stats = merge_blocks(
         (own_sum[x], upright(own_stat[x])), (their_sum[x], upright(their_stat[x])), 4
     )

time: 147 us -> 144 us (0.980)
  Pallas kernels: 145 us -> 142 us
    pallas_call x1, Pallas kernels: 114 us -> 111 us  [attend_and_route(): pl.pallas_call(layer_kernel, out_shape=jax.ShapeDtypeStruct((ROWS, 256),...]
where the time goes in v6:
time: 144 us
  Pallas kernels  142 us (99%)
  local copies, waits for them, and re-layouts  1.47 us (1%)
    pallas_call x1, Pallas kernels, attend_and_route(): pl.pallas_call(layer_kernel, out_shape=jax.ShapeDtypeStruct((ROWS, 256),...  111 us
    pallas_call x1, Pallas kernels, node_partials(): pl.pallas_call(node_kernel, out_shape=(jax.ShapeDtypeStruct((8, ROWS, 512...  16.5 us
    pallas_call x1, Pallas kernels, gather_queries(): pl.pallas_call(query_kernel, out_shape=(jax.ShapeDtypeStruct((4, 2, ROWS,...  14.7 us

profile of v6, /device:TPU:0, one launch (start us, length us, event | category | flops | bytes accessed | tf_op | source)
XLA Modules:
  0.0 143.7 jit_solution(17606960122549035516)
XLA Ops:
  0.0 14.7 %gather_queries.1 = (bf16[4,2,128,512]{3,2,1,0:T(8,128)(2,1)}, s32[4,2,2,128]{3,2,1,0:T(2,128)}, s32[8,1024]{1,0:T(8,128)}) custom-call(bf16[128,4096]{1,0:T(8,128)(2,1)} %refs_2_.1, s32[2,128]{1,0:T(2,128)} %bitcast.29, s32[1,1024]{1,0:T(1,128)} %bitcast.24, s32[1,1024]{1,0:T(1,128)} %bitcast.25, s32[1,64]{1,0:T(1,128)} %bitcast.31, s32[1,16]{1,0:T(1,128)} %bitcast.27, ...), custom_call_target="tpu_custom_call" | custom-call | tf_op jit(solution)/shard_map/gather_queries/pallas_call | solution.py:512
  14.8 16.5 %node_partials.1 = (bf16[8,128,512]{2,1,0:T(8,128)(2,1)}, f32[8,8,128]{2,1,0:T(8,128)}) custom-call(s32[16]{0:T(128)} %root_owner_ref.1, s32[64]{0:T(128)} %branch_owner_ref.1, s32[16,32]{1,0:T(8,128)} %root_pages_ref.1, s32[4,64]{1,0:T(4,128)} %bitcast.26, s32[16]{0:T(128)} %root_len_ref.1, s32[64]{0:T(128)} %branch_len_ref.1, bf16[1024,512]{1,0:T(8,128)(2,1)} %bitcast.19, ...), custom_call_target="tpu_custom_call" | custom-call | tf_op jit(solution)/shard_map/node_partials/pallas_call | solution.py:710
  31.3 111.0 %attend_and_route.1 = bf16[128,256]{1,0:T(8,128)(2,1)} custom-call(bf16[4,2,128,512]{3,2,1,0:T(8,128)(2,1)} %bitcast.20, f32[4,2,8,128]{3,2,1,0:T(8,128)} %bitcast.22, bf16[128,4096]{1,0:T(8,128)(2,1)} %refs_2_.1, bf16[2,128,1,64,128]{4,3,2,1,0:T(8,128)(2,1)} %refs_3_.1, s32[1,128]{1,0:T(1,128)} %bitcast.30, bf16[2,128,1024]{2,1,0:T(8,128)(2,1)} %refs_5_.1, ...), custom_call_target="tpu_custom_call" | custom-call | tf_op jit(solution)/shard_map/attend_and_route/pallas_call | solution.py:937
  142.3 1.5 %copy.23 = bf16[128,256]{1,0:T(8,128)(2,1)} copy(bf16[128,256]{1,0:T(8,128)(2,1)} %attend_and_route.1) | data formatting | bytes 131072

commit v7 on v6

--- a/solution.py
+++ b/solution.py
@@ -120,18 +120,27 @@
         axis = ORDERS[part][2]
         key = base + part * 8
         ref = slab(part, 2, at[axis], both, core)
-        link.send(ref, ref, key, step_along(at, axis, 1))
-        link.send(ref, ref, key + 1, step_along(at, axis, 3))
+        for side in range(2):
+            for late in range(2):
+                half = slab(part, 2, at[axis], side if late == 0 else 1 - side, core)
+                spare = base + 24 + part * 2 + side
+                link.send(half, half, spare if late else key + side, step_along(at, axis, 1 + 2 * side))
         link.send(ref, ref, key + 4, link.sibling)
     for part in range(3):
         axis = ORDERS[part][2]
         key = base + part * 8
         for side, by in ((0, 3), (1, 1)):
             value = (at[axis] + by) % 4
+            half = slab(part, 2, value, side, core)
+            link.arrive(half, key + side)
+            link.send(half, half, key + 2 + side, step_along(at, axis, 1 + 2 * side))
+    for part in range(3):
+        axis = ORDERS[part][2]
+        key = base + part * 8
+        for side, by in ((0, 3), (1, 1)):
+            value = (at[axis] + by) % 4
+            link.arrive(slab(part, 2, value, 1 - side, core), base + 24 + part * 2 + side)
             ref = slab(part, 2, value, both, core)
-            link.arrive(ref, key + side)
-            half = slab(part, 2, value, side, core)
-            link.send(half, half, key + 2 + side, step_along(at, axis, 1 + 2 * side))
             link.send(ref, ref, key + 5 + side, link.sibling)
     for part in range(3):
         axis = ORDERS[part][2]
@@ -151,7 +160,7 @@
     return others
 
 
-GATHER_KEYS = 18 + 24
+GATHER_KEYS = 18 + 30
 
 
 def ring_reduce(at, link, sum_ref, dims, orders, part_rows, relay, lands, base, finish):
@@ -190,6 +199,13 @@
                         keys[part] + side,
                         step_along(at, axis, by),
                     )
+                for side, by in ((0, 1), (1, 3)):
+                    link.send(
+                        sum_ref.at[view(part, phase, (at[axis] + by) % 4, 1 - side)],
+                        fulls.at[spot(part, phase, side, 1 - side)],
+                        base + 12 * phases + part * 2 + side,
+                        step_along(at, axis, by),
+                    )
             for part in parts:
                 axis = orders[part][phase]
                 for side, by in ((0, 1), (1, 3)):
@@ -198,8 +214,8 @@
                     target = view(part, phase, (at[axis] + by) % 4, side)
                     sum_ref[target] = accumulate(target, [(halves, index)]).astype(BF)
                     link.send(
-                        sum_ref.at[view(part, phase, (at[axis] + by) % 4, both)],
-                        fulls.at[spot(part, phase, side, both)],
+                        sum_ref.at[target],
+                        fulls.at[spot(part, phase, side, side)],
                         keys[part] + 2 + side,
                         step_along(at, axis, by),
                     )
@@ -219,7 +235,11 @@
         for part in parts:
             axis = orders[part][phase]
             for slot in range(slots):
-                link.arrive(fulls.at[spot(part, phase, slot, both)], keys[part] + first + slot)
+                if phase < relay:
+                    link.arrive(fulls.at[spot(part, phase, slot, 1 - slot)], base + 12 * phases + part * 2 + slot)
+                    link.arrive(fulls.at[spot(part, phase, slot, slot)], keys[part] + first + slot)
+                else:
+                    link.arrive(fulls.at[spot(part, phase, slot, both)], keys[part] + first + slot)
             for half in range(2):
                 target = view(part, phase, at[axis], half)
                 total = accumulate(target, [(fulls, spot(part, phase, slot, half)) for slot in range(slots)])
@@ -932,7 +952,7 @@
 def attend_and_route(
     sums, stats, queries, leaf, leaf_len, fresh, out_weight, residual, routes, gain, router, expert_in, expert_out
 ):
-    keys = GATHER_KEYS + 4 + 36
+    keys = GATHER_KEYS + 4 + 42
     vmem, hbm = pl.BlockSpec(memory_space=pltpu.VMEM), pl.BlockSpec(memory_space=pl.ANY)
     return pl.pallas_call(
         layer_kernel,

time: 144 us -> 141 us (0.979)
  Pallas kernels: 142 us -> 139 us
    pallas_call x1, Pallas kernels: 16.5 us -> 14.6 us  [node_partials(): pl.pallas_call(node_kernel, out_shape=(jax.ShapeDtypeStruct((8, ROWS, 512...]
    pallas_call x1, Pallas kernels: 111 us -> 109 us  [attend_and_route(): pl.pallas_call(layer_kernel, out_shape=jax.ShapeDtypeStruct((ROWS, 256),...]
where the time goes in v7:
time: 141 us; the launch traced here: 140 us
  Pallas kernels  139 us (99%)
  local copies, waits for them, and re-layouts  1.47 us (1%)
    pallas_call x1, Pallas kernels, attend_and_route(): pl.pallas_call(layer_kernel, out_shape=jax.ShapeDtypeStruct((ROWS, 256),...  109 us
    pallas_call x1, Pallas kernels, gather_queries(): pl.pallas_call(query_kernel, out_shape=(jax.ShapeDtypeStruct((4, 2, ROWS,...  14.7 us
    pallas_call x1, Pallas kernels, node_partials(): pl.pallas_call(node_kernel, out_shape=(jax.ShapeDtypeStruct((8, ROWS, 512...  14.6 us

profile of v7, /device:TPU:0, one launch (start us, length us, event | category | flops | bytes accessed | tf_op | source)
XLA Modules:
  0.0 140.2 jit_solution(17418183366910811313)
XLA Ops:
  0.0 14.7 %gather_queries.1 = (bf16[4,2,128,512]{3,2,1,0:T(8,128)(2,1)}, s32[4,2,2,128]{3,2,1,0:T(2,128)}, s32[8,1024]{1,0:T(8,128)}) custom-call(bf16[128,4096]{1,0:T(8,128)(2,1)} %refs_2_.1, s32[2,128]{1,0:T(2,128)} %bitcast.29, s32[1,1024]{1,0:T(1,128)} %bitcast.24, s32[1,1024]{1,0:T(1,128)} %bitcast.25, s32[1,64]{1,0:T(1,128)} %bitcast.31, s32[1,16]{1,0:T(1,128)} %bitcast.27, ...), custom_call_target="tpu_custom_call" | custom-call | tf_op jit(solution)/shard_map/gather_queries/pallas_call | solution.py:532
  14.8 14.6 %node_partials.1 = (bf16[8,128,512]{2,1,0:T(8,128)(2,1)}, f32[8,8,128]{2,1,0:T(8,128)}) custom-call(s32[16]{0:T(128)} %root_owner_ref.1, s32[64]{0:T(128)} %branch_owner_ref.1, s32[16,32]{1,0:T(8,128)} %root_pages_ref.1, s32[4,64]{1,0:T(4,128)} %bitcast.26, s32[16]{0:T(128)} %root_len_ref.1, s32[64]{0:T(128)} %branch_len_ref.1, bf16[1024,512]{1,0:T(8,128)(2,1)} %bitcast.19, ...), custom_call_target="tpu_custom_call" | custom-call | tf_op jit(solution)/shard_map/node_partials/pallas_call | solution.py:730
  29.4 109.4 %attend_and_route.1 = bf16[128,256]{1,0:T(8,128)(2,1)} custom-call(bf16[4,2,128,512]{3,2,1,0:T(8,128)(2,1)} %bitcast.20, f32[4,2,8,128]{3,2,1,0:T(8,128)} %bitcast.22, bf16[128,4096]{1,0:T(8,128)(2,1)} %refs_2_.1, bf16[2,128,1,64,128]{4,3,2,1,0:T(8,128)(2,1)} %refs_3_.1, s32[1,128]{1,0:T(1,128)} %bitcast.30, bf16[2,128,1024]{2,1,0:T(8,128)(2,1)} %refs_5_.1, ...), custom_call_target="tpu_custom_call" | custom-call | tf_op jit(solution)/shard_map/attend_and_route/pallas_call | solution.py:957
  138.8 1.5 %copy.23 = bf16[128,256]{1,0:T(8,128)(2,1)} copy(bf16[128,256]{1,0:T(8,128)(2,1)} %attend_and_route.1) | data formatting | bytes 131072
